TPU v7x, 32 devices: a whole 2x2x4 slice. The times are simulated.
32 devices in a mesh: groups: 1, ep: 8 (over z, core), tp: 4 (over y, x).
Axes of the slice: x: 2, y: 2, z: 4, core: 2. Of those that a mesh axis runs over, the one named last changes fastest.
Arguments:
- hidden: bfloat16 [2048, 3584], P(('groups', 'ep')), may hold values from -2.1 to 2.1
- moe_gain: float32 [3584], replicated, may hold values from 0.5 to 1.5
- route_logits: float32 [2048, 8], P(('groups', 'ep')), may hold values from -2 to 2
- routes: int32 [2048, 8], P(('groups', 'ep')), may hold values from 0 to 255, as said below
- gate_weight: bfloat16 [8, 3584, 1024], P('ep', None, 'tp'), may hold values from -0.09375 to 0.09375
- up_weight: bfloat16 [8, 3584, 1024], P('ep', None, 'tp'), may hold values from -0.09375 to 0.09375
- down_weight: bfloat16 [8, 1024, 3584], P('ep', 'tp'), may hold values from -0.5 to 0.5
- attn_gain: float32 [3584], P('tp'), may hold values from 0.5 to 1.5
- latent_weight: bfloat16 [3584, 576], P('tp'), may hold values from -0.09375 to 0.09375
- latent_gain: float32 [512], replicated, may hold values from 0.5 to 1.5
- positions: int32 [2048], P(('groups', 'ep')), may hold values from 0 to 32767
- owners: int32 [2048], P(('groups', 'ep')), may hold values from 0 to 3, as said below
Outputs:
- cache_latent: bfloat16 [2048, 512], P(('groups', 'ep', 'tp'))
- cache_rotary: bfloat16 [2048, 64], P(('groups', 'ep', 'tp'))
Inputs may be any that keep to these rules, and one draw needn't show every extreme that they name: `routes`: each row names 8 different experts. Within each ep block of 256 rows every expert below 8 is named by at most 16 rows, and one such expert is named by exactly 16 rows in every block. `owners`: within each aligned block of 64 rows each owner is named by at most 16 rows, and one owner reaches 16 in every block.
All inputs are finite; a program needn't handle non-finite values.
Results may differ from a plain program's by a relative error of at most 0.014.
Values may be sent and summed in bfloat16 or wider, within the bound.
No kernel may reach another device: no remote copies, remote signals or barrier semaphores. Data moves between devices by JAX's collectives and lax.ppermute only.
A program may use at most 64 MiB of HBM per device.

v0:
```python
import functools

import jax
import jax.numpy as jnp
from jax import lax
from jax.experimental import pallas as pl
from jax.experimental.pallas import tpu as pltpu
from jax.sharding import PartitionSpec as P

CAP = 16
EPS = 1e-06
ROUTE_SCALE = 2.5
ROPE_BASE = 10000.0
BF16 = jnp.bfloat16
F32 = jnp.float32
VMEM_LIMIT = 40 * 1024 * 1024


def columns_of(ref, index, count, share):
    if share % 128 == 0:
        return ref[:, pl.ds(pl.multiple_of(index * share, 128), share)]
    out = ref[:, 0:share]
    for q in range(1, count):
        out = jnp.where(index == q, ref[:, q * share : (q + 1) * share], out)
    return out


def dispatch_kernel(n_ep, n_tp, routes_hbm, logits_hbm, hidden_hbm, gain_hbm, *refs):
    own_ref, core_ref, near_ref = refs[:3]
    outs, combine_ref = refs[3 : n_ep - 1], refs[n_ep - 1]
    routes_ref, logits_ref, hidden_ref, gain_ref, pick_ref, head_ref, sems = refs[n_ep:]
    me = lax.axis_index("ep")
    part = lax.axis_index("tp")
    tokens, width = hidden_ref.shape
    share = width // n_tp
    step = 512 if width % 512 == 0 else width
    starts = range(0, width, step)
    small = [
        pltpu.make_async_copy(routes_hbm, routes_ref, sems.at[0]),
        pltpu.make_async_copy(logits_hbm, logits_ref, sems.at[1]),
        pltpu.make_async_copy(gain_hbm, gain_ref.at[0], sems.at[2]),
    ]
    large = [
        pltpu.make_async_copy(
            hidden_hbm.at[:, c : c + step], hidden_ref.at[:, c : c + step], sems.at[3 + i]
        )
        for i, c in enumerate(starts)
    ]
    for copy in small + large:
        copy.start()
    small[0].wait()
    small[1].wait()
    routes = routes_ref[...]
    affinity = jax.nn.sigmoid(logits_ref[...])
    weight = ROUTE_SCALE * affinity / jnp.sum(affinity, axis=0, keepdims=True)
    weight = weight.astype(BF16).astype(F32)
    expert = lax.broadcasted_iota(jnp.int32, (n_ep, tokens), 0) ^ me
    hit = jnp.zeros((n_ep, tokens), F32)
    gain_of = jnp.zeros((n_ep, tokens), F32)
    for k in range(routes.shape[0]):
        same = routes[k : k + 1, :] == expert
        hit = jnp.where(same, 1.0, hit)
        gain_of = jnp.where(same, weight[k : k + 1, :], gain_of)
    earlier = lax.broadcasted_iota(jnp.int32, (tokens, tokens), 0) < lax.broadcasted_iota(
        jnp.int32, (tokens, tokens), 1
    )
    rank = jnp.dot(hit.astype(BF16), earlier.astype(F32).astype(BF16), preferred_element_type=F32)
    rank = jnp.where(hit > 0, rank, -1.0)
    place = lax.broadcasted_iota(jnp.int32, (CAP, tokens), 0).astype(F32)
    for d in range(n_ep):
        match = rank[d : d + 1, :] == place
        rows = slice(d * CAP, (d + 1) * CAP)
        pick_ref[rows, :] = jnp.where(match, 1.0, 0.0).astype(BF16)
        combine_ref[rows, :] = jnp.where(match, gain_of[d : d + 1, :], 0.0).astype(BF16)
    pick = pick_ref[...]
    head = 4 * CAP
    square = jnp.zeros((n_ep * CAP, 1), F32)
    middle = len(large) // 2
    for i, c in enumerate(starts):
        if i == 0 or i == middle:
            for copy in large[:middle] if i < middle else large[i:]:
                copy.wait()
        got = jnp.dot(pick, hidden_ref[:, c : c + step], preferred_element_type=F32)
        square = square + jnp.sum(got * got, axis=1, keepdims=True)
        head_ref[:, c : c + step] = got[:head]
    small[2].wait()
    scale = lax.rsqrt(square / width + EPS)
    got = jnp.dot(pick[head:], columns_of(hidden_ref, part, n_tp, share), preferred_element_type=F32)
    rest = (got * scale[head:] * columns_of(gain_ref, part, n_tp, share)).astype(BF16)
    at = 0
    for out in outs:
        out[...] = rest[at : at + out.shape[0]]
        at += out.shape[0]
    whole = (head_ref[...] * scale[:head] * gain_ref[...]).astype(BF16)
    own_ref[...] = whole[:CAP]
    for q in range(n_tp):
        columns = slice(q * share, (q + 1) * share)
        core_ref[q * CAP : (q + 1) * CAP, :] = whole[CAP : 2 * CAP, columns]
        near_ref[q * CAP : (q + 1) * CAP, :] = whole[2 * CAP : 3 * CAP, columns]
        near_ref[(n_tp + q) * CAP : (n_tp + q + 1) * CAP, :] = whole[3 * CAP :, columns]


def load_kernel(after_ref, *refs):
    count = (len(refs) - 2) // 2
    mark_ref, sems = refs[-2:]
    copies = [
        pltpu.make_async_copy(refs[i], refs[count + i], sems.at[i]) for i in range(count)
    ]
    for copy in copies:
        copy.start()
    mark_ref[...] = jnp.zeros(mark_ref.shape, F32)
    for copy in copies:
        copy.wait()


def first_kernel(
    n_tp,
    own_ref,
    core_ref,
    near_ref,
    cross_ref,
    mine_ref,
    gate_ref,
    up_ref,
    mark_ref,
    inner_ref,
    gate_sum_ref,
    up_sum_ref,
    head_ref,
):
    part = lax.axis_index("tp")
    share = mine_ref.shape[1]
    head_ref[:CAP, :] = own_ref[...]
    for i, ref in enumerate((core_ref, near_ref, cross_ref)):
        for q in range(n_tp):
            rows = slice((i + 1) * CAP, (i + 2) * CAP)
            head_ref[rows, q * share : (q + 1) * share] = ref[q * CAP : (q + 1) * CAP, :]
    depth = pl.ds(pl.multiple_of(part * share, CAP), share)
    gate, upper = (
        jnp.dot(head_ref[...], ref[...], preferred_element_type=F32) for ref in (gate_ref, up_ref)
    )
    for weight_ref, sum_ref in zip((gate_ref, up_ref), (gate_sum_ref, up_sum_ref)):
        sum_ref[...] = jnp.dot(mine_ref[...], weight_ref[depth, :], preferred_element_type=F32)
    inner_ref[...] = (gate / (1.0 + jnp.exp(-gate)) * upper).astype(BF16)


def expert_kernel(n_tp, *refs):
    rows = refs[: n_tp - 1]
    gate_ref, up_ref, down_ref, near_ref, gate_sum_ref, up_sum_ref = refs[n_tp - 1 : n_tp + 5]
    far_outs = refs[n_tp + 5 : 2 * n_tp + 5]
    near_outs = refs[2 * n_tp + 5 :]
    part = lax.axis_index("tp")
    share = rows[0].shape[1]
    gate = gate_sum_ref[...]
    upper = up_sum_ref[...]
    for d in range(1, n_tp):
        value = rows[n_tp - 1 - d][...]
        depth = pl.ds(pl.multiple_of((part ^ d) * share, CAP), share)
        gate = gate + jnp.dot(value, gate_ref[depth, :], preferred_element_type=F32)
        upper = upper + jnp.dot(value, up_ref[depth, :], preferred_element_type=F32)
    far = (gate / (1.0 + jnp.exp(-gate)) * upper).astype(BF16)
    inner = jnp.concatenate([far, near_ref[...]], axis=0)
    count = far.shape[0]
    for d in range(n_tp):
        down = columns_of(down_ref, part ^ d, n_tp, share)
        out = jnp.dot(inner, down, preferred_element_type=F32).astype(BF16)
        far_outs[d][...] = out[:count]
        near_outs[d][...] = out[count:]


def sum_kernel(n_tp, *refs):
    parts, outs = refs[:n_tp], refs[n_tp:]
    at = 0
    for out in outs:
        rows = slice(at, at + out.shape[0])
        total = parts[0][rows, :].astype(F32)
        for other in parts[1:]:
            total = total + other[rows, :].astype(F32)
        out[...] = total.astype(BF16)
        at += out.shape[0]


def seats_kernel(
    n_tp,
    seat_cap,
    owners_ref,
    positions_ref,
    combine_ref,
    hidden_hbm,
    rows_ref,
    mix_ref,
    at_ref,
    hidden_ref,
    sem,
):
    part = lax.axis_index("tp")
    tokens, share = hidden_ref.shape
    if hidden_hbm.shape[1] != share:
        hidden_hbm = hidden_hbm.at[:, pl.ds(pl.multiple_of(part * share, 128), share)]
    copy = pltpu.make_async_copy(hidden_hbm, hidden_ref, sem)
    copy.start()
    source_rows = tokens // n_tp
    owners = owners_ref[...] ^ part
    owner = lax.broadcasted_iota(jnp.int32, (n_tp, tokens), 0)
    hot = jnp.where(owners == owner, 1.0, 0.0)
    first = lax.broadcasted_iota(jnp.int32, (tokens, tokens), 0)
    second = lax.broadcasted_iota(jnp.int32, (tokens, tokens), 1)
    earlier = jnp.where((first < second) & (first // source_rows == second // source_rows), 1.0, 0.0)
    before = jnp.dot(hot.astype(BF16), earlier.astype(BF16), preferred_element_type=F32)
    seat = jnp.sum(before * hot, axis=0, keepdims=True).astype(jnp.int32)
    source = lax.broadcasted_iota(jnp.int32, (1, tokens), 1) // source_rows
    code = owners * (n_tp * seat_cap) + source * seat_cap + seat
    seats = n_tp * seat_cap
    held = lax.broadcasted_iota(jnp.int32, (n_tp * seats, tokens), 0) == code
    pick = jnp.where(held, 1.0, 0.0).astype(BF16)
    mix_ref[...] = lax.dot_general(
        pick, combine_ref[...], (((1,), (1,)), ((), ())), preferred_element_type=F32
    ).astype(BF16)
    place = jnp.where(held[:seats], positions_ref[...].astype(F32), 0.0)
    at_ref[...] = jnp.sum(place, axis=1, keepdims=True)
    copy.wait()
    rows_ref[...] = jnp.dot(pick, hidden_ref[...], preferred_element_type=F32).astype(BF16)


def cache_kernel(n_z, n_tp, cache_width, *refs):
    near, far, core_ref = refs[:4], refs[4 : n_z + 2], refs[n_z + 2]
    mix_ref, rows_ref, gain_ref, weight_ref = refs[n_z + 3 : n_z + 7]
    outs, back_ref = refs[n_z + 7 : n_z + 7 + n_tp], refs[n_z + 7 + n_tp]
    for d in range(4):
        back_ref[d * CAP : (d + 1) * CAP, :] = near[d][...]
    for d in range(n_z - 2):
        at = (2 * d + 4) * CAP
        back_ref[at : at + CAP, :] = far[d][:CAP, :]
        back_ref[at + CAP : at + 2 * CAP, :] = core_ref[d * CAP : (d + 1) * CAP, :]
    mixed = jnp.dot(mix_ref[...], back_ref[...], preferred_element_type=F32)
    state = rows_ref[...].astype(F32) + mixed
    square = jnp.sum(state * state, axis=1, keepdims=True)
    scaled = (state * gain_ref[...]).astype(BF16)
    value = lax.dot_general(
        scaled, weight_ref[...], (((1,), (1,)), ((), ())), preferred_element_type=F32
    ).astype(BF16)
    high = square.astype(BF16).astype(F32)
    rest = square - high
    middle = rest.astype(BF16).astype(F32)
    low = rest - middle
    seats, wide = outs[0].shape
    lane = lax.broadcasted_iota(jnp.int32, (square.shape[0], wide - cache_width), 1)
    extra = jnp.where(lane == 0, high, jnp.where(lane == 1, middle, jnp.where(lane == 2, low, 0.0)))
    extra = extra.astype(BF16)
    for d in range(n_tp):
        outs[d][:, :cache_width] = value[d * seats : (d + 1) * seats]
        outs[d][:, cache_width:] = extra[d * seats : (d + 1) * seats]


def finish_kernel(n_tp, width, rank_width, *refs):
    parts = refs[:n_tp]
    gain_ref, cos_ref, sin_ref, latent_ref, rotary_ref = refs[n_tp:]
    total = parts[0][...].astype(F32)
    for other in parts[1:]:
        total = total + other[...].astype(F32)
    half = cos_ref.shape[1]
    cache_width = rank_width + 2 * half
    square = jnp.sum(total[:, cache_width : cache_width + 3], axis=1, keepdims=True)
    cache = total[:, :cache_width] * lax.rsqrt(square / width + EPS)
    latent = cache[:, :rank_width]
    scale = lax.rsqrt(jnp.mean(latent * latent, axis=1, keepdims=True) + EPS)
    latent_ref[...] = (latent * scale * gain_ref[...]).astype(BF16)
    first = cache[:, rank_width : rank_width + half]
    second = cache[:, rank_width + half :]
    cosine, sine = cos_ref[...], sin_ref[...]
    rotary_ref[:, :half] = (first * cosine - second * sine).astype(BF16)
    rotary_ref[:, half:] = (second * cosine + first * sine).astype(BF16)


def call(kernel, out_shape, args, scratch=(), flops=0, hbm=()):
    moved = sum(a.size * a.dtype.itemsize for a in args)
    vmem = pl.BlockSpec(memory_space=pltpu.VMEM)
    args = [
        pltpu.with_memory_space_constraint(a, pltpu.HBM) if i in hbm else a
        for i, a in enumerate(args)
    ]
    return pl.pallas_call(
        kernel,
        out_shape=out_shape,
        in_specs=[
            pl.BlockSpec(memory_space=pltpu.HBM) if i in hbm else vmem for i in range(len(args))
        ],
        out_specs=[vmem] * len(out_shape),
        scratch_shapes=list(scratch),
        compiler_params=pltpu.CompilerParams(vmem_limit_bytes=VMEM_LIMIT),
        cost_estimate=pl.CostEstimate(flops=flops, bytes_accessed=moved, transcendentals=0),
    )(*args)


def swap(value, axis, d):
    return lax.ppermute(value, axis, [(i, i ^ d) for i in range(lax.axis_size(axis))])


def spread(value, n_tp):
    return [swap(value, "tp", d) for d in reversed(range(1, n_tp))]


def collect(values):
    return [swap(values[d], "tp", d) for d in reversed(range(1, len(values)))] + [values[0]]


def on_device(
    hidden,
    moe_gain,
    route_logits,
    routes,
    gate_weight,
    up_weight,
    down_weight,
    attn_gain,
    latent_weight,
    latent_gain,
    positions,
    owners,
):
    n_ep = lax.axis_size("ep")
    n_tp = lax.axis_size("tp")
    n_z = n_ep // 2
    tokens, width = hidden.shape
    share = width // n_tp
    ff = gate_weight.shape[2]
    slots = n_ep * CAP
    seat_cap = max(2, tokens // n_tp // 4)
    seats = n_tp * seat_cap
    rank_width = latent_gain.shape[0]
    cache_width = latent_weight.shape[1]
    half = (cache_width - rank_width) // 2
    wide = (cache_width + 3 + 127) // 128 * 128
    struct = jax.ShapeDtypeStruct
    chunks = width // 512 if width % 512 == 0 else 1

    own, to_core, to_near, *outgoing, combine = call(
        functools.partial(dispatch_kernel, n_ep, n_tp),
        [struct((CAP, width), BF16), struct((n_tp * CAP, share), BF16)]
        + [struct((2 * n_tp * CAP, share), BF16)]
        + [struct((CAP, share), BF16)] * (n_ep - 4)
        + [struct((slots, tokens), BF16)],
        (routes.T, route_logits.T, hidden, moe_gain),
        [
            pltpu.VMEM(routes.T.shape, jnp.int32),
            pltpu.VMEM(routes.T.shape, F32),
            pltpu.VMEM(hidden.shape, BF16),
            pltpu.VMEM((1, width), F32),
            pltpu.VMEM((slots, tokens), BF16),
            pltpu.VMEM((4 * CAP, width), F32),
            pltpu.SemaphoreType.DMA((3 + chunks,)),
        ],
        flops=4 * slots * tokens * width,
        hbm=(0, 1, 2, 3),
    )
    order = [*range(4, n_ep, 2), *range(5, n_ep, 2)]
    arrived = [swap(outgoing[d - 4], "ep", d) for d in order]
    near = swap(to_near[: n_tp * CAP], "ep", 2)
    near_crossed = swap(to_near[n_tp * CAP :], "ep", 3)
    from_core = swap(to_core, "ep", 1)
    gate_w, up_w, down_w = gate_weight[0], up_weight[0], down_weight[0]
    *loaded, mark = call(
        load_kernel,
        [struct(w.shape, BF16) for w in (gate_w, up_w, down_w)] + [struct((8, 128), F32)],
        (combine, gate_w, up_w, down_w),
        [pltpu.SemaphoreType.DMA((3,))],
        hbm=(1, 2, 3),
    )
    mine = jnp.concatenate([arrived[order.index(d)] for d in range(4, n_ep)], axis=0)
    shares = spread(mine, n_tp)
    near_rows, far_rows = 4 * CAP, slots - 4 * CAP
    inner, gate_sum, up_sum = call(
        functools.partial(first_kernel, n_tp),
        [struct((near_rows, ff), BF16)] + [struct((far_rows, ff), F32)] * 2,
        (own, from_core, near, near_crossed, mine, *loaded[:2], mark),
        [pltpu.VMEM((4 * CAP, width), BF16)],
        flops=2 * slots * width * ff,
    )
    terms = call(
        functools.partial(expert_kernel, n_tp),
        [struct((far_rows, share), BF16)] * n_tp + [struct((near_rows, share), BF16)] * n_tp,
        (*shares, *loaded, inner, gate_sum, up_sum),
        flops=2 * slots * width * ff * 3,
    )
    terms = list(terms)
    combine, terms[0] = lax.optimization_barrier((combine, terms[0]))
    share_of = hidden
    if share % 128:
        share_of = lax.dynamic_slice_in_dim(hidden, lax.axis_index("tp") * share, share, 1)
    rows, mix, at = call(
        functools.partial(seats_kernel, n_tp, seat_cap),
        [
            struct((n_tp * seats, share), BF16),
            struct((n_tp * seats, slots), BF16),
            struct((seats, 1), F32),
        ],
        (owners[None, :], positions[None, :], combine, share_of),
        [pltpu.VMEM((tokens, share), BF16), pltpu.SemaphoreType.DMA(())],
        flops=2 * n_tp * seats * tokens * (share + slots),
        hbm=(3,),
    )
    near_pieces, rows, mix = lax.optimization_barrier((list(terms[n_tp:]), rows, mix))
    freqs = ROPE_BASE ** (-jnp.arange(half, dtype=F32) / half)
    angles = at * freqs[None, :]
    cosine, sine = jnp.cos(angles), jnp.sin(angles)

    far_terms = collect(terms[:n_tp])
    near_terms = collect(near_pieces)
    far_done = call(
        functools.partial(sum_kernel, n_tp),
        [struct((2 * CAP, share), BF16)] * (n_z - 2),
        far_terms,
    )
    far_back = [swap(far_done[d - 2], "ep", 2 * d) for d in range(2, n_z)]
    near_done = call(
        functools.partial(sum_kernel, n_tp), [struct((CAP, share), BF16)] * 4, near_terms
    )
    near_back = [near_done[0]] + [swap(near_done[d], "ep", d) for d in (1, 2, 3)]
    crossed = swap(jnp.concatenate([piece[CAP:] for piece in far_back], axis=0), "ep", 1)
    partial = call(
        functools.partial(cache_kernel, n_z, n_tp, cache_width),
        [struct((seats, wide), BF16)] * n_tp,
        (*near_back, *far_back, crossed, mix, rows, attn_gain[None, :], latent_weight.T),
        [pltpu.VMEM((slots, share), BF16)],
        flops=2 * n_tp * seats * share * (slots + cache_width),
    )
    return tuple(
        call(
            functools.partial(finish_kernel, n_tp, width, rank_width),
            [struct((seats, rank_width), BF16), struct((seats, 2 * half), BF16)],
            (*collect(partial), latent_gain[None, :], cosine, sine),
        )
    )


def solution(mesh):
    placed = (
        P(("groups", "ep"), None),
        P(),
        P(("groups", "ep"), None),
        P(("groups", "ep"), None),
        P("ep", None, "tp"),
        P("ep", None, "tp"),
        P("ep", "tp", None),
        P("tp"),
        P("tp", None),
        P(),
        P(("groups", "ep")),
        P(("groups", "ep")),
    )
    return jax.shard_map(
        on_device,
        mesh=mesh,
        in_specs=placed,
        out_specs=(P(("groups", "ep", "tp"), None), P(("groups", "ep", "tp"), None)),
        check_vma=False,
    )
```

profile of v0, /device:TPU:0, one launch (start us, length us, event | category | flops | bytes accessed | tf_op | source)
XLA Modules:
  0.0 52.6 jit_solution(17775647523138111937)
XLA Ops:
  0.6 2.3 %shard_map.131 = (bf16[16,3584]{1,0:T(8,128)(2,1)S(1)}, bf16[64,896]{1,0:T(8,128)(2,1)S(1)}, bf16[128,896]{1,0:T(8,128)(2,1)S(1)}, bf16[16,896]{1,0:T(8,128)(2,1...) custom-call(s32[8,256]{1,0:T(8,128)} %bitcast.16, ...), custom_call_target="tpu_custom_call" | custom-call | flops 469762048 | bytes 1865728 | tf_op jit(solution)/shard_map/pallas_call | solution.py:282
  3.0 4.1 %collective-permute-start = (bf16[16,896]{1,0:T(8,128)(2,1)S(1)}, bf16[16,896]{1,0:T(8,128)(2,1)S(1)}, u32[]{:S(2)}, u32[]{:S(2)}) collective-permute-start(bf16[16,896]{1,0:T(8,128)(2,1)S(1)} %get-tuple-element.46), channel_id=1, source_target_pairs={{0,16},{4,20},{8,24},{12,28},{16,0},{20,4},{24,8},{28,12},{1,17},{... | collective-permute-start | bytes 86024 | tf_op jit(solution)/shard_map/ppermute | solution.py:296
  7.1 3.1 %collective-permute-start.2 = (bf16[16,896]{1,0:T(8,128)(2,1)S(1)}, bf16[16,896]{1,0:T(8,128)(2,1)S(1)}, u32[]{:S(2)}, u32[]{:S(2)}) collective-permute-start(bf16[16,896]{1,0:T(8,128)(2,1)S(1)} %get-tuple-element.48), channel_id=1, source_target_pairs={{0,24},{4,28},{8,16},{12,20},{16,8},{20,12},{24,0},{28,4},{1,25},{... | collective-permute-start | bytes 86024 | tf_op jit(solution)/shard_map/ppermute | solution.py:296
  10.2 0.6 %collective-permute-start.3 = (bf16[16,896]{1,0:T(8,128)(2,1)S(1)}, bf16[16,896]{1,0:T(8,128)(2,1)S(1)}, u32[]{:S(2)}, u32[]{:S(2)}) collective-permute-start(bf16[16,896]{1,0:T(8,128)(2,1)S(1)} %get-tuple-element.49), channel_id=1, source_target_pairs={{0,28},{4,24},{8,20},{12,16},{16,12},{20,8},{24,4},{28,0},{1,29},{... | collective-permute-start | bytes 86024 | tf_op jit(solution)/shard_map/ppermute | solution.py:296
  10.9 1.6 %collective-permute-start.9 = (bf16[64,896]{1,0:T(8,128)(2,1)S(1)}, bf16[64,896]{1,0:T(8,128)(2,1)S(1)}, u32[]{:S(2)}, u32[]{:S(2)}) collective-permute-start(bf16[64,896]{1,0:T(8,128)(2,1)S(1)} %get-tuple-element.90), channel_id=1, source_target_pairs={{0,12},{4,8},{8,4},{12,0},{16,28},{20,24},{24,20},{28,16},{1,13},{... | collective-permute-start | bytes 344072 | tf_op jit(solution)/shard_map/ppermute | solution.py:296
  12.5 0.5 %collective-permute-start.7 = (bf16[64,896]{1,0:T(8,128)(2,1)S(1)}, bf16[64,896]{1,0:T(8,128)(2,1)S(1)}, u32[]{:S(2)}, u32[]{:S(2)}) collective-permute-start(bf16[64,896]{1,0:T(8,128)(2,1)S(1)} %get-tuple-element.55), channel_id=1, source_target_pairs={{0,4},{4,0},{8,12},{12,8},{16,20},{20,16},{24,28},{28,24},{1,5},{5... | collective-permute-start | bytes 344072 | tf_op jit(solution)/shard_map/ppermute | solution.py:296
  13.1 2.3 %collective-permute-done.3 = bf16[16,896]{1,0:T(8,128)(2,1)S(1)} collective-permute-done((bf16[16,896]{1,0:T(8,128)(2,1)S(1)}, bf16[16,896]{1,0:T(8,128)(2,1)S(1)}, u32[]{:S(2)}, u32[]{:S(2)}) %collective-permute-start.3) | collective-permute-done | bytes 28704 | tf_op jit(solution)/shard_map/ppermute | solution.py:296
  15.4 2.5 %collective-permute-start.4 = (bf16[64,896]{1,0:T(8,128)(2,1)S(1)}, bf16[64,896]{1,0:T(8,128)(2,1)S(1)}, u32[]{:S(2)}, u32[]{:S(2)}) collective-permute-start(bf16[64,896]{1,0:T(8,128)(2,1)S(1)} %constant_dynamic-update-slice_fusion.mine_ref), channel_id=1, source_target_pairs={{0,3},{1,2},{2,1},{3,0},{4,7},{5,6},{6,5},{7,4},{8,11},{9,10},{10,... | collective-permute-start | bytes 344072 | tf_op jit(solution)/shard_map/ppermute | solution.py:296
  18.4 0.6 %collective-permute-start.6 = (bf16[64,896]{1,0:T(8,128)(2,1)S(1)}, bf16[64,896]{1,0:T(8,128)(2,1)S(1)}, u32[]{:S(2)}, u32[]{:S(2)}) collective-permute-start(bf16[64,896]{1,0:T(8,128)(2,1)S(1)} %constant_dynamic-update-slice_fusion.mine_ref), channel_id=1, source_target_pairs={{0,1},{1,0},{2,3},{3,2},{4,5},{5,4},{6,7},{7,6},{8,9},{9,8},{10,11... | collective-permute-start | bytes 344072 | tf_op jit(solution)/shard_map/ppermute | solution.py:296
  19.0 2.6 %shard_map.132 = (bf16[3584,256]{1,0:T(8,128)(2,1)S(1)}, bf16[3584,256]{1,0:T(8,128)(2,1)S(1)}, bf16[256,3584]{1,0:T(8,128)(2,1)S(1)}, f32[8,128]{1,0:T(8,128)S(1)}) custom-call(bf16[128,256]{1,0:T(8,128)(2,1)S(1)} %get-tuple-element.66.after_ref.combine_ref, bf16[3584,256]{1,0:T(8,128)(2,1)} %bitcast.13, bf16[3584,256]{1,0:T(8,128)(2,1)} %bitcast.14, ...), custom_call_target="tpu_custom_call" | custom-call | bytes 5570560 | tf_op jit(solution)/shard_map/pallas_call | solution.py:282
  21.6 0.9 %shard_map.133 = (bf16[64,256]{1,0:T(8,128)(2,1)S(1)}, f32[64,256]{1,0:T(8,128)S(1)}, f32[64,256]{1,0:T(8,128)S(1)}) custom-call(bf16[16,3584]{1,0:T(8,128)(2,1)S(1)} %get-tuple-element.54.own_ref, bf16[64,896]{1,0:T(8,128)(2,1)S(1)} %collective-permute-done.7.core_ref, bf16[64,896]{1,0:T(8,128)(2,1)S(1)} %collective-permute-done.8.near_ref, ...), custom_call_target="tpu_custom_call" | custom-call | flops 234881024 | bytes 4247552 | tf_op jit(solution)/shard_map/pallas_call | solution.py:282
  22.6 2.1 %collective-permute-done.5.refs_1_ = bf16[64,896]{1,0:T(8,128)(2,1)S(1)} collective-permute-done((bf16[64,896]{1,0:T(8,128)(2,1)S(1)}, bf16[64,896]{1,0:T(8,128)(2,1)S(1)}, u32[]{:S(2)}, u32[]{:S(2)}) %collective-permute-start.5) | collective-permute-done | bytes 114720 | tf_op jit(solution)/shard_map/ppermute | solution.py:296
  24.8 1.0 %shard_map.134 = (bf16[64,896]{1,0:T(8,128)(2,1)S(1)}, bf16[64,896]{1,0:T(8,128)(2,1)S(1)}, bf16[64,896]{1,0:T(8,128)(2,1)S(1)}, bf16[64,896]{1,0:T(8,128)(2,1)S...) custom-call(bf16[64,896]{1,0:T(8,128)(2,1)S(1)} %collective-permute-, ...), custom_call_target="tpu_custom_call" | custom-call | flops 704643072 | bytes 6012928 | tf_op jit(solution)/shard_map/pallas_call | solution.py:282
  25.9 1.7 %collective-permute-start.16 = (bf16[64,896]{1,0:T(8,128)(2,1)S(1)}, bf16[64,896]{1,0:T(8,128)(2,1)S(1)}, u32[]{:S(2)}, u32[]{:S(2)}) collective-permute-start(bf16[64,896]{1,0:T(8,128)(2,1)S(1)} %get-tuple-element.77), channel_id=1, source_target_pairs={{0,3},{1,2},{2,1},{3,0},{4,7},{5,6},{6,5},{7,4},{8,11},{9,10},{10,... | collective-permute-start | bytes 344072 | tf_op jit(solution)/shard_map/ppermute | solution.py:296
  27.5 1.3 %collective-permute-start.17 = (bf16[64,896]{1,0:T(8,128)(2,1)S(1)}, bf16[64,896]{1,0:T(8,128)(2,1)S(1)}, u32[]{:S(2)}, u32[]{:S(2)}) collective-permute-start(bf16[64,896]{1,0:T(8,128)(2,1)S(1)} %get-tuple-element.78), channel_id=1, source_target_pairs={{0,2},{1,3},{2,0},{3,1},{4,6},{5,7},{6,4},{7,5},{8,10},{9,11},{10,... | collective-permute-start | bytes 344072 | tf_op jit(solution)/shard_map/ppermute | solution.py:296
  29.4 1.4 %shard_map.135 = (bf16[256,896]{1,0:T(8,128)(2,1)S(1)}, bf16[256,128]{1,0:T(8,128)(2,1)S(1)}, f32[64,1]{1,0:T(8,128)S(1)}) custom-call(s32[1,256]{1,0:T(1,128)S(1)} %bitcast.11, s32[1,256]{1,0:T(1,128)S(1)} %bitcast.12, bf16[128,256]{1,0:T(8,128)(2,1)S(1)} %get-tuple-element.66.after_ref.combine_ref, bf16[256,3584]{1,0:T(8,128)(2,1)} %hidden_hbm.3), custom_call_target="tpu_custom_call" | custom-call | flops 134217728 | bytes 1902592 | tf_op jit(solution)/shard_map/pallas_call | solution.py:282
  30.8 1.7 %collective-permute-start.10 = (bf16[64,896]{1,0:T(8,128)(2,1)S(1)}, bf16[64,896]{1,0:T(8,128)(2,1)S(1)}, u32[]{:S(2)}, u32[]{:S(2)}) collective-permute-start(bf16[64,896]{1,0:T(8,128)(2,1)S(1)} %get-tuple-element.69), channel_id=1, source_target_pairs={{0,3},{1,2},{2,1},{3,0},{4,7},{5,6},{6,5},{7,4},{8,11},{9,10},{10,... | collective-permute-start | bytes 344072 | tf_op jit(solution)/shard_map/ppermute | solution.py:296
  32.5 1.3 %collective-permute-start.11 = (bf16[64,896]{1,0:T(8,128)(2,1)S(1)}, bf16[64,896]{1,0:T(8,128)(2,1)S(1)}, u32[]{:S(2)}, u32[]{:S(2)}) collective-permute-start(bf16[64,896]{1,0:T(8,128)(2,1)S(1)} %get-tuple-element.70), channel_id=1, source_target_pairs={{0,2},{1,3},{2,0},{3,1},{4,6},{5,7},{6,4},{7,5},{8,10},{9,11},{10,... | collective-permute-start | bytes 344072 | tf_op jit(solution)/shard_map/ppermute | solution.py:296
  33.8 0.5 %collective-permute-start.12 = (bf16[64,896]{1,0:T(8,128)(2,1)S(1)}, bf16[64,896]{1,0:T(8,128)(2,1)S(1)}, u32[]{:S(2)}, u32[]{:S(2)}) collective-permute-start(bf16[64,896]{1,0:T(8,128)(2,1)S(1)} %get-tuple-element.71), channel_id=1, source_target_pairs={{0,1},{1,0},{2,3},{3,2},{4,5},{5,4},{6,7},{7,6},{8,9},{9,8},{10,11... | collective-permute-start | bytes 344072 | tf_op jit(solution)/shard_map/ppermute | solution.py:296
  34.4 1.4 %collective-permute-done.17.refs_1_ = bf16[64,896]{1,0:T(8,128)(2,1)S(1)} collective-permute-done((bf16[64,896]{1,0:T(8,128)(2,1)S(1)}, bf16[64,896]{1,0:T(8,128)(2,1)S(1)}, u32[]{:S(2)}, u32[]{:S(2)}) %collective-permute-start.17) | collective-permute-done | bytes 114720 | tf_op jit(solution)/shard_map/ppermute | solution.py:296
  36.2 1.3 %collective-permute-start.20 = (bf16[32,896]{1,0:T(8,128)(2,1)S(1)}, bf16[32,896]{1,0:T(8,128)(2,1)S(1)}, u32[]{:S(2)}, u32[]{:S(2)}) collective-permute-start(bf16[32,896]{1,0:T(8,128)(2,1)S(1)} %get-tuple-element.82), channel_id=1, source_target_pairs={{0,24},{4,28},{8,16},{12,20},{16,8},{20,12},{24,0},{28,4},{1,25},{... | collective-permute-start | bytes 172040 | tf_op jit(solution)/shard_map/ppermute | solution.py:296
  37.9 1.4 %collective-permute-done.11.refs_1_ = bf16[64,896]{1,0:T(8,128)(2,1)S(1)} collective-permute-done((bf16[64,896]{1,0:T(8,128)(2,1)S(1)}, bf16[64,896]{1,0:T(8,128)(2,1)S(1)}, u32[]{:S(2)}, u32[]{:S(2)}) %collective-permute-start.11) | collective-permute-done | bytes 114720 | tf_op jit(solution)/shard_map/ppermute | solution.py:296
  39.7 1.6 %collective-permute-start.15 = (bf16[16,896]{1,0:T(8,128)(2,1)S(1)}, bf16[16,896]{1,0:T(8,128)(2,1)S(1)}, u32[]{:S(2)}, u32[]{:S(2)}) collective-permute-start(bf16[16,896]{1,0:T(8,128)(2,1)S(1)} %get-tuple-element.76), channel_id=1, source_target_pairs={{0,12},{4,8},{8,4},{12,0},{16,28},{20,24},{24,20},{28,16},{1,13},{... | collective-permute-start | bytes 86024 | tf_op jit(solution)/shard_map/ppermute | solution.py:296
  41.7 0.7 %collective-permute-done.20.refs_5_ = bf16[32,896]{1,0:T(8,128)(2,1)S(1)} collective-permute-done((bf16[32,896]{1,0:T(8,128)(2,1)S(1)}, bf16[32,896]{1,0:T(8,128)(2,1)S(1)}, u32[]{:S(2)}, u32[]{:S(2)}) %collective-permute-start.20) | collective-permute-done | bytes 57376 | tf_op jit(solution)/shard_map/ppermute | solution.py:296
  42.6 0.9 %collective-permute-done.14.refs_2_ = bf16[16,896]{1,0:T(8,128)(2,1)S(1)} collective-permute-done((bf16[16,896]{1,0:T(8,128)(2,1)S(1)}, bf16[16,896]{1,0:T(8,128)(2,1)S(1)}, u32[]{:S(2)}, u32[]{:S(2)}) %collective-permute-start.14) | collective-permute-done | bytes 28704 | tf_op jit(solution)/shard_map/ppermute | solution.py:296
  43.6 0.8 %shard_map.138 = (bf16[64,640]{1,0:T(8,128)(2,1)S(1)}, bf16[64,640]{1,0:T(8,128)(2,1)S(1)}, bf16[64,640]{1,0:T(8,128)(2,1)S(1)}, bf16[64,640]{1,0:T(8,128)(2,1)S(1)}) custom-call(bf16[16,896]{1,0:T(8,128)(2,1)S(1)} %get-tuple-element.73.refs_0_, bf16[16,896]{1,0:T(8,128)(2,1)S(1)} %collective-permute-done.13.refs_1_, ...), custom_call_target="tpu_custom_call" | custom-call | flops 322961408 | bytes 1846784 | tf_op jit(solution)/shard_map/pallas_call | solution.py:282
  44.4 1.3 %collective-permute-start.22 = (bf16[64,640]{1,0:T(8,128)(2,1)S(1)}, bf16[64,640]{1,0:T(8,128)(2,1)S(1)}, u32[]{:S(2)}, u32[]{:S(2)}) collective-permute-start(bf16[64,640]{1,0:T(8,128)(2,1)S(1)} %get-tuple-element.85), channel_id=1, source_target_pairs={{0,3},{1,2},{2,1},{3,0},{4,7},{5,6},{6,5},{7,4},{8,11},{9,10},{10,... | collective-permute-start | bytes 245768 | tf_op jit(solution)/shard_map/ppermute | solution.py:296
  45.7 1.5 %collective-permute-start.23 = (bf16[64,640]{1,0:T(8,128)(2,1)S(1)}, bf16[64,640]{1,0:T(8,128)(2,1)S(1)}, u32[]{:S(2)}, u32[]{:S(2)}) collective-permute-start(bf16[64,640]{1,0:T(8,128)(2,1)S(1)} %get-tuple-element.86), channel_id=1, source_target_pairs={{0,2},{1,3},{2,0},{3,1},{4,6},{5,7},{6,4},{7,5},{8,10},{9,11},{10,... | collective-permute-start | bytes 245768 | tf_op jit(solution)/shard_map/ppermute | solution.py:296
  47.2 0.7 %collective-permute-start.24 = (bf16[64,640]{1,0:T(8,128)(2,1)S(1)}, bf16[64,640]{1,0:T(8,128)(2,1)S(1)}, u32[]{:S(2)}, u32[]{:S(2)}) collective-permute-start(bf16[64,640]{1,0:T(8,128)(2,1)S(1)} %get-tuple-element.87), channel_id=1, source_target_pairs={{0,1},{1,0},{2,3},{3,2},{4,5},{5,4},{6,7},{7,6},{8,9},{9,8},{10,11... | collective-permute-start | bytes 245768 | tf_op jit(solution)/shard_map/ppermute | solution.py:296
  48.2 2.3 %collective-permute-done.22.refs_0_ = bf16[64,640]{1,0:T(8,128)(2,1)S(1)} collective-permute-done((bf16[64,640]{1,0:T(8,128)(2,1)S(1)}, bf16[64,640]{1,0:T(8,128)(2,1)S(1)}, u32[]{:S(2)}, u32[]{:S(2)}) %collective-permute-start.22) | collective-permute-done | bytes 81952 | tf_op jit(solution)/shard_map/ppermute | solution.py:296
  50.5 1.2 %collective-permute-done.23.refs_1_ = bf16[64,640]{1,0:T(8,128)(2,1)S(1)} collective-permute-done((bf16[64,640]{1,0:T(8,128)(2,1)S(1)}, bf16[64,640]{1,0:T(8,128)(2,1)S(1)}, u32[]{:S(2)}, u32[]{:S(2)}) %collective-permute-start.23) | collective-permute-done | bytes 81952 | tf_op jit(solution)/shard_map/ppermute | solution.py:296
  51.7 0.9 %shard_map.139 = (bf16[64,512]{1,0:T(8,128)(2,1)}, bf16[64,64]{1,0:T(8,128)(2,1)}) custom-call(bf16[64,640]{1,0:T(8,128)(2,1)S(1)} %collective-permute-done.22.refs_0_, bf16[64,640]{1,0:T(8,128)(2,1)S(1)} %collective-permute-done.23.refs_1_, bf16[64,640]{1,0:T(8,128)(2,1)S(1)} %collective-permute-done.24.refs_2_, ...), custom_call_target="tpu_custom_call" | custom-call | bytes 346112 | tf_op jit(solution)/shard_map/pallas_call | solution.py:282
  (49 shorter events, 3.5 us)
Async XLA Ops:
  3.0 7.9 %collective-permute-start = (bf16[16,896]{1,0:T(8,128)(2,1)S(1)}, bf16[16,896]{1,0:T(8,128)(2,1)S(1)}, u32[]{:S(2)}, u32[]{:S(2)}) collective-permute-start(bf16[16,896]{1,0:T(8,128)(2,1)S(1)} %get-tuple-element.46), channel_id=1, source_target_pairs={{0,16},{4,20},{8,24},{12,28},{16,0},{20,4},{24,8},{28,12},{1,17},{... | collective-permute-start | bytes 86024 | tf_op jit(solution)/shard_map/ppermute | solution.py:296
  7.1 5.4 %collective-permute-start.1 = (bf16[16,896]{1,0:T(8,128)(2,1)S(1)}, bf16[16,896]{1,0:T(8,128)(2,1)S(1)}, u32[]{:S(2)}, u32[]{:S(2)}) collective-permute-start(bf16[16,896]{1,0:T(8,128)(2,1)S(1)} %get-tuple-element.47), channel_id=1, source_target_pairs={{0,20},{4,16},{8,28},{12,24},{16,4},{20,0},{24,12},{28,8},{1,21},{... | collective-permute-start | bytes 86024 | tf_op jit(solution)/shard_map/ppermute | solution.py:296
  7.1 6.0 %collective-permute-start.2 = (bf16[16,896]{1,0:T(8,128)(2,1)S(1)}, bf16[16,896]{1,0:T(8,128)(2,1)S(1)}, u32[]{:S(2)}, u32[]{:S(2)}) collective-permute-start(bf16[16,896]{1,0:T(8,128)(2,1)S(1)} %get-tuple-element.48), channel_id=1, source_target_pairs={{0,24},{4,28},{8,16},{12,20},{16,8},{20,12},{24,0},{28,4},{1,25},{... | collective-permute-start | bytes 86024 | tf_op jit(solution)/shard_map/ppermute | solution.py:296
  10.2 5.2 %collective-permute-start.3 = (bf16[16,896]{1,0:T(8,128)(2,1)S(1)}, bf16[16,896]{1,0:T(8,128)(2,1)S(1)}, u32[]{:S(2)}, u32[]{:S(2)}) collective-permute-start(bf16[16,896]{1,0:T(8,128)(2,1)S(1)} %get-tuple-element.49), channel_id=1, source_target_pairs={{0,28},{4,24},{8,20},{12,16},{16,12},{20,8},{24,4},{28,0},{1,29},{... | collective-permute-start | bytes 86024 | tf_op jit(solution)/shard_map/ppermute | solution.py:296
  10.8 7.6 %collective-permute-start.8 = (bf16[64,896]{1,0:T(8,128)(2,1)S(1)}, bf16[64,896]{1,0:T(8,128)(2,1)S(1)}, u32[]{:S(2)}, u32[]{:S(2)}) collective-permute-start(bf16[64,896]{1,0:T(8,128)(2,1)S(1)} %get-tuple-element.91), channel_id=1, source_target_pairs={{0,8},{4,12},{8,0},{12,4},{16,24},{20,28},{24,16},{28,20},{1,9},{5... | collective-permute-start | bytes 344072 | tf_op jit(solution)/shard_map/ppermute | solution.py:296
  10.9 10.7 %collective-permute-start.9 = (bf16[64,896]{1,0:T(8,128)(2,1)S(1)}, bf16[64,896]{1,0:T(8,128)(2,1)S(1)}, u32[]{:S(2)}, u32[]{:S(2)}) collective-permute-start(bf16[64,896]{1,0:T(8,128)(2,1)S(1)} %get-tuple-element.90), channel_id=1, source_target_pairs={{0,12},{4,8},{8,4},{12,0},{16,28},{20,24},{24,20},{28,16},{1,13},{... | collective-permute-start | bytes 344072 | tf_op jit(solution)/shard_map/ppermute | solution.py:296
  12.5 9.1 %collective-permute-start.7 = (bf16[64,896]{1,0:T(8,128)(2,1)S(1)}, bf16[64,896]{1,0:T(8,128)(2,1)S(1)}, u32[]{:S(2)}, u32[]{:S(2)}) collective-permute-start(bf16[64,896]{1,0:T(8,128)(2,1)S(1)} %get-tuple-element.55), channel_id=1, source_target_pairs={{0,4},{4,0},{8,12},{12,8},{16,20},{20,16},{24,28},{28,24},{1,5},{5... | collective-permute-start | bytes 344072 | tf_op jit(solution)/shard_map/ppermute | solution.py:296
  15.4 7.2 %collective-permute-start.4 = (bf16[64,896]{1,0:T(8,128)(2,1)S(1)}, bf16[64,896]{1,0:T(8,128)(2,1)S(1)}, u32[]{:S(2)}, u32[]{:S(2)}) collective-permute-start(bf16[64,896]{1,0:T(8,128)(2,1)S(1)} %constant_dynamic-update-slice_fusion.mine_ref), channel_id=1, source_target_pairs={{0,3},{1,2},{2,1},{3,0},{4,7},{5,6},{6,5},{7,4},{8,11},{9,10},{10,... | collective-permute-start | bytes 344072 | tf_op jit(solution)/shard_map/ppermute | solution.py:296
  17.9 6.8 %collective-permute-start.5 = (bf16[64,896]{1,0:T(8,128)(2,1)S(1)}, bf16[64,896]{1,0:T(8,128)(2,1)S(1)}, u32[]{:S(2)}, u32[]{:S(2)}) collective-permute-start(bf16[64,896]{1,0:T(8,128)(2,1)S(1)} %constant_dynamic-update-slice_fusion.mine_ref), channel_id=1, source_target_pairs={{0,2},{1,3},{2,0},{3,1},{4,6},{5,7},{6,4},{7,5},{8,10},{9,11},{10,... | collective-permute-start | bytes 344072 | tf_op jit(solution)/shard_map/ppermute | solution.py:296
  18.4 6.4 %collective-permute-start.6 = (bf16[64,896]{1,0:T(8,128)(2,1)S(1)}, bf16[64,896]{1,0:T(8,128)(2,1)S(1)}, u32[]{:S(2)}, u32[]{:S(2)}) collective-permute-start(bf16[64,896]{1,0:T(8,128)(2,1)S(1)} %constant_dynamic-update-slice_fusion.mine_ref), channel_id=1, source_target_pairs={{0,1},{1,0},{2,3},{3,2},{4,5},{5,4},{6,7},{7,6},{8,9},{9,8},{10,11... | collective-permute-start | bytes 344072 | tf_op jit(solution)/shard_map/ppermute | solution.py:296
  24.8 4.6 %copy-start.2 = (s32[256]{0:T(256)S(1)}, s32[256]{0:T(256)}, u32[]{:S(2)}) copy-start(s32[256]{0:T(256)} %param.23) | copy-start | bytes 3076
  24.8 4.6 %copy-start.3 = (s32[256]{0:T(256)S(1)}, s32[256]{0:T(256)}, u32[]{:S(2)}) copy-start(s32[256]{0:T(256)} %param.22) | copy-start | bytes 3076
  25.8 16.6 %copy-start.4 = (f32[896]{0:T(1024)S(1)}, f32[896]{0:T(1024)}, u32[]{:S(2)}) copy-start(f32[896]{0:T(1024)} %param.19) | copy-start | bytes 10756
  25.8 17.8 %copy-start = (bf16[896,576]{0,1:T(8,128)(2,1)S(1)}, bf16[896,576]{0,1:T(8,128)(2,1)}, u32[]{:S(2)}) copy-start(bf16[896,576]{0,1:T(8,128)(2,1)} %param.20) | copy-start | bytes 3096580
  25.9 8.0 %collective-permute-start.16 = (bf16[64,896]{1,0:T(8,128)(2,1)S(1)}, bf16[64,896]{1,0:T(8,128)(2,1)S(1)}, u32[]{:S(2)}, u32[]{:S(2)}) collective-permute-start(bf16[64,896]{1,0:T(8,128)(2,1)S(1)} %get-tuple-element.77), channel_id=1, source_target_pairs={{0,3},{1,2},{2,1},{3,0},{4,7},{5,6},{6,5},{7,4},{8,11},{9,10},{10,... | collective-permute-start | bytes 344072 | tf_op jit(solution)/shard_map/ppermute | solution.py:296
  27.5 8.3 %collective-permute-start.17 = (bf16[64,896]{1,0:T(8,128)(2,1)S(1)}, bf16[64,896]{1,0:T(8,128)(2,1)S(1)}, u32[]{:S(2)}, u32[]{:S(2)}) collective-permute-start(bf16[64,896]{1,0:T(8,128)(2,1)S(1)} %get-tuple-element.78), channel_id=1, source_target_pairs={{0,2},{1,3},{2,0},{3,1},{4,6},{5,7},{6,4},{7,5},{8,10},{9,11},{10,... | collective-permute-start | bytes 344072 | tf_op jit(solution)/shard_map/ppermute | solution.py:296
  28.9 7.0 %collective-permute-start.18 = (bf16[64,896]{1,0:T(8,128)(2,1)S(1)}, bf16[64,896]{1,0:T(8,128)(2,1)S(1)}, u32[]{:S(2)}, u32[]{:S(2)}) collective-permute-start(bf16[64,896]{1,0:T(8,128)(2,1)S(1)} %get-tuple-element.79), channel_id=1, source_target_pairs={{0,1},{1,0},{2,3},{3,2},{4,5},{5,4},{6,7},{7,6},{8,9},{9,8},{10,11... | collective-permute-start | bytes 344072 | tf_op jit(solution)/shard_map/ppermute | solution.py:296
  30.8 20.8 %copy-start.1 = (f32[512]{0:T(512)S(1)}, f32[512]{0:T(512)}, u32[]{:S(2)}) copy-start(f32[512]{0:T(512)} %param.21) | copy-start | bytes 6148
  30.8 7.0 %collective-permute-start.10 = (bf16[64,896]{1,0:T(8,128)(2,1)S(1)}, bf16[64,896]{1,0:T(8,128)(2,1)S(1)}, u32[]{:S(2)}, u32[]{:S(2)}) collective-permute-start(bf16[64,896]{1,0:T(8,128)(2,1)S(1)} %get-tuple-element.69), channel_id=1, source_target_pairs={{0,3},{1,2},{2,1},{3,0},{4,7},{5,6},{6,5},{7,4},{8,11},{9,10},{10,... | collective-permute-start | bytes 344072 | tf_op jit(solution)/shard_map/ppermute | solution.py:296
  32.5 6.7 %collective-permute-start.11 = (bf16[64,896]{1,0:T(8,128)(2,1)S(1)}, bf16[64,896]{1,0:T(8,128)(2,1)S(1)}, u32[]{:S(2)}, u32[]{:S(2)}) collective-permute-start(bf16[64,896]{1,0:T(8,128)(2,1)S(1)} %get-tuple-element.70), channel_id=1, source_target_pairs={{0,2},{1,3},{2,0},{3,1},{4,6},{5,7},{6,4},{7,5},{8,10},{9,11},{10,... | collective-permute-start | bytes 344072 | tf_op jit(solution)/shard_map/ppermute | solution.py:296
  33.8 5.4 %collective-permute-start.12 = (bf16[64,896]{1,0:T(8,128)(2,1)S(1)}, bf16[64,896]{1,0:T(8,128)(2,1)S(1)}, u32[]{:S(2)}, u32[]{:S(2)}) collective-permute-start(bf16[64,896]{1,0:T(8,128)(2,1)S(1)} %get-tuple-element.71), channel_id=1, source_target_pairs={{0,1},{1,0},{2,3},{3,2},{4,5},{5,4},{6,7},{7,6},{8,9},{9,8},{10,11... | collective-permute-start | bytes 344072 | tf_op jit(solution)/shard_map/ppermute | solution.py:296
  35.9 5.7 %collective-permute-start.19 = (bf16[32,896]{1,0:T(8,128)(2,1)S(1)}, bf16[32,896]{1,0:T(8,128)(2,1)S(1)}, u32[]{:S(2)}, u32[]{:S(2)}) collective-permute-start(bf16[32,896]{1,0:T(8,128)(2,1)S(1)} %get-tuple-element.81), channel_id=1, source_target_pairs={{0,16},{4,20},{8,24},{12,28},{16,0},{20,4},{24,8},{28,12},{1,17},{... | collective-permute-start | bytes 172040 | tf_op jit(solution)/shard_map/ppermute | solution.py:296
  36.2 6.1 %collective-permute-start.20 = (bf16[32,896]{1,0:T(8,128)(2,1)S(1)}, bf16[32,896]{1,0:T(8,128)(2,1)S(1)}, u32[]{:S(2)}, u32[]{:S(2)}) collective-permute-start(bf16[32,896]{1,0:T(8,128)(2,1)S(1)} %get-tuple-element.82), channel_id=1, source_target_pairs={{0,24},{4,28},{8,16},{12,20},{16,8},{20,12},{24,0},{28,4},{1,25},{... | collective-permute-start | bytes 172040 | tf_op jit(solution)/shard_map/ppermute | solution.py:296
  39.4 3.2 %collective-permute-start.13 = (bf16[16,896]{1,0:T(8,128)(2,1)S(1)}, bf16[16,896]{1,0:T(8,128)(2,1)S(1)}, u32[]{:S(2)}, u32[]{:S(2)}) collective-permute-start(bf16[16,896]{1,0:T(8,128)(2,1)S(1)} %get-tuple-element.74), channel_id=1, source_target_pairs={{0,4},{4,0},{8,12},{12,8},{16,20},{20,16},{24,28},{28,24},{1,5},{5... | collective-permute-start | bytes 86024 | tf_op jit(solution)/shard_map/ppermute | solution.py:296
  39.4 4.0 %collective-permute-start.14 = (bf16[16,896]{1,0:T(8,128)(2,1)S(1)}, bf16[16,896]{1,0:T(8,128)(2,1)S(1)}, u32[]{:S(2)}, u32[]{:S(2)}) collective-permute-start(bf16[16,896]{1,0:T(8,128)(2,1)S(1)} %get-tuple-element.75), channel_id=1, source_target_pairs={{0,8},{4,12},{8,0},{12,4},{16,24},{20,28},{24,16},{28,20},{1,9},{5... | collective-permute-start | bytes 86024 | tf_op jit(solution)/shard_map/ppermute | solution.py:296
  39.7 3.8 %collective-permute-start.15 = (bf16[16,896]{1,0:T(8,128)(2,1)S(1)}, bf16[16,896]{1,0:T(8,128)(2,1)S(1)}, u32[]{:S(2)}, u32[]{:S(2)}) collective-permute-start(bf16[16,896]{1,0:T(8,128)(2,1)S(1)} %get-tuple-element.76), channel_id=1, source_target_pairs={{0,12},{4,8},{8,4},{12,0},{16,28},{20,24},{24,20},{28,16},{1,13},{... | collective-permute-start | bytes 86024 | tf_op jit(solution)/shard_map/ppermute | solution.py:296
  42.3 1.3 %collective-permute-start.21 = (bf16[32,896]{1,0:T(8,128)(2,1)S(1)}, bf16[32,896]{1,0:T(8,128)(2,1)S(1)}, u32[]{:S(2)}, u32[]{:S(2)}) collective-permute-start(bf16[32,896]{1,0:T(8,128)(2,1)S(1)} %pad_maximum_fusion), channel_id=1, source_target_pairs={{0,4},{4,0},{8,12},{12,8},{16,20},{20,16},{24,28},{28,24},{1,5},{5... | collective-permute-start | bytes 172040 | tf_op jit(solution)/shard_map/ppermute | solution.py:296
  44.4 6.1 %collective-permute-start.22 = (bf16[64,640]{1,0:T(8,128)(2,1)S(1)}, bf16[64,640]{1,0:T(8,128)(2,1)S(1)}, u32[]{:S(2)}, u32[]{:S(2)}) collective-permute-start(bf16[64,640]{1,0:T(8,128)(2,1)S(1)} %get-tuple-element.85), channel_id=1, source_target_pairs={{0,3},{1,2},{2,1},{3,0},{4,7},{5,6},{6,5},{7,4},{8,11},{9,10},{10,... | collective-permute-start | bytes 245768 | tf_op jit(solution)/shard_map/ppermute | solution.py:296
  45.7 5.9 %collective-permute-start.23 = (bf16[64,640]{1,0:T(8,128)(2,1)S(1)}, bf16[64,640]{1,0:T(8,128)(2,1)S(1)}, u32[]{:S(2)}, u32[]{:S(2)}) collective-permute-start(bf16[64,640]{1,0:T(8,128)(2,1)S(1)} %get-tuple-element.86), channel_id=1, source_target_pairs={{0,2},{1,3},{2,0},{3,1},{4,6},{5,7},{6,4},{7,5},{8,10},{9,11},{10,... | collective-permute-start | bytes 245768 | tf_op jit(solution)/shard_map/ppermute | solution.py:296
  47.2 4.4 %collective-permute-start.24 = (bf16[64,640]{1,0:T(8,128)(2,1)S(1)}, bf16[64,640]{1,0:T(8,128)(2,1)S(1)}, u32[]{:S(2)}, u32[]{:S(2)}) collective-permute-start(bf16[64,640]{1,0:T(8,128)(2,1)S(1)} %get-tuple-element.87), channel_id=1, source_target_pairs={{0,1},{1,0},{2,3},{3,2},{4,5},{5,4},{6,7},{7,6},{8,9},{9,8},{10,11... | collective-permute-start | bytes 245768 | tf_op jit(solution)/shard_map/ppermute | solution.py:296
where the time goes:
time: 52.8 us; the launch traced here: 52.6 us
  starting transfers between devices  27.8 us (53%)
  waiting for transfers between devices  13.4 us (25%)
  Pallas kernels  10.1 us (19%)
  between operations  0.83 us (2%)
    ppermute x25, starting transfers between devices, swap(): lax.ppermute(value, axis, [(i, i ^ d) for i in range(lax.axis_size(axis))])  27.8 us
    ppermute x25, waiting for transfers between devices, swap(): lax.ppermute(value, axis, [(i, i ^ d) for i in range(lax.axis_size(axis))])  13.4 us
    pallas_call x9, Pallas kernels, call(): pl.pallas_call(kernel, out_shape=out_shape, in_specs=[pl.BlockSpec(memory...  10.1 us
  transfers between devices with their start and end apart: 25, of which 12 were waited for; matrix products, arithmetic and copies ran while one was open for 1% of the time, Pallas kernels for 10%

commit v1 on v0

--- a/solution.py
+++ b/solution.py
@@ -159,8 +159,13 @@
         gate = gate + jnp.dot(value, gate_ref[depth, :], preferred_element_type=F32)
         upper = upper + jnp.dot(value, up_ref[depth, :], preferred_element_type=F32)
     far = (gate / (1.0 + jnp.exp(-gate)) * upper).astype(BF16)
-    inner = jnp.concatenate([far, near_ref[...]], axis=0)
     count = far.shape[0]
+    groups = [
+        far[start : start + CAP]
+        for at in range(0, count // 2, CAP)
+        for start in (at, count // 2 + at)
+    ]
+    inner = jnp.concatenate([*groups, near_ref[...]], axis=0)
     for d in range(n_tp):
         down = columns_of(down_ref, part ^ d, n_tp, share)
         out = jnp.dot(inner, down, preferred_element_type=F32).astype(BF16)
@@ -366,7 +371,7 @@
         [pltpu.SemaphoreType.DMA((3,))],
         hbm=(1, 2, 3),
     )
-    mine = jnp.concatenate([arrived[order.index(d)] for d in range(4, n_ep)], axis=0)
+    mine = jnp.concatenate(arrived, axis=0)
     shares = spread(mine, n_tp)
     near_rows, far_rows = 4 * CAP, slots - 4 * CAP
     inner, gate_sum, up_sum = call(

time: 52.8 us -> 52 us (0.985)
  waiting for transfers between devices: 13.4 us -> 11.6 us
  starting transfers between devices: 27.8 us -> 28.8 us
    ppermute x25, waiting for transfers between devices: 13.4 us -> 11.6 us  [swap(): lax.ppermute(value, axis, [(i, i ^ d) for i in range(lax.axis_size(axis))])]
    ppermute x25, starting transfers between devices: 27.8 us -> 28.8 us  [swap(): lax.ppermute(value, axis, [(i, i ^ d) for i in range(lax.axis_size(axis))])]
  transfers between devices with their start and end apart: 25 -> 25, of which waited for: 12 -> 13; matrix products, arithmetic and copies ran while one was open for 1% -> 1% of each run, Pallas kernels for 10% -> 10%
where the time goes in v1:
time: 52 us; the launch traced here: 51.8 us
  starting transfers between devices  28.8 us (55%)
  waiting for transfers between devices  11.6 us (22%)
  Pallas kernels  10.1 us (19%)
  between operations  0.82 us (2%)
    ppermute x25, starting transfers between devices, swap(): lax.ppermute(value, axis, [(i, i ^ d) for i in range(lax.axis_size(axis))])  28.8 us
    ppermute x25, waiting for transfers between devices, swap(): lax.ppermute(value, axis, [(i, i ^ d) for i in range(lax.axis_size(axis))])  11.6 us
    pallas_call x9, Pallas kernels, call(): pl.pallas_call(kernel, out_shape=out_shape, in_specs=[pl.BlockSpec(memory...  10.1 us
  transfers between devices with their start and end apart: 25, of which 13 were waited for; matrix products, arithmetic and copies ran while one was open for 1% of the time, Pallas kernels for 10%

profile of v1, /device:TPU:0, one launch (start us, length us, event | category | flops | bytes accessed | tf_op | source)
XLA Modules:
  0.0 51.8 jit_solution(2289214992494614512)
XLA Ops:
  0.6 2.3 %shard_map.131 = (bf16[16,3584]{1,0:T(8,128)(2,1)S(1)}, bf16[64,896]{1,0:T(8,128)(2,1)S(1)}, bf16[128,896]{1,0:T(8,128)(2,1)S(1)}, bf16[16,896]{1,0:T(8,128)(2,1...) custom-call(s32[8,256]{1,0:T(8,128)} %bitcast.16, ...), custom_call_target="tpu_custom_call" | custom-call | flops 469762048 | bytes 1865728 | tf_op jit(solution)/shard_map/pallas_call | solution.py:287
  3.0 4.1 %collective-permute-start = (bf16[16,896]{1,0:T(8,128)(2,1)S(1)}, bf16[16,896]{1,0:T(8,128)(2,1)S(1)}, u32[]{:S(2)}, u32[]{:S(2)}) collective-permute-start(bf16[16,896]{1,0:T(8,128)(2,1)S(1)} %get-tuple-element.46), channel_id=1, source_target_pairs={{0,16},{4,20},{8,24},{12,28},{16,0},{20,4},{24,8},{28,12},{1,17},{... | collective-permute-start | bytes 86024 | tf_op jit(solution)/shard_map/ppermute | solution.py:301
  7.1 1.3 %collective-permute-start.1 = (bf16[16,896]{1,0:T(8,128)(2,1)S(1)}, bf16[16,896]{1,0:T(8,128)(2,1)S(1)}, u32[]{:S(2)}, u32[]{:S(2)}) collective-permute-start(bf16[16,896]{1,0:T(8,128)(2,1)S(1)} %get-tuple-element.47), channel_id=1, source_target_pairs={{0,24},{4,28},{8,16},{12,20},{16,8},{20,12},{24,0},{28,4},{1,25},{... | collective-permute-start | bytes 86024 | tf_op jit(solution)/shard_map/ppermute | solution.py:301
  9.0 1.7 %collective-permute-start.3 = (bf16[16,896]{1,0:T(8,128)(2,1)S(1)}, bf16[16,896]{1,0:T(8,128)(2,1)S(1)}, u32[]{:S(2)}, u32[]{:S(2)}) collective-permute-start(bf16[16,896]{1,0:T(8,128)(2,1)S(1)} %get-tuple-element.49), channel_id=1, source_target_pairs={{0,28},{4,24},{8,20},{12,16},{16,12},{20,8},{24,4},{28,0},{1,29},{... | collective-permute-start | bytes 86024 | tf_op jit(solution)/shard_map/ppermute | solution.py:301
  10.8 1.0 %collective-permute-start.8 = (bf16[64,896]{1,0:T(8,128)(2,1)S(1)}, bf16[64,896]{1,0:T(8,128)(2,1)S(1)}, u32[]{:S(2)}, u32[]{:S(2)}) collective-permute-start(bf16[64,896]{1,0:T(8,128)(2,1)S(1)} %get-tuple-element.91), channel_id=1, source_target_pairs={{0,8},{4,12},{8,0},{12,4},{16,24},{20,28},{24,16},{28,20},{1,9},{5... | collective-permute-start | bytes 344072 | tf_op jit(solution)/shard_map/ppermute | solution.py:301
  11.7 0.7 %collective-permute-start.9 = (bf16[64,896]{1,0:T(8,128)(2,1)S(1)}, bf16[64,896]{1,0:T(8,128)(2,1)S(1)}, u32[]{:S(2)}, u32[]{:S(2)}) collective-permute-start(bf16[64,896]{1,0:T(8,128)(2,1)S(1)} %get-tuple-element.90), channel_id=1, source_target_pairs={{0,12},{4,8},{8,4},{12,0},{16,28},{20,24},{24,20},{28,16},{1,13},{... | collective-permute-start | bytes 344072 | tf_op jit(solution)/shard_map/ppermute | solution.py:301
  13.5 0.7 %collective-permute-done.3 = bf16[16,896]{1,0:T(8,128)(2,1)S(1)} collective-permute-done((bf16[16,896]{1,0:T(8,128)(2,1)S(1)}, bf16[16,896]{1,0:T(8,128)(2,1)S(1)}, u32[]{:S(2)}, u32[]{:S(2)}) %collective-permute-start.3) | collective-permute-done | bytes 28704 | tf_op jit(solution)/shard_map/ppermute | solution.py:301
  14.2 2.5 %collective-permute-start.4 = (bf16[64,896]{1,0:T(8,128)(2,1)S(1)}, bf16[64,896]{1,0:T(8,128)(2,1)S(1)}, u32[]{:S(2)}, u32[]{:S(2)}) collective-permute-start(bf16[64,896]{1,0:T(8,128)(2,1)S(1)} %constant_dynamic-update-slice_fusion.mine_ref), channel_id=1, source_target_pairs={{0,3},{1,2},{2,1},{3,0},{4,7},{5,6},{6,5},{7,4},{8,11},{9,10},{10,... | collective-permute-start | bytes 344072 | tf_op jit(solution)/shard_map/ppermute | solution.py:301
  17.2 1.4 %collective-permute-start.6 = (bf16[64,896]{1,0:T(8,128)(2,1)S(1)}, bf16[64,896]{1,0:T(8,128)(2,1)S(1)}, u32[]{:S(2)}, u32[]{:S(2)}) collective-permute-start(bf16[64,896]{1,0:T(8,128)(2,1)S(1)} %constant_dynamic-update-slice_fusion.mine_ref), channel_id=1, source_target_pairs={{0,1},{1,0},{2,3},{3,2},{4,5},{5,4},{6,7},{7,6},{8,9},{9,8},{10,11... | collective-permute-start | bytes 344072 | tf_op jit(solution)/shard_map/ppermute | solution.py:301
  18.6 2.6 %shard_map.132 = (bf16[3584,256]{1,0:T(8,128)(2,1)S(1)}, bf16[3584,256]{1,0:T(8,128)(2,1)S(1)}, bf16[256,3584]{1,0:T(8,128)(2,1)S(1)}, f32[8,128]{1,0:T(8,128)S(1)}) custom-call(bf16[128,256]{1,0:T(8,128)(2,1)S(1)} %get-tuple-element.66.after_ref.combine_ref, bf16[3584,256]{1,0:T(8,128)(2,1)} %bitcast.13, bf16[3584,256]{1,0:T(8,128)(2,1)} %bitcast.14, ...), custom_call_target="tpu_custom_call" | custom-call | bytes 5570560 | tf_op jit(solution)/shard_map/pallas_call | solution.py:287
  21.3 0.9 %shard_map.133 = (bf16[64,256]{1,0:T(8,128)(2,1)S(1)}, f32[64,256]{1,0:T(8,128)S(1)}, f32[64,256]{1,0:T(8,128)S(1)}) custom-call(bf16[16,3584]{1,0:T(8,128)(2,1)S(1)} %get-tuple-element.54.own_ref, bf16[64,896]{1,0:T(8,128)(2,1)S(1)} %collective-permute-done.7.core_ref, bf16[64,896]{1,0:T(8,128)(2,1)S(1)} %collective-permute-done.8.near_ref, ...), custom_call_target="tpu_custom_call" | custom-call | flops 234881024 | bytes 4247552 | tf_op jit(solution)/shard_map/pallas_call | solution.py:287
  22.2 1.4 %collective-permute-done.5.refs_1_ = bf16[64,896]{1,0:T(8,128)(2,1)S(1)} collective-permute-done((bf16[64,896]{1,0:T(8,128)(2,1)S(1)}, bf16[64,896]{1,0:T(8,128)(2,1)S(1)}, u32[]{:S(2)}, u32[]{:S(2)}) %collective-permute-start.5) | collective-permute-done | bytes 114720 | tf_op jit(solution)/shard_map/ppermute | solution.py:301
  23.6 1.0 %shard_map.134 = (bf16[64,896]{1,0:T(8,128)(2,1)S(1)}, bf16[64,896]{1,0:T(8,128)(2,1)S(1)}, bf16[64,896]{1,0:T(8,128)(2,1)S(1)}, bf16[64,896]{1,0:T(8,128)(2,1)S...) custom-call(bf16[64,896]{1,0:T(8,128)(2,1)S(1)} %collective-permute-, ...), custom_call_target="tpu_custom_call" | custom-call | flops 704643072 | bytes 6012928 | tf_op jit(solution)/shard_map/pallas_call | solution.py:287
  24.6 2.0 %collective-permute-start.16 = (bf16[64,896]{1,0:T(8,128)(2,1)S(1)}, bf16[64,896]{1,0:T(8,128)(2,1)S(1)}, u32[]{:S(2)}, u32[]{:S(2)}) collective-permute-start(bf16[64,896]{1,0:T(8,128)(2,1)S(1)} %get-tuple-element.77), channel_id=1, source_target_pairs={{0,3},{1,2},{2,1},{3,0},{4,7},{5,6},{6,5},{7,4},{8,11},{9,10},{10,... | collective-permute-start | bytes 344072 | tf_op jit(solution)/shard_map/ppermute | solution.py:301
  26.6 1.1 %collective-permute-start.17 = (bf16[64,896]{1,0:T(8,128)(2,1)S(1)}, bf16[64,896]{1,0:T(8,128)(2,1)S(1)}, u32[]{:S(2)}, u32[]{:S(2)}) collective-permute-start(bf16[64,896]{1,0:T(8,128)(2,1)S(1)} %get-tuple-element.78), channel_id=1, source_target_pairs={{0,2},{1,3},{2,0},{3,1},{4,6},{5,7},{6,4},{7,5},{8,10},{9,11},{10,... | collective-permute-start | bytes 344072 | tf_op jit(solution)/shard_map/ppermute | solution.py:301
  28.2 1.4 %shard_map.135 = (bf16[256,896]{1,0:T(8,128)(2,1)S(1)}, bf16[256,128]{1,0:T(8,128)(2,1)S(1)}, f32[64,1]{1,0:T(8,128)S(1)}) custom-call(s32[1,256]{1,0:T(1,128)S(1)} %bitcast.11, s32[1,256]{1,0:T(1,128)S(1)} %bitcast.12, bf16[128,256]{1,0:T(8,128)(2,1)S(1)} %get-tuple-element.66.after_ref.combine_ref, bf16[256,3584]{1,0:T(8,128)(2,1)} %hidden_hbm.3), custom_call_target="tpu_custom_call" | custom-call | flops 134217728 | bytes 1902592 | tf_op jit(solution)/shard_map/pallas_call | solution.py:287
  29.6 2.0 %collective-permute-start.10 = (bf16[64,896]{1,0:T(8,128)(2,1)S(1)}, bf16[64,896]{1,0:T(8,128)(2,1)S(1)}, u32[]{:S(2)}, u32[]{:S(2)}) collective-permute-start(bf16[64,896]{1,0:T(8,128)(2,1)S(1)} %get-tuple-element.69), channel_id=1, source_target_pairs={{0,3},{1,2},{2,1},{3,0},{4,7},{5,6},{6,5},{7,4},{8,11},{9,10},{10,... | collective-permute-start | bytes 344072 | tf_op jit(solution)/shard_map/ppermute | solution.py:301
  31.6 1.1 %collective-permute-start.11 = (bf16[64,896]{1,0:T(8,128)(2,1)S(1)}, bf16[64,896]{1,0:T(8,128)(2,1)S(1)}, u32[]{:S(2)}, u32[]{:S(2)}) collective-permute-start(bf16[64,896]{1,0:T(8,128)(2,1)S(1)} %get-tuple-element.70), channel_id=1, source_target_pairs={{0,2},{1,3},{2,0},{3,1},{4,6},{5,7},{6,4},{7,5},{8,10},{9,11},{10,... | collective-permute-start | bytes 344072 | tf_op jit(solution)/shard_map/ppermute | solution.py:301
  33.2 1.7 %collective-permute-done.17.refs_1_ = bf16[64,896]{1,0:T(8,128)(2,1)S(1)} collective-permute-done((bf16[64,896]{1,0:T(8,128)(2,1)S(1)}, bf16[64,896]{1,0:T(8,128)(2,1)S(1)}, u32[]{:S(2)}, u32[]{:S(2)}) %collective-permute-start.17) | collective-permute-done | bytes 114720 | tf_op jit(solution)/shard_map/ppermute | solution.py:301
  35.0 0.7 %collective-permute-start.19 = (bf16[32,896]{1,0:T(8,128)(2,1)S(1)}, bf16[32,896]{1,0:T(8,128)(2,1)S(1)}, u32[]{:S(2)}, u32[]{:S(2)}) collective-permute-start(bf16[32,896]{1,0:T(8,128)(2,1)S(1)} %get-tuple-element.81), channel_id=1, source_target_pairs={{0,16},{4,20},{8,24},{12,28},{16,0},{20,4},{24,8},{28,12},{1,17},{... | collective-permute-start | bytes 172040 | tf_op jit(solution)/shard_map/ppermute | solution.py:301
  35.6 1.4 %collective-permute-start.20 = (bf16[32,896]{1,0:T(8,128)(2,1)S(1)}, bf16[32,896]{1,0:T(8,128)(2,1)S(1)}, u32[]{:S(2)}, u32[]{:S(2)}) collective-permute-start(bf16[32,896]{1,0:T(8,128)(2,1)S(1)} %get-tuple-element.82), channel_id=1, source_target_pairs={{0,24},{4,28},{8,16},{12,20},{16,8},{20,12},{24,0},{28,4},{1,25},{... | collective-permute-start | bytes 172040 | tf_op jit(solution)/shard_map/ppermute | solution.py:301
  37.0 1.1 %collective-permute-done.11.refs_1_ = bf16[64,896]{1,0:T(8,128)(2,1)S(1)} collective-permute-done((bf16[64,896]{1,0:T(8,128)(2,1)S(1)}, bf16[64,896]{1,0:T(8,128)(2,1)S(1)}, u32[]{:S(2)}, u32[]{:S(2)}) %collective-permute-start.11) | collective-permute-done | bytes 114720 | tf_op jit(solution)/shard_map/ppermute | solution.py:301
  38.8 1.5 %collective-permute-start.15 = (bf16[16,896]{1,0:T(8,128)(2,1)S(1)}, bf16[16,896]{1,0:T(8,128)(2,1)S(1)}, u32[]{:S(2)}, u32[]{:S(2)}) collective-permute-start(bf16[16,896]{1,0:T(8,128)(2,1)S(1)} %get-tuple-element.76), channel_id=1, source_target_pairs={{0,12},{4,8},{8,4},{12,0},{16,28},{20,24},{24,20},{28,16},{1,13},{... | collective-permute-start | bytes 86024 | tf_op jit(solution)/shard_map/ppermute | solution.py:301
  40.7 1.1 %collective-permute-done.20.refs_5_ = bf16[32,896]{1,0:T(8,128)(2,1)S(1)} collective-permute-done((bf16[32,896]{1,0:T(8,128)(2,1)S(1)}, bf16[32,896]{1,0:T(8,128)(2,1)S(1)}, u32[]{:S(2)}, u32[]{:S(2)}) %collective-permute-start.20) | collective-permute-done | bytes 57376 | tf_op jit(solution)/shard_map/ppermute | solution.py:301
  42.0 0.7 %collective-permute-done.14.refs_2_ = bf16[16,896]{1,0:T(8,128)(2,1)S(1)} collective-permute-done((bf16[16,896]{1,0:T(8,128)(2,1)S(1)}, bf16[16,896]{1,0:T(8,128)(2,1)S(1)}, u32[]{:S(2)}, u32[]{:S(2)}) %collective-permute-start.14) | collective-permute-done | bytes 28704 | tf_op jit(solution)/shard_map/ppermute | solution.py:301
  43.0 0.8 %shard_map.138 = (bf16[64,640]{1,0:T(8,128)(2,1)S(1)}, bf16[64,640]{1,0:T(8,128)(2,1)S(1)}, bf16[64,640]{1,0:T(8,128)(2,1)S(1)}, bf16[64,640]{1,0:T(8,128)(2,1)S(1)}) custom-call(bf16[16,896]{1,0:T(8,128)(2,1)S(1)} %get-tuple-element.73.refs_0_, bf16[16,896]{1,0:T(8,128)(2,1)S(1)} %collective-permute-done.13.refs_1_, ...), custom_call_target="tpu_custom_call" | custom-call | flops 322961408 | bytes 1846784 | tf_op jit(solution)/shard_map/pallas_call | solution.py:287
  43.8 1.1 %collective-permute-start.22 = (bf16[64,640]{1,0:T(8,128)(2,1)S(1)}, bf16[64,640]{1,0:T(8,128)(2,1)S(1)}, u32[]{:S(2)}, u32[]{:S(2)}) collective-permute-start(bf16[64,640]{1,0:T(8,128)(2,1)S(1)} %get-tuple-element.85), channel_id=1, source_target_pairs={{0,3},{1,2},{2,1},{3,0},{4,7},{5,6},{6,5},{7,4},{8,11},{9,10},{10,... | collective-permute-start | bytes 245768 | tf_op jit(solution)/shard_map/ppermute | solution.py:301
  44.9 1.4 %collective-permute-start.23 = (bf16[64,640]{1,0:T(8,128)(2,1)S(1)}, bf16[64,640]{1,0:T(8,128)(2,1)S(1)}, u32[]{:S(2)}, u32[]{:S(2)}) collective-permute-start(bf16[64,640]{1,0:T(8,128)(2,1)S(1)} %get-tuple-element.86), channel_id=1, source_target_pairs={{0,2},{1,3},{2,0},{3,1},{4,6},{5,7},{6,4},{7,5},{8,10},{9,11},{10,... | collective-permute-start | bytes 245768 | tf_op jit(solution)/shard_map/ppermute | solution.py:301
  46.3 1.1 %collective-permute-start.24 = (bf16[64,640]{1,0:T(8,128)(2,1)S(1)}, bf16[64,640]{1,0:T(8,128)(2,1)S(1)}, u32[]{:S(2)}, u32[]{:S(2)}) collective-permute-start(bf16[64,640]{1,0:T(8,128)(2,1)S(1)} %get-tuple-element.87), channel_id=1, source_target_pairs={{0,1},{1,0},{2,3},{3,2},{4,5},{5,4},{6,7},{7,6},{8,9},{9,8},{10,11... | collective-permute-start | bytes 245768 | tf_op jit(solution)/shard_map/ppermute | solution.py:301
  47.6 2.5 %collective-permute-done.22.refs_0_ = bf16[64,640]{1,0:T(8,128)(2,1)S(1)} collective-permute-done((bf16[64,640]{1,0:T(8,128)(2,1)S(1)}, bf16[64,640]{1,0:T(8,128)(2,1)S(1)}, u32[]{:S(2)}, u32[]{:S(2)}) %collective-permute-start.22) | collective-permute-done | bytes 81952 | tf_op jit(solution)/shard_map/ppermute | solution.py:301
  50.1 0.7 %collective-permute-done.23.refs_1_ = bf16[64,640]{1,0:T(8,128)(2,1)S(1)} collective-permute-done((bf16[64,640]{1,0:T(8,128)(2,1)S(1)}, bf16[64,640]{1,0:T(8,128)(2,1)S(1)}, u32[]{:S(2)}, u32[]{:S(2)}) %collective-permute-start.23) | collective-permute-done | bytes 81952 | tf_op jit(solution)/shard_map/ppermute | solution.py:301
  50.9 0.9 %shard_map.139 = (bf16[64,512]{1,0:T(8,128)(2,1)}, bf16[64,64]{1,0:T(8,128)(2,1)}) custom-call(bf16[64,640]{1,0:T(8,128)(2,1)S(1)} %collective-permute-done.22.refs_0_, bf16[64,640]{1,0:T(8,128)(2,1)S(1)} %collective-permute-done.23.refs_1_, bf16[64,640]{1,0:T(8,128)(2,1)S(1)} %collective-permute-done.24.refs_2_, ...), custom_call_target="tpu_custom_call" | custom-call | bytes 346112 | tf_op jit(solution)/shard_map/pallas_call | solution.py:287
  (49 shorter events, 5.1 us)
Async XLA Ops:
  3.0 8.7 %collective-permute-start = (bf16[16,896]{1,0:T(8,128)(2,1)S(1)}, bf16[16,896]{1,0:T(8,128)(2,1)S(1)}, u32[]{:S(2)}, u32[]{:S(2)}) collective-permute-start(bf16[16,896]{1,0:T(8,128)(2,1)S(1)} %get-tuple-element.46), channel_id=1, source_target_pairs={{0,16},{4,20},{8,24},{12,28},{16,0},{20,4},{24,8},{28,12},{1,17},{... | collective-permute-start | bytes 86024 | tf_op jit(solution)/shard_map/ppermute | solution.py:301
  7.1 5.7 %collective-permute-start.1 = (bf16[16,896]{1,0:T(8,128)(2,1)S(1)}, bf16[16,896]{1,0:T(8,128)(2,1)S(1)}, u32[]{:S(2)}, u32[]{:S(2)}) collective-permute-start(bf16[16,896]{1,0:T(8,128)(2,1)S(1)} %get-tuple-element.47), channel_id=1, source_target_pairs={{0,24},{4,28},{8,16},{12,20},{16,8},{20,12},{24,0},{28,4},{1,25},{... | collective-permute-start | bytes 86024 | tf_op jit(solution)/shard_map/ppermute | solution.py:301
  8.4 5.1 %collective-permute-start.2 = (bf16[16,896]{1,0:T(8,128)(2,1)S(1)}, bf16[16,896]{1,0:T(8,128)(2,1)S(1)}, u32[]{:S(2)}, u32[]{:S(2)}) collective-permute-start(bf16[16,896]{1,0:T(8,128)(2,1)S(1)} %get-tuple-element.48), channel_id=1, source_target_pairs={{0,20},{4,16},{8,28},{12,24},{16,4},{20,0},{24,12},{28,8},{1,21},{... | collective-permute-start | bytes 86024 | tf_op jit(solution)/shard_map/ppermute | solution.py:301
  9.0 5.2 %collective-permute-start.3 = (bf16[16,896]{1,0:T(8,128)(2,1)S(1)}, bf16[16,896]{1,0:T(8,128)(2,1)S(1)}, u32[]{:S(2)}, u32[]{:S(2)}) collective-permute-start(bf16[16,896]{1,0:T(8,128)(2,1)S(1)} %get-tuple-element.49), channel_id=1, source_target_pairs={{0,28},{4,24},{8,20},{12,16},{16,12},{20,8},{24,4},{28,0},{1,29},{... | collective-permute-start | bytes 86024 | tf_op jit(solution)/shard_map/ppermute | solution.py:301
  10.8 6.4 %collective-permute-start.8 = (bf16[64,896]{1,0:T(8,128)(2,1)S(1)}, bf16[64,896]{1,0:T(8,128)(2,1)S(1)}, u32[]{:S(2)}, u32[]{:S(2)}) collective-permute-start(bf16[64,896]{1,0:T(8,128)(2,1)S(1)} %get-tuple-element.91), channel_id=1, source_target_pairs={{0,8},{4,12},{8,0},{12,4},{16,24},{20,28},{24,16},{28,20},{1,9},{5... | collective-permute-start | bytes 344072 | tf_op jit(solution)/shard_map/ppermute | solution.py:301
  11.7 9.5 %collective-permute-start.9 = (bf16[64,896]{1,0:T(8,128)(2,1)S(1)}, bf16[64,896]{1,0:T(8,128)(2,1)S(1)}, u32[]{:S(2)}, u32[]{:S(2)}) collective-permute-start(bf16[64,896]{1,0:T(8,128)(2,1)S(1)} %get-tuple-element.90), channel_id=1, source_target_pairs={{0,12},{4,8},{8,4},{12,0},{16,28},{20,24},{24,20},{28,16},{1,13},{... | collective-permute-start | bytes 344072 | tf_op jit(solution)/shard_map/ppermute | solution.py:301
  12.7 8.5 %collective-permute-start.7 = (bf16[64,896]{1,0:T(8,128)(2,1)S(1)}, bf16[64,896]{1,0:T(8,128)(2,1)S(1)}, u32[]{:S(2)}, u32[]{:S(2)}) collective-permute-start(bf16[64,896]{1,0:T(8,128)(2,1)S(1)} %get-tuple-element.55), channel_id=1, source_target_pairs={{0,4},{4,0},{8,12},{12,8},{16,20},{20,16},{24,28},{28,24},{1,5},{5... | collective-permute-start | bytes 344072 | tf_op jit(solution)/shard_map/ppermute | solution.py:301
  14.2 8.0 %collective-permute-start.4 = (bf16[64,896]{1,0:T(8,128)(2,1)S(1)}, bf16[64,896]{1,0:T(8,128)(2,1)S(1)}, u32[]{:S(2)}, u32[]{:S(2)}) collective-permute-start(bf16[64,896]{1,0:T(8,128)(2,1)S(1)} %constant_dynamic-update-slice_fusion.mine_ref), channel_id=1, source_target_pairs={{0,3},{1,2},{2,1},{3,0},{4,7},{5,6},{6,5},{7,4},{8,11},{9,10},{10,... | collective-permute-start | bytes 344072 | tf_op jit(solution)/shard_map/ppermute | solution.py:301
  16.7 6.9 %collective-permute-start.5 = (bf16[64,896]{1,0:T(8,128)(2,1)S(1)}, bf16[64,896]{1,0:T(8,128)(2,1)S(1)}, u32[]{:S(2)}, u32[]{:S(2)}) collective-permute-start(bf16[64,896]{1,0:T(8,128)(2,1)S(1)} %constant_dynamic-update-slice_fusion.mine_ref), channel_id=1, source_target_pairs={{0,2},{1,3},{2,0},{3,1},{4,6},{5,7},{6,4},{7,5},{8,10},{9,11},{10,... | collective-permute-start | bytes 344072 | tf_op jit(solution)/shard_map/ppermute | solution.py:301
  17.2 6.4 %collective-permute-start.6 = (bf16[64,896]{1,0:T(8,128)(2,1)S(1)}, bf16[64,896]{1,0:T(8,128)(2,1)S(1)}, u32[]{:S(2)}, u32[]{:S(2)}) collective-permute-start(bf16[64,896]{1,0:T(8,128)(2,1)S(1)} %constant_dynamic-update-slice_fusion.mine_ref), channel_id=1, source_target_pairs={{0,1},{1,0},{2,3},{3,2},{4,5},{5,4},{6,7},{7,6},{8,9},{9,8},{10,11... | collective-permute-start | bytes 344072 | tf_op jit(solution)/shard_map/ppermute | solution.py:301
  23.6 4.6 %copy-start.2 = (s32[256]{0:T(256)S(1)}, s32[256]{0:T(256)}, u32[]{:S(2)}) copy-start(s32[256]{0:T(256)} %param.23) | copy-start | bytes 3076
  23.6 4.6 %copy-start.3 = (s32[256]{0:T(256)S(1)}, s32[256]{0:T(256)}, u32[]{:S(2)}) copy-start(s32[256]{0:T(256)} %param.22) | copy-start | bytes 3076
  24.6 17.2 %copy-start.4 = (f32[896]{0:T(1024)S(1)}, f32[896]{0:T(1024)}, u32[]{:S(2)}) copy-start(f32[896]{0:T(1024)} %param.19) | copy-start | bytes 10756
  24.6 18.4 %copy-start = (bf16[896,576]{0,1:T(8,128)(2,1)S(1)}, bf16[896,576]{0,1:T(8,128)(2,1)}, u32[]{:S(2)}) copy-start(bf16[896,576]{0,1:T(8,128)(2,1)} %param.20) | copy-start | bytes 3096580
  24.6 8.0 %collective-permute-start.16 = (bf16[64,896]{1,0:T(8,128)(2,1)S(1)}, bf16[64,896]{1,0:T(8,128)(2,1)S(1)}, u32[]{:S(2)}, u32[]{:S(2)}) collective-permute-start(bf16[64,896]{1,0:T(8,128)(2,1)S(1)} %get-tuple-element.77), channel_id=1, source_target_pairs={{0,3},{1,2},{2,1},{3,0},{4,7},{5,6},{6,5},{7,4},{8,11},{9,10},{10,... | collective-permute-start | bytes 344072 | tf_op jit(solution)/shard_map/ppermute | solution.py:301
  26.6 8.3 %collective-permute-start.17 = (bf16[64,896]{1,0:T(8,128)(2,1)S(1)}, bf16[64,896]{1,0:T(8,128)(2,1)S(1)}, u32[]{:S(2)}, u32[]{:S(2)}) collective-permute-start(bf16[64,896]{1,0:T(8,128)(2,1)S(1)} %get-tuple-element.78), channel_id=1, source_target_pairs={{0,2},{1,3},{2,0},{3,1},{4,6},{5,7},{6,4},{7,5},{8,10},{9,11},{10,... | collective-permute-start | bytes 344072 | tf_op jit(solution)/shard_map/ppermute | solution.py:301
  27.7 7.2 %collective-permute-start.18 = (bf16[64,896]{1,0:T(8,128)(2,1)S(1)}, bf16[64,896]{1,0:T(8,128)(2,1)S(1)}, u32[]{:S(2)}, u32[]{:S(2)}) collective-permute-start(bf16[64,896]{1,0:T(8,128)(2,1)S(1)} %get-tuple-element.79), channel_id=1, source_target_pairs={{0,1},{1,0},{2,3},{3,2},{4,5},{5,4},{6,7},{7,6},{8,9},{9,8},{10,11... | collective-permute-start | bytes 344072 | tf_op jit(solution)/shard_map/ppermute | solution.py:301
  29.6 21.3 %copy-start.1 = (f32[512]{0:T(512)S(1)}, f32[512]{0:T(512)}, u32[]{:S(2)}) copy-start(f32[512]{0:T(512)} %param.21) | copy-start | bytes 6148
  29.6 7.4 %collective-permute-start.10 = (bf16[64,896]{1,0:T(8,128)(2,1)S(1)}, bf16[64,896]{1,0:T(8,128)(2,1)S(1)}, u32[]{:S(2)}, u32[]{:S(2)}) collective-permute-start(bf16[64,896]{1,0:T(8,128)(2,1)S(1)} %get-tuple-element.69), channel_id=1, source_target_pairs={{0,3},{1,2},{2,1},{3,0},{4,7},{5,6},{6,5},{7,4},{8,11},{9,10},{10,... | collective-permute-start | bytes 344072 | tf_op jit(solution)/shard_map/ppermute | solution.py:301
  31.6 6.5 %collective-permute-start.11 = (bf16[64,896]{1,0:T(8,128)(2,1)S(1)}, bf16[64,896]{1,0:T(8,128)(2,1)S(1)}, u32[]{:S(2)}, u32[]{:S(2)}) collective-permute-start(bf16[64,896]{1,0:T(8,128)(2,1)S(1)} %get-tuple-element.70), channel_id=1, source_target_pairs={{0,2},{1,3},{2,0},{3,1},{4,6},{5,7},{6,4},{7,5},{8,10},{9,11},{10,... | collective-permute-start | bytes 344072 | tf_op jit(solution)/shard_map/ppermute | solution.py:301
  32.7 5.6 %collective-permute-start.12 = (bf16[64,896]{1,0:T(8,128)(2,1)S(1)}, bf16[64,896]{1,0:T(8,128)(2,1)S(1)}, u32[]{:S(2)}, u32[]{:S(2)}) collective-permute-start(bf16[64,896]{1,0:T(8,128)(2,1)S(1)} %get-tuple-element.71), channel_id=1, source_target_pairs={{0,1},{1,0},{2,3},{3,2},{4,5},{5,4},{6,7},{7,6},{8,9},{9,8},{10,11... | collective-permute-start | bytes 344072 | tf_op jit(solution)/shard_map/ppermute | solution.py:301
  35.0 5.7 %collective-permute-start.19 = (bf16[32,896]{1,0:T(8,128)(2,1)S(1)}, bf16[32,896]{1,0:T(8,128)(2,1)S(1)}, u32[]{:S(2)}, u32[]{:S(2)}) collective-permute-start(bf16[32,896]{1,0:T(8,128)(2,1)S(1)} %get-tuple-element.81), channel_id=1, source_target_pairs={{0,16},{4,20},{8,24},{12,28},{16,0},{20,4},{24,8},{28,12},{1,17},{... | collective-permute-start | bytes 172040 | tf_op jit(solution)/shard_map/ppermute | solution.py:301
  35.6 6.1 %collective-permute-start.20 = (bf16[32,896]{1,0:T(8,128)(2,1)S(1)}, bf16[32,896]{1,0:T(8,128)(2,1)S(1)}, u32[]{:S(2)}, u32[]{:S(2)}) collective-permute-start(bf16[32,896]{1,0:T(8,128)(2,1)S(1)} %get-tuple-element.82), channel_id=1, source_target_pairs={{0,24},{4,28},{8,16},{12,20},{16,8},{20,12},{24,0},{28,4},{1,25},{... | collective-permute-start | bytes 172040 | tf_op jit(solution)/shard_map/ppermute | solution.py:301
  38.3 3.7 %collective-permute-start.13 = (bf16[16,896]{1,0:T(8,128)(2,1)S(1)}, bf16[16,896]{1,0:T(8,128)(2,1)S(1)}, u32[]{:S(2)}, u32[]{:S(2)}) collective-permute-start(bf16[16,896]{1,0:T(8,128)(2,1)S(1)} %get-tuple-element.74), channel_id=1, source_target_pairs={{0,4},{4,0},{8,12},{12,8},{16,20},{20,16},{24,28},{28,24},{1,5},{5... | collective-permute-start | bytes 86024 | tf_op jit(solution)/shard_map/ppermute | solution.py:301
  38.4 4.2 %collective-permute-start.14 = (bf16[16,896]{1,0:T(8,128)(2,1)S(1)}, bf16[16,896]{1,0:T(8,128)(2,1)S(1)}, u32[]{:S(2)}, u32[]{:S(2)}) collective-permute-start(bf16[16,896]{1,0:T(8,128)(2,1)S(1)} %get-tuple-element.75), channel_id=1, source_target_pairs={{0,8},{4,12},{8,0},{12,4},{16,24},{20,28},{24,16},{28,20},{1,9},{5... | collective-permute-start | bytes 86024 | tf_op jit(solution)/shard_map/ppermute | solution.py:301
  38.8 3.9 %collective-permute-start.15 = (bf16[16,896]{1,0:T(8,128)(2,1)S(1)}, bf16[16,896]{1,0:T(8,128)(2,1)S(1)}, u32[]{:S(2)}, u32[]{:S(2)}) collective-permute-start(bf16[16,896]{1,0:T(8,128)(2,1)S(1)} %get-tuple-element.76), channel_id=1, source_target_pairs={{0,12},{4,8},{8,4},{12,0},{16,28},{20,24},{24,20},{28,16},{1,13},{... | collective-permute-start | bytes 86024 | tf_op jit(solution)/shard_map/ppermute | solution.py:301
  41.7 1.3 %collective-permute-start.21 = (bf16[32,896]{1,0:T(8,128)(2,1)S(1)}, bf16[32,896]{1,0:T(8,128)(2,1)S(1)}, u32[]{:S(2)}, u32[]{:S(2)}) collective-permute-start(bf16[32,896]{1,0:T(8,128)(2,1)S(1)} %pad_maximum_fusion), channel_id=1, source_target_pairs={{0,4},{4,0},{8,12},{12,8},{16,20},{20,16},{24,28},{28,24},{1,5},{5... | collective-permute-start | bytes 172040 | tf_op jit(solution)/shard_map/ppermute | solution.py:301
  43.8 6.3 %collective-permute-start.22 = (bf16[64,640]{1,0:T(8,128)(2,1)S(1)}, bf16[64,640]{1,0:T(8,128)(2,1)S(1)}, u32[]{:S(2)}, u32[]{:S(2)}) collective-permute-start(bf16[64,640]{1,0:T(8,128)(2,1)S(1)} %get-tuple-element.85), channel_id=1, source_target_pairs={{0,3},{1,2},{2,1},{3,0},{4,7},{5,6},{6,5},{7,4},{8,11},{9,10},{10,... | collective-permute-start | bytes 245768 | tf_op jit(solution)/shard_map/ppermute | solution.py:301
  44.9 5.9 %collective-permute-start.23 = (bf16[64,640]{1,0:T(8,128)(2,1)S(1)}, bf16[64,640]{1,0:T(8,128)(2,1)S(1)}, u32[]{:S(2)}, u32[]{:S(2)}) collective-permute-start(bf16[64,640]{1,0:T(8,128)(2,1)S(1)} %get-tuple-element.86), channel_id=1, source_target_pairs={{0,2},{1,3},{2,0},{3,1},{4,6},{5,7},{6,4},{7,5},{8,10},{9,11},{10,... | collective-permute-start | bytes 245768 | tf_op jit(solution)/shard_map/ppermute | solution.py:301
  46.3 4.6 %collective-permute-start.24 = (bf16[64,640]{1,0:T(8,128)(2,1)S(1)}, bf16[64,640]{1,0:T(8,128)(2,1)S(1)}, u32[]{:S(2)}, u32[]{:S(2)}) collective-permute-start(bf16[64,640]{1,0:T(8,128)(2,1)S(1)} %get-tuple-element.87), channel_id=1, source_target_pairs={{0,1},{1,0},{2,3},{3,2},{4,5},{5,4},{6,7},{7,6},{8,9},{9,8},{10,11... | collective-permute-start | bytes 245768 | tf_op jit(solution)/shard_map/ppermute | solution.py:301

commit v2 on v1

--- a/solution.py
+++ b/solution.py
@@ -113,21 +113,9 @@
         copy.wait()
 
 
-def first_kernel(
-    n_tp,
-    own_ref,
-    core_ref,
-    near_ref,
-    cross_ref,
-    mine_ref,
-    gate_ref,
-    up_ref,
-    mark_ref,
-    inner_ref,
-    gate_sum_ref,
-    up_sum_ref,
-    head_ref,
-):
+def first_kernel(n_tp, own_ref, core_ref, near_ref, cross_ref, mine_ref, *refs):
+    gate_ref, up_ref, down_ref, _ = refs[:4]
+    outs, (gate_sum_ref, up_sum_ref, head_ref) = refs[4 : n_tp + 4], refs[n_tp + 4 :]
     part = lax.axis_index("tp")
     share = mine_ref.shape[1]
     head_ref[:CAP, :] = own_ref[...]
@@ -141,14 +129,16 @@
     )
     for weight_ref, sum_ref in zip((gate_ref, up_ref), (gate_sum_ref, up_sum_ref)):
         sum_ref[...] = jnp.dot(mine_ref[...], weight_ref[depth, :], preferred_element_type=F32)
-    inner_ref[...] = (gate / (1.0 + jnp.exp(-gate)) * upper).astype(BF16)
+    inner = (gate / (1.0 + jnp.exp(-gate)) * upper).astype(BF16)
+    for d in range(n_tp):
+        down = columns_of(down_ref, part ^ d, n_tp, share)
+        outs[d][...] = jnp.dot(inner, down, preferred_element_type=F32).astype(BF16)
 
 
 def expert_kernel(n_tp, *refs):
     rows = refs[: n_tp - 1]
-    gate_ref, up_ref, down_ref, near_ref, gate_sum_ref, up_sum_ref = refs[n_tp - 1 : n_tp + 5]
-    far_outs = refs[n_tp + 5 : 2 * n_tp + 5]
-    near_outs = refs[2 * n_tp + 5 :]
+    gate_ref, up_ref, down_ref, gate_sum_ref, up_sum_ref = refs[n_tp - 1 : n_tp + 4]
+    outs = refs[n_tp + 4 :]
     part = lax.axis_index("tp")
     share = rows[0].shape[1]
     gate = gate_sum_ref[...]
@@ -165,12 +155,10 @@
         for at in range(0, count // 2, CAP)
         for start in (at, count // 2 + at)
     ]
-    inner = jnp.concatenate([*groups, near_ref[...]], axis=0)
+    inner = jnp.concatenate(groups, axis=0)
     for d in range(n_tp):
         down = columns_of(down_ref, part ^ d, n_tp, share)
-        out = jnp.dot(inner, down, preferred_element_type=F32).astype(BF16)
-        far_outs[d][...] = out[:count]
-        near_outs[d][...] = out[count:]
+        outs[d][...] = jnp.dot(inner, down, preferred_element_type=F32).astype(BF16)
 
 
 def sum_kernel(n_tp, *refs):
@@ -371,20 +359,21 @@
         [pltpu.SemaphoreType.DMA((3,))],
         hbm=(1, 2, 3),
     )
+    arrived, from_core = lax.optimization_barrier((arrived, from_core))
     mine = jnp.concatenate(arrived, axis=0)
     shares = spread(mine, n_tp)
     near_rows, far_rows = 4 * CAP, slots - 4 * CAP
-    inner, gate_sum, up_sum = call(
+    *near_pieces, gate_sum, up_sum = call(
         functools.partial(first_kernel, n_tp),
-        [struct((near_rows, ff), BF16)] + [struct((far_rows, ff), F32)] * 2,
-        (own, from_core, near, near_crossed, mine, *loaded[:2], mark),
+        [struct((near_rows, share), BF16)] * n_tp + [struct((far_rows, ff), F32)] * 2,
+        (own, from_core, near, near_crossed, mine, *loaded, mark),
         [pltpu.VMEM((4 * CAP, width), BF16)],
         flops=2 * slots * width * ff,
     )
     terms = call(
         functools.partial(expert_kernel, n_tp),
-        [struct((far_rows, share), BF16)] * n_tp + [struct((near_rows, share), BF16)] * n_tp,
-        (*shares, *loaded, inner, gate_sum, up_sum),
+        [struct((far_rows, share), BF16)] * n_tp,
+        (*shares, *loaded, gate_sum, up_sum),
         flops=2 * slots * width * ff * 3,
     )
     terms = list(terms)
@@ -404,12 +393,12 @@
         flops=2 * n_tp * seats * tokens * (share + slots),
         hbm=(3,),
     )
-    near_pieces, rows, mix = lax.optimization_barrier((list(terms[n_tp:]), rows, mix))
+    near_pieces, rows, mix = lax.optimization_barrier((near_pieces, rows, mix))
     freqs = ROPE_BASE ** (-jnp.arange(half, dtype=F32) / half)
     angles = at * freqs[None, :]
     cosine, sine = jnp.cos(angles), jnp.sin(angles)
 
-    far_terms = collect(terms[:n_tp])
+    far_terms = collect(terms)
     near_terms = collect(near_pieces)
     far_done = call(
         functools.partial(sum_kernel, n_tp),

time: 52 us -> 52.7 us (1.013)
  waiting for transfers between devices: 11.6 us -> 14.7 us
  starting transfers between devices: 28.8 us -> 26.2 us
    ppermute x25, waiting for transfers between devices: 11.6 us -> 14.7 us  [swap(): lax.ppermute(value, axis, [(i, i ^ d) for i in range(lax.axis_size(axis))])]
    ppermute x25, starting transfers between devices: 28.8 us -> 26.2 us  [swap(): lax.ppermute(value, axis, [(i, i ^ d) for i in range(lax.axis_size(axis))])]
  transfers between devices with their start and end apart: 25 -> 25, of which waited for: 13 -> 15; matrix products, arithmetic and copies ran while one was open for 1% -> 1% of each run, Pallas kernels for 10% -> 10%
where the time goes in v2:
time: 52.7 us; the launch traced here: 52.5 us
  starting transfers between devices  26.2 us (50%)
  waiting for transfers between devices  14.7 us (28%)
  Pallas kernels  10.3 us (20%)
  between operations  0.83 us (2%)
    ppermute x25, starting transfers between devices, swap(): lax.ppermute(value, axis, [(i, i ^ d) for i in range(lax.axis_size(axis))])  26.2 us
    ppermute x25, waiting for transfers between devices, swap(): lax.ppermute(value, axis, [(i, i ^ d) for i in range(lax.axis_size(axis))])  14.7 us
    pallas_call x9, Pallas kernels, call(): pl.pallas_call(kernel, out_shape=out_shape, in_specs=[pl.BlockSpec(memory...  10.3 us
  transfers between devices with their start and end apart: 25, of which 15 were waited for; matrix products, arithmetic and copies ran while one was open for 1% of the time, Pallas kernels for 10%

profile of v2, /device:TPU:0, one launch (start us, length us, event | category | flops | bytes accessed | tf_op | source)
XLA Modules:
  0.0 52.5 jit_solution(1963367422377411818)
XLA Ops:
  0.6 2.3 %shard_map.131 = (bf16[16,3584]{1,0:T(8,128)(2,1)S(1)}, bf16[64,896]{1,0:T(8,128)(2,1)S(1)}, bf16[128,896]{1,0:T(8,128)(2,1)S(1)}, bf16[16,896]{1,0:T(8,128)(2,1...) custom-call(s32[8,256]{1,0:T(8,128)} %bitcast.16, ...), custom_call_target="tpu_custom_call" | custom-call | flops 469762048 | bytes 1865728 | tf_op jit(solution)/shard_map/pallas_call | solution.py:275
  3.0 4.1 %collective-permute-start = (bf16[16,896]{1,0:T(8,128)(2,1)S(1)}, bf16[16,896]{1,0:T(8,128)(2,1)S(1)}, u32[]{:S(2)}, u32[]{:S(2)}) collective-permute-start(bf16[16,896]{1,0:T(8,128)(2,1)S(1)} %get-tuple-element.51), channel_id=1, source_target_pairs={{0,16},{4,20},{8,24},{12,28},{16,0},{20,4},{24,8},{28,12},{1,17},{... | collective-permute-start | bytes 86024 | tf_op jit(solution)/shard_map/ppermute | solution.py:289
  7.1 1.3 %collective-permute-start.1 = (bf16[16,896]{1,0:T(8,128)(2,1)S(1)}, bf16[16,896]{1,0:T(8,128)(2,1)S(1)}, u32[]{:S(2)}, u32[]{:S(2)}) collective-permute-start(bf16[16,896]{1,0:T(8,128)(2,1)S(1)} %get-tuple-element.52), channel_id=1, source_target_pairs={{0,24},{4,28},{8,16},{12,20},{16,8},{20,12},{24,0},{28,4},{1,25},{... | collective-permute-start | bytes 86024 | tf_op jit(solution)/shard_map/ppermute | solution.py:289
  9.0 1.7 %collective-permute-start.3 = (bf16[16,896]{1,0:T(8,128)(2,1)S(1)}, bf16[16,896]{1,0:T(8,128)(2,1)S(1)}, u32[]{:S(2)}, u32[]{:S(2)}) collective-permute-start(bf16[16,896]{1,0:T(8,128)(2,1)S(1)} %get-tuple-element.54), channel_id=1, source_target_pairs={{0,28},{4,24},{8,20},{12,16},{16,12},{20,8},{24,4},{28,0},{1,29},{... | collective-permute-start | bytes 86024 | tf_op jit(solution)/shard_map/ppermute | solution.py:289
  11.1 0.7 %collective-permute-start.5 = (bf16[64,896]{1,0:T(8,128)(2,1)S(1)}, bf16[64,896]{1,0:T(8,128)(2,1)S(1)}, u32[]{:S(2)}, u32[]{:S(2)}) collective-permute-start(bf16[64,896]{1,0:T(8,128)(2,1)S(1)} %get-tuple-element.99), channel_id=1, source_target_pairs={{0,8},{4,12},{8,0},{12,4},{16,24},{20,28},{24,16},{28,20},{1,9},{5... | collective-permute-start | bytes 344072 | tf_op jit(solution)/shard_map/ppermute | solution.py:289
  11.7 1.0 %collective-permute-done.1 = bf16[16,896]{1,0:T(8,128)(2,1)S(1)} collective-permute-done((bf16[16,896]{1,0:T(8,128)(2,1)S(1)}, bf16[16,896]{1,0:T(8,128)(2,1)S(1)}, u32[]{:S(2)}, u32[]{:S(2)}) %collective-permute-start.1) | collective-permute-done | bytes 28704 | tf_op jit(solution)/shard_map/ppermute | solution.py:289
  12.8 0.7 %collective-permute-done.2 = bf16[16,896]{1,0:T(8,128)(2,1)S(1)} collective-permute-done((bf16[16,896]{1,0:T(8,128)(2,1)S(1)}, bf16[16,896]{1,0:T(8,128)(2,1)S(1)}, u32[]{:S(2)}, u32[]{:S(2)}) %collective-permute-start.2) | collective-permute-done | bytes 28704 | tf_op jit(solution)/shard_map/ppermute | solution.py:289
  13.5 0.6 %collective-permute-done.3 = bf16[16,896]{1,0:T(8,128)(2,1)S(1)} collective-permute-done((bf16[16,896]{1,0:T(8,128)(2,1)S(1)}, bf16[16,896]{1,0:T(8,128)(2,1)S(1)}, u32[]{:S(2)}, u32[]{:S(2)}) %collective-permute-start.3) | collective-permute-done | bytes 28704 | tf_op jit(solution)/shard_map/ppermute | solution.py:289
  14.2 2.5 %collective-permute-start.7 = (bf16[64,896]{1,0:T(8,128)(2,1)S(1)}, bf16[64,896]{1,0:T(8,128)(2,1)S(1)}, u32[]{:S(2)}, u32[]{:S(2)}) collective-permute-start(bf16[64,896]{1,0:T(8,128)(2,1)S(1)} %constant_dynamic-update-slice_fusion.mine_ref), channel_id=1, source_target_pairs={{0,3},{1,2},{2,1},{3,0},{4,7},{5,6},{6,5},{7,4},{8,11},{9,10},{10,... | collective-permute-start | bytes 344072 | tf_op jit(solution)/shard_map/ppermute | solution.py:289
  17.7 2.6 %shard_map.132 = (bf16[3584,256]{1,0:T(8,128)(2,1)S(1)}, bf16[3584,256]{1,0:T(8,128)(2,1)S(1)}, bf16[256,3584]{1,0:T(8,128)(2,1)S(1)}, f32[8,128]{1,0:T(8,128)S(1)}) custom-call(bf16[128,256]{1,0:T(8,128)(2,1)S(1)} %get-tuple-element.74.after_ref.combine_ref, bf16[3584,256]{1,0:T(8,128)(2,1)} %bitcast.13, bf16[3584,256]{1,0:T(8,128)(2,1)} %bitcast.14, ...), custom_call_target="tpu_custom_call" | custom-call | bytes 5570560 | tf_op jit(solution)/shard_map/pallas_call | solution.py:275
  20.4 1.2 %shard_map.133 = (bf16[64,896]{1,0:T(8,128)(2,1)S(1)}, bf16[64,896]{1,0:T(8,128)(2,1)S(1)}, bf16[64,896]{1,0:T(8,128)(2,1)S(1)}, bf16[64,896]{1,0:T(8,128)(2,1)S...) custom-call(bf16[16,3584]{1,0:T(8,128)(2,1)S(1)} %get-tuple-element.50.own_ref, ...), custom_call_target="tpu_custom_call" | custom-call | flops 234881024 | bytes 6082560 | tf_op jit(solution)/shard_map/pallas_call | solution.py:275
  21.6 2.0 %collective-permute-done.8.refs_1_ = bf16[64,896]{1,0:T(8,128)(2,1)S(1)} collective-permute-done((bf16[64,896]{1,0:T(8,128)(2,1)S(1)}, bf16[64,896]{1,0:T(8,128)(2,1)S(1)}, u32[]{:S(2)}, u32[]{:S(2)}) %collective-permute-start.8) | collective-permute-done | bytes 114720 | tf_op jit(solution)/shard_map/ppermute | solution.py:289
  23.6 1.0 %shard_map.134 = (bf16[64,896]{1,0:T(8,128)(2,1)S(1)}, bf16[64,896]{1,0:T(8,128)(2,1)S(1)}, bf16[64,896]{1,0:T(8,128)(2,1)S(1)}, bf16[64,896]{1,0:T(8,128)(2,1)S(1)}) custom-call(bf16[64,896]{1,0:T(8,128)(2,1)S(1)} %collective-permute-done.7.refs_0_, bf16[64,896]{1,0:T(8,128)(2,1)S(1)} %collective-permute-done.8.refs_1_, ...), custom_call_target="tpu_custom_call" | custom-call | flops 704643072 | bytes 5980160 | tf_op jit(solution)/shard_map/pallas_call | solution.py:275
  24.6 1.9 %collective-permute-start.16 = (bf16[64,896]{1,0:T(8,128)(2,1)S(1)}, bf16[64,896]{1,0:T(8,128)(2,1)S(1)}, u32[]{:S(2)}, u32[]{:S(2)}) collective-permute-start(bf16[64,896]{1,0:T(8,128)(2,1)S(1)} %get-tuple-element.85), channel_id=1, source_target_pairs={{0,3},{1,2},{2,1},{3,0},{4,7},{5,6},{6,5},{7,4},{8,11},{9,10},{10,... | collective-permute-start | bytes 344072 | tf_op jit(solution)/shard_map/ppermute | solution.py:289
  26.5 1.1 %collective-permute-start.17 = (bf16[64,896]{1,0:T(8,128)(2,1)S(1)}, bf16[64,896]{1,0:T(8,128)(2,1)S(1)}, u32[]{:S(2)}, u32[]{:S(2)}) collective-permute-start(bf16[64,896]{1,0:T(8,128)(2,1)S(1)} %get-tuple-element.86), channel_id=1, source_target_pairs={{0,2},{1,3},{2,0},{3,1},{4,6},{5,7},{6,4},{7,5},{8,10},{9,11},{10,... | collective-permute-start | bytes 344072 | tf_op jit(solution)/shard_map/ppermute | solution.py:289
  28.2 1.4 %shard_map.135 = (bf16[256,896]{1,0:T(8,128)(2,1)S(1)}, bf16[256,128]{1,0:T(8,128)(2,1)S(1)}, f32[64,1]{1,0:T(8,128)S(1)}) custom-call(s32[1,256]{1,0:T(1,128)S(1)} %bitcast.11, s32[1,256]{1,0:T(1,128)S(1)} %bitcast.12, bf16[128,256]{1,0:T(8,128)(2,1)S(1)} %get-tuple-element.74.after_ref.combine_ref, bf16[256,3584]{1,0:T(8,128)(2,1)} %hidden_hbm.3), custom_call_target="tpu_custom_call" | custom-call | flops 134217728 | bytes 1902592 | tf_op jit(solution)/shard_map/pallas_call | solution.py:275
  29.6 1.9 %collective-permute-start.10 = (bf16[64,896]{1,0:T(8,128)(2,1)S(1)}, bf16[64,896]{1,0:T(8,128)(2,1)S(1)}, u32[]{:S(2)}, u32[]{:S(2)}) collective-permute-start(bf16[64,896]{1,0:T(8,128)(2,1)S(1)} %get-tuple-element.77), channel_id=1, source_target_pairs={{0,3},{1,2},{2,1},{3,0},{4,7},{5,6},{6,5},{7,4},{8,11},{9,10},{10,... | collective-permute-start | bytes 344072 | tf_op jit(solution)/shard_map/ppermute | solution.py:289
  31.5 1.1 %collective-permute-start.11 = (bf16[64,896]{1,0:T(8,128)(2,1)S(1)}, bf16[64,896]{1,0:T(8,128)(2,1)S(1)}, u32[]{:S(2)}, u32[]{:S(2)}) collective-permute-start(bf16[64,896]{1,0:T(8,128)(2,1)S(1)} %get-tuple-element.78), channel_id=1, source_target_pairs={{0,2},{1,3},{2,0},{3,1},{4,6},{5,7},{6,4},{7,5},{8,10},{9,11},{10,... | collective-permute-start | bytes 344072 | tf_op jit(solution)/shard_map/ppermute | solution.py:289
  33.1 1.7 %collective-permute-done.17.refs_1_ = bf16[64,896]{1,0:T(8,128)(2,1)S(1)} collective-permute-done((bf16[64,896]{1,0:T(8,128)(2,1)S(1)}, bf16[64,896]{1,0:T(8,128)(2,1)S(1)}, u32[]{:S(2)}, u32[]{:S(2)}) %collective-permute-start.17) | collective-permute-done | bytes 114720 | tf_op jit(solution)/shard_map/ppermute | solution.py:289
  34.9 1.2 %collective-permute-start.20 = (bf16[32,896]{1,0:T(8,128)(2,1)S(1)}, bf16[32,896]{1,0:T(8,128)(2,1)S(1)}, u32[]{:S(2)}, u32[]{:S(2)}) collective-permute-start(bf16[32,896]{1,0:T(8,128)(2,1)S(1)} %get-tuple-element.90), channel_id=1, source_target_pairs={{0,24},{4,28},{8,16},{12,20},{16,8},{20,12},{24,0},{28,4},{1,25},{... | collective-permute-start | bytes 172040 | tf_op jit(solution)/shard_map/ppermute | solution.py:289
  36.6 1.5 %collective-permute-done.11.refs_1_ = bf16[64,896]{1,0:T(8,128)(2,1)S(1)} collective-permute-done((bf16[64,896]{1,0:T(8,128)(2,1)S(1)}, bf16[64,896]{1,0:T(8,128)(2,1)S(1)}, u32[]{:S(2)}, u32[]{:S(2)}) %collective-permute-start.11) | collective-permute-done | bytes 114720 | tf_op jit(solution)/shard_map/ppermute | solution.py:289
  38.4 1.3 %collective-permute-start.14 = (bf16[16,896]{1,0:T(8,128)(2,1)S(1)}, bf16[16,896]{1,0:T(8,128)(2,1)S(1)}, u32[]{:S(2)}, u32[]{:S(2)}) collective-permute-start(bf16[16,896]{1,0:T(8,128)(2,1)S(1)} %get-tuple-element.83), channel_id=1, source_target_pairs={{0,8},{4,12},{8,0},{12,4},{16,24},{20,28},{24,16},{28,20},{1,9},{5... | collective-permute-start | bytes 86024 | tf_op jit(solution)/shard_map/ppermute | solution.py:289
  40.2 0.8 %collective-permute-done.20.refs_5_ = bf16[32,896]{1,0:T(8,128)(2,1)S(1)} collective-permute-done((bf16[32,896]{1,0:T(8,128)(2,1)S(1)}, bf16[32,896]{1,0:T(8,128)(2,1)S(1)}, u32[]{:S(2)}, u32[]{:S(2)}) %collective-permute-start.20) | collective-permute-done | bytes 57376 | tf_op jit(solution)/shard_map/ppermute | solution.py:289
  41.0 1.3 %collective-permute-done.19.refs_4_ = bf16[32,896]{1,0:T(8,128)(2,1)S(1)} collective-permute-done((bf16[32,896]{1,0:T(8,128)(2,1)S(1)}, bf16[32,896]{1,0:T(8,128)(2,1)S(1)}, u32[]{:S(2)}, u32[]{:S(2)}) %collective-permute-start.19) | collective-permute-done | bytes 57376 | tf_op jit(solution)/shard_map/ppermute | solution.py:289
  42.9 0.7 %collective-permute-done.21.refs_6_ = bf16[32,896]{1,0:T(8,128)(2,1)S(1)} collective-permute-done((bf16[32,896]{1,0:T(8,128)(2,1)S(1)}, bf16[32,896]{1,0:T(8,128)(2,1)S(1)}, u32[]{:S(2)}, u32[]{:S(2)}) %collective-permute-start.21) | collective-permute-done | bytes 57376 | tf_op jit(solution)/shard_map/ppermute | solution.py:289
  43.6 0.8 %shard_map.138 = (bf16[64,640]{1,0:T(8,128)(2,1)S(1)}, bf16[64,640]{1,0:T(8,128)(2,1)S(1)}, bf16[64,640]{1,0:T(8,128)(2,1)S(1)}, bf16[64,640]{1,0:T(8,128)(2,1)S(1)}) custom-call(bf16[16,896]{1,0:T(8,128)(2,1)S(1)} %get-tuple-element.81.refs_0_, bf16[16,896]{1,0:T(8,128)(2,1)S(1)} %collective-permute-done.13.refs_1_, ...), custom_call_target="tpu_custom_call" | custom-call | flops 322961408 | bytes 1846784 | tf_op jit(solution)/shard_map/pallas_call | solution.py:275
  44.4 0.7 %collective-permute-start.22 = (bf16[64,640]{1,0:T(8,128)(2,1)S(1)}, bf16[64,640]{1,0:T(8,128)(2,1)S(1)}, u32[]{:S(2)}, u32[]{:S(2)}) collective-permute-start(bf16[64,640]{1,0:T(8,128)(2,1)S(1)} %get-tuple-element.93), channel_id=1, source_target_pairs={{0,3},{1,2},{2,1},{3,0},{4,7},{5,6},{6,5},{7,4},{8,11},{9,10},{10,... | collective-permute-start | bytes 245768 | tf_op jit(solution)/shard_map/ppermute | solution.py:289
  45.1 2.0 %collective-permute-start.23 = (bf16[64,640]{1,0:T(8,128)(2,1)S(1)}, bf16[64,640]{1,0:T(8,128)(2,1)S(1)}, u32[]{:S(2)}, u32[]{:S(2)}) collective-permute-start(bf16[64,640]{1,0:T(8,128)(2,1)S(1)} %get-tuple-element.94), channel_id=1, source_target_pairs={{0,2},{1,3},{2,0},{3,1},{4,6},{5,7},{6,4},{7,5},{8,10},{9,11},{10,... | collective-permute-start | bytes 245768 | tf_op jit(solution)/shard_map/ppermute | solution.py:289
  47.1 0.8 %collective-permute-start.24 = (bf16[64,640]{1,0:T(8,128)(2,1)S(1)}, bf16[64,640]{1,0:T(8,128)(2,1)S(1)}, u32[]{:S(2)}, u32[]{:S(2)}) collective-permute-start(bf16[64,640]{1,0:T(8,128)(2,1)S(1)} %get-tuple-element.95), channel_id=1, source_target_pairs={{0,1},{1,0},{2,3},{3,2},{4,5},{5,4},{6,7},{7,6},{8,9},{9,8},{10,11... | collective-permute-start | bytes 245768 | tf_op jit(solution)/shard_map/ppermute | solution.py:289
  48.1 2.5 %collective-permute-done.22.refs_0_ = bf16[64,640]{1,0:T(8,128)(2,1)S(1)} collective-permute-done((bf16[64,640]{1,0:T(8,128)(2,1)S(1)}, bf16[64,640]{1,0:T(8,128)(2,1)S(1)}, u32[]{:S(2)}, u32[]{:S(2)}) %collective-permute-start.22) | collective-permute-done | bytes 81952 | tf_op jit(solution)/shard_map/ppermute | solution.py:289
  50.7 0.7 %collective-permute-done.23.refs_1_ = bf16[64,640]{1,0:T(8,128)(2,1)S(1)} collective-permute-done((bf16[64,640]{1,0:T(8,128)(2,1)S(1)}, bf16[64,640]{1,0:T(8,128)(2,1)S(1)}, u32[]{:S(2)}, u32[]{:S(2)}) %collective-permute-start.23) | collective-permute-done | bytes 81952 | tf_op jit(solution)/shard_map/ppermute | solution.py:289
  51.6 0.9 %shard_map.139 = (bf16[64,512]{1,0:T(8,128)(2,1)}, bf16[64,64]{1,0:T(8,128)(2,1)}) custom-call(bf16[64,640]{1,0:T(8,128)(2,1)S(1)} %collective-permute-done.22.refs_0_, bf16[64,640]{1,0:T(8,128)(2,1)S(1)} %collective-permute-done.23.refs_1_, bf16[64,640]{1,0:T(8,128)(2,1)S(1)} %collective-permute-done.24.refs_2_, ...), custom_call_target="tpu_custom_call" | custom-call | bytes 346112 | tf_op jit(solution)/shard_map/pallas_call | solution.py:275
  (49 shorter events, 5.4 us)
Async XLA Ops:
  3.0 8.1 %collective-permute-start = (bf16[16,896]{1,0:T(8,128)(2,1)S(1)}, bf16[16,896]{1,0:T(8,128)(2,1)S(1)}, u32[]{:S(2)}, u32[]{:S(2)}) collective-permute-start(bf16[16,896]{1,0:T(8,128)(2,1)S(1)} %get-tuple-element.51), channel_id=1, source_target_pairs={{0,16},{4,20},{8,24},{12,28},{16,0},{20,4},{24,8},{28,12},{1,17},{... | collective-permute-start | bytes 86024 | tf_op jit(solution)/shard_map/ppermute | solution.py:289
  7.1 5.7 %collective-permute-start.1 = (bf16[16,896]{1,0:T(8,128)(2,1)S(1)}, bf16[16,896]{1,0:T(8,128)(2,1)S(1)}, u32[]{:S(2)}, u32[]{:S(2)}) collective-permute-start(bf16[16,896]{1,0:T(8,128)(2,1)S(1)} %get-tuple-element.52), channel_id=1, source_target_pairs={{0,24},{4,28},{8,16},{12,20},{16,8},{20,12},{24,0},{28,4},{1,25},{... | collective-permute-start | bytes 86024 | tf_op jit(solution)/shard_map/ppermute | solution.py:289
  8.4 5.1 %collective-permute-start.2 = (bf16[16,896]{1,0:T(8,128)(2,1)S(1)}, bf16[16,896]{1,0:T(8,128)(2,1)S(1)}, u32[]{:S(2)}, u32[]{:S(2)}) collective-permute-start(bf16[16,896]{1,0:T(8,128)(2,1)S(1)} %get-tuple-element.53), channel_id=1, source_target_pairs={{0,20},{4,16},{8,28},{12,24},{16,4},{20,0},{24,12},{28,8},{1,21},{... | collective-permute-start | bytes 86024 | tf_op jit(solution)/shard_map/ppermute | solution.py:289
  9.0 5.1 %collective-permute-start.3 = (bf16[16,896]{1,0:T(8,128)(2,1)S(1)}, bf16[16,896]{1,0:T(8,128)(2,1)S(1)}, u32[]{:S(2)}, u32[]{:S(2)}) collective-permute-start(bf16[16,896]{1,0:T(8,128)(2,1)S(1)} %get-tuple-element.54), channel_id=1, source_target_pairs={{0,28},{4,24},{8,20},{12,16},{16,12},{20,8},{24,4},{28,0},{1,29},{... | collective-permute-start | bytes 86024 | tf_op jit(solution)/shard_map/ppermute | solution.py:289
  10.7 3.4 %collective-permute-start.4 = (bf16[64,896]{1,0:T(8,128)(2,1)S(1)}, bf16[64,896]{1,0:T(8,128)(2,1)S(1)}, u32[]{:S(2)}, u32[]{:S(2)}) collective-permute-start(bf16[64,896]{1,0:T(8,128)(2,1)S(1)} %get-tuple-element.55), channel_id=1, source_target_pairs={{0,4},{4,0},{8,12},{12,8},{16,20},{20,16},{24,28},{28,24},{1,5},{5... | collective-permute-start | bytes 344072 | tf_op jit(solution)/shard_map/ppermute | solution.py:289
  11.1 9.3 %collective-permute-start.5 = (bf16[64,896]{1,0:T(8,128)(2,1)S(1)}, bf16[64,896]{1,0:T(8,128)(2,1)S(1)}, u32[]{:S(2)}, u32[]{:S(2)}) collective-permute-start(bf16[64,896]{1,0:T(8,128)(2,1)S(1)} %get-tuple-element.99), channel_id=1, source_target_pairs={{0,8},{4,12},{8,0},{12,4},{16,24},{20,28},{24,16},{28,20},{1,9},{5... | collective-permute-start | bytes 344072 | tf_op jit(solution)/shard_map/ppermute | solution.py:289
  12.7 7.6 %collective-permute-start.6 = (bf16[64,896]{1,0:T(8,128)(2,1)S(1)}, bf16[64,896]{1,0:T(8,128)(2,1)S(1)}, u32[]{:S(2)}, u32[]{:S(2)}) collective-permute-start(bf16[64,896]{1,0:T(8,128)(2,1)S(1)} %get-tuple-element.98), channel_id=1, source_target_pairs={{0,12},{4,8},{8,4},{12,0},{16,28},{20,24},{24,20},{28,16},{1,13},{... | collective-permute-start | bytes 344072 | tf_op jit(solution)/shard_map/ppermute | solution.py:289
  14.2 7.4 %collective-permute-start.7 = (bf16[64,896]{1,0:T(8,128)(2,1)S(1)}, bf16[64,896]{1,0:T(8,128)(2,1)S(1)}, u32[]{:S(2)}, u32[]{:S(2)}) collective-permute-start(bf16[64,896]{1,0:T(8,128)(2,1)S(1)} %constant_dynamic-update-slice_fusion.mine_ref), channel_id=1, source_target_pairs={{0,3},{1,2},{2,1},{3,0},{4,7},{5,6},{6,5},{7,4},{8,11},{9,10},{10,... | collective-permute-start | bytes 344072 | tf_op jit(solution)/shard_map/ppermute | solution.py:289
  16.7 6.9 %collective-permute-start.8 = (bf16[64,896]{1,0:T(8,128)(2,1)S(1)}, bf16[64,896]{1,0:T(8,128)(2,1)S(1)}, u32[]{:S(2)}, u32[]{:S(2)}) collective-permute-start(bf16[64,896]{1,0:T(8,128)(2,1)S(1)} %constant_dynamic-update-slice_fusion.mine_ref), channel_id=1, source_target_pairs={{0,2},{1,3},{2,0},{3,1},{4,6},{5,7},{6,4},{7,5},{8,10},{9,11},{10,... | collective-permute-start | bytes 344072 | tf_op jit(solution)/shard_map/ppermute | solution.py:289
  17.2 6.4 %collective-permute-start.9 = (bf16[64,896]{1,0:T(8,128)(2,1)S(1)}, bf16[64,896]{1,0:T(8,128)(2,1)S(1)}, u32[]{:S(2)}, u32[]{:S(2)}) collective-permute-start(bf16[64,896]{1,0:T(8,128)(2,1)S(1)} %constant_dynamic-update-slice_fusion.mine_ref), channel_id=1, source_target_pairs={{0,1},{1,0},{2,3},{3,2},{4,5},{5,4},{6,7},{7,6},{8,9},{9,8},{10,11... | collective-permute-start | bytes 344072 | tf_op jit(solution)/shard_map/ppermute | solution.py:289
  23.6 4.6 %copy-start.2 = (s32[256]{0:T(256)S(1)}, s32[256]{0:T(256)}, u32[]{:S(2)}) copy-start(s32[256]{0:T(256)} %param.23) | copy-start | bytes 3076
  23.6 4.6 %copy-start.3 = (s32[256]{0:T(256)S(1)}, s32[256]{0:T(256)}, u32[]{:S(2)}) copy-start(s32[256]{0:T(256)} %param.22) | copy-start | bytes 3076
  24.6 17.8 %copy-start.4 = (f32[896]{0:T(1024)S(1)}, f32[896]{0:T(1024)}, u32[]{:S(2)}) copy-start(f32[896]{0:T(1024)} %param.19) | copy-start | bytes 10756
  24.6 19.0 %copy-start = (bf16[896,576]{0,1:T(8,128)(2,1)S(1)}, bf16[896,576]{0,1:T(8,128)(2,1)}, u32[]{:S(2)}) copy-start(bf16[896,576]{0,1:T(8,128)(2,1)} %param.20) | copy-start | bytes 3096580
  24.6 8.0 %collective-permute-start.16 = (bf16[64,896]{1,0:T(8,128)(2,1)S(1)}, bf16[64,896]{1,0:T(8,128)(2,1)S(1)}, u32[]{:S(2)}, u32[]{:S(2)}) collective-permute-start(bf16[64,896]{1,0:T(8,128)(2,1)S(1)} %get-tuple-element.85), channel_id=1, source_target_pairs={{0,3},{1,2},{2,1},{3,0},{4,7},{5,6},{6,5},{7,4},{8,11},{9,10},{10,... | collective-permute-start | bytes 344072 | tf_op jit(solution)/shard_map/ppermute | solution.py:289
  26.5 8.3 %collective-permute-start.17 = (bf16[64,896]{1,0:T(8,128)(2,1)S(1)}, bf16[64,896]{1,0:T(8,128)(2,1)S(1)}, u32[]{:S(2)}, u32[]{:S(2)}) collective-permute-start(bf16[64,896]{1,0:T(8,128)(2,1)S(1)} %get-tuple-element.86), channel_id=1, source_target_pairs={{0,2},{1,3},{2,0},{3,1},{4,6},{5,7},{6,4},{7,5},{8,10},{9,11},{10,... | collective-permute-start | bytes 344072 | tf_op jit(solution)/shard_map/ppermute | solution.py:289
  27.7 7.2 %collective-permute-start.18 = (bf16[64,896]{1,0:T(8,128)(2,1)S(1)}, bf16[64,896]{1,0:T(8,128)(2,1)S(1)}, u32[]{:S(2)}, u32[]{:S(2)}) collective-permute-start(bf16[64,896]{1,0:T(8,128)(2,1)S(1)} %get-tuple-element.87), channel_id=1, source_target_pairs={{0,1},{1,0},{2,3},{3,2},{4,5},{5,4},{6,7},{7,6},{8,9},{9,8},{10,11... | collective-permute-start | bytes 344072 | tf_op jit(solution)/shard_map/ppermute | solution.py:289
  29.6 22.0 %copy-start.1 = (f32[512]{0:T(512)S(1)}, f32[512]{0:T(512)}, u32[]{:S(2)}) copy-start(f32[512]{0:T(512)} %param.21) | copy-start | bytes 6148
  29.6 7.1 %collective-permute-start.10 = (bf16[64,896]{1,0:T(8,128)(2,1)S(1)}, bf16[64,896]{1,0:T(8,128)(2,1)S(1)}, u32[]{:S(2)}, u32[]{:S(2)}) collective-permute-start(bf16[64,896]{1,0:T(8,128)(2,1)S(1)} %get-tuple-element.77), channel_id=1, source_target_pairs={{0,3},{1,2},{2,1},{3,0},{4,7},{5,6},{6,5},{7,4},{8,11},{9,10},{10,... | collective-permute-start | bytes 344072 | tf_op jit(solution)/shard_map/ppermute | solution.py:289
  31.5 6.6 %collective-permute-start.11 = (bf16[64,896]{1,0:T(8,128)(2,1)S(1)}, bf16[64,896]{1,0:T(8,128)(2,1)S(1)}, u32[]{:S(2)}, u32[]{:S(2)}) collective-permute-start(bf16[64,896]{1,0:T(8,128)(2,1)S(1)} %get-tuple-element.78), channel_id=1, source_target_pairs={{0,2},{1,3},{2,0},{3,1},{4,6},{5,7},{6,4},{7,5},{8,10},{9,11},{10,... | collective-permute-start | bytes 344072 | tf_op jit(solution)/shard_map/ppermute | solution.py:289
  32.6 5.6 %collective-permute-start.12 = (bf16[64,896]{1,0:T(8,128)(2,1)S(1)}, bf16[64,896]{1,0:T(8,128)(2,1)S(1)}, u32[]{:S(2)}, u32[]{:S(2)}) collective-permute-start(bf16[64,896]{1,0:T(8,128)(2,1)S(1)} %get-tuple-element.79), channel_id=1, source_target_pairs={{0,1},{1,0},{2,3},{3,2},{4,5},{5,4},{6,7},{7,6},{8,9},{9,8},{10,11... | collective-permute-start | bytes 344072 | tf_op jit(solution)/shard_map/ppermute | solution.py:289
  34.9 6.1 %collective-permute-start.20 = (bf16[32,896]{1,0:T(8,128)(2,1)S(1)}, bf16[32,896]{1,0:T(8,128)(2,1)S(1)}, u32[]{:S(2)}, u32[]{:S(2)}) collective-permute-start(bf16[32,896]{1,0:T(8,128)(2,1)S(1)} %get-tuple-element.90), channel_id=1, source_target_pairs={{0,24},{4,28},{8,16},{12,20},{16,8},{20,12},{24,0},{28,4},{1,25},{... | collective-permute-start | bytes 172040 | tf_op jit(solution)/shard_map/ppermute | solution.py:289
  36.1 6.2 %collective-permute-start.19 = (bf16[32,896]{1,0:T(8,128)(2,1)S(1)}, bf16[32,896]{1,0:T(8,128)(2,1)S(1)}, u32[]{:S(2)}, u32[]{:S(2)}) collective-permute-start(bf16[32,896]{1,0:T(8,128)(2,1)S(1)} %get-tuple-element.89), channel_id=1, source_target_pairs={{0,16},{4,20},{8,24},{12,28},{16,0},{20,4},{24,8},{28,12},{1,17},{... | collective-permute-start | bytes 172040 | tf_op jit(solution)/shard_map/ppermute | solution.py:289
  38.3 4.3 %collective-permute-start.13 = (bf16[16,896]{1,0:T(8,128)(2,1)S(1)}, bf16[16,896]{1,0:T(8,128)(2,1)S(1)}, u32[]{:S(2)}, u32[]{:S(2)}) collective-permute-start(bf16[16,896]{1,0:T(8,128)(2,1)S(1)} %get-tuple-element.82), channel_id=1, source_target_pairs={{0,4},{4,0},{8,12},{12,8},{16,20},{20,16},{24,28},{28,24},{1,5},{5... | collective-permute-start | bytes 86024 | tf_op jit(solution)/shard_map/ppermute | solution.py:289
  38.4 4.2 %collective-permute-start.14 = (bf16[16,896]{1,0:T(8,128)(2,1)S(1)}, bf16[16,896]{1,0:T(8,128)(2,1)S(1)}, u32[]{:S(2)}, u32[]{:S(2)}) collective-permute-start(bf16[16,896]{1,0:T(8,128)(2,1)S(1)} %get-tuple-element.83), channel_id=1, source_target_pairs={{0,8},{4,12},{8,0},{12,4},{16,24},{20,28},{24,16},{28,20},{1,9},{5... | collective-permute-start | bytes 86024 | tf_op jit(solution)/shard_map/ppermute | solution.py:289
  39.6 3.3 %collective-permute-start.15 = (bf16[16,896]{1,0:T(8,128)(2,1)S(1)}, bf16[16,896]{1,0:T(8,128)(2,1)S(1)}, u32[]{:S(2)}, u32[]{:S(2)}) collective-permute-start(bf16[16,896]{1,0:T(8,128)(2,1)S(1)} %get-tuple-element.84), channel_id=1, source_target_pairs={{0,12},{4,8},{8,4},{12,0},{16,28},{20,24},{24,20},{28,16},{1,13},{... | collective-permute-start | bytes 86024 | tf_op jit(solution)/shard_map/ppermute | solution.py:289
  42.3 1.3 %collective-permute-start.21 = (bf16[32,896]{1,0:T(8,128)(2,1)S(1)}, bf16[32,896]{1,0:T(8,128)(2,1)S(1)}, u32[]{:S(2)}, u32[]{:S(2)}) collective-permute-start(bf16[32,896]{1,0:T(8,128)(2,1)S(1)} %pad_maximum_fusion), channel_id=1, source_target_pairs={{0,4},{4,0},{8,12},{12,8},{16,20},{20,16},{24,28},{28,24},{1,5},{5... | collective-permute-start | bytes 172040 | tf_op jit(solution)/shard_map/ppermute | solution.py:289
  44.4 6.3 %collective-permute-start.22 = (bf16[64,640]{1,0:T(8,128)(2,1)S(1)}, bf16[64,640]{1,0:T(8,128)(2,1)S(1)}, u32[]{:S(2)}, u32[]{:S(2)}) collective-permute-start(bf16[64,640]{1,0:T(8,128)(2,1)S(1)} %get-tuple-element.93), channel_id=1, source_target_pairs={{0,3},{1,2},{2,1},{3,0},{4,7},{5,6},{6,5},{7,4},{8,11},{9,10},{10,... | collective-permute-start | bytes 245768 | tf_op jit(solution)/shard_map/ppermute | solution.py:289
  45.1 6.3 %collective-permute-start.23 = (bf16[64,640]{1,0:T(8,128)(2,1)S(1)}, bf16[64,640]{1,0:T(8,128)(2,1)S(1)}, u32[]{:S(2)}, u32[]{:S(2)}) collective-permute-start(bf16[64,640]{1,0:T(8,128)(2,1)S(1)} %get-tuple-element.94), channel_id=1, source_target_pairs={{0,2},{1,3},{2,0},{3,1},{4,6},{5,7},{6,4},{7,5},{8,10},{9,11},{10,... | collective-permute-start | bytes 245768 | tf_op jit(solution)/shard_map/ppermute | solution.py:289
  47.1 4.4 %collective-permute-start.24 = (bf16[64,640]{1,0:T(8,128)(2,1)S(1)}, bf16[64,640]{1,0:T(8,128)(2,1)S(1)}, u32[]{:S(2)}, u32[]{:S(2)}) collective-permute-start(bf16[64,640]{1,0:T(8,128)(2,1)S(1)} %get-tuple-element.95), channel_id=1, source_target_pairs={{0,1},{1,0},{2,3},{3,2},{4,5},{5,4},{6,7},{7,6},{8,9},{9,8},{10,11... | collective-permute-start | bytes 245768 | tf_op jit(solution)/shard_map/ppermute | solution.py:289

commit v3 on v2

--- a/solution.py
+++ b/solution.py
@@ -26,9 +26,8 @@
 
 
 def dispatch_kernel(n_ep, n_tp, routes_hbm, logits_hbm, hidden_hbm, gain_hbm, *refs):
-    own_ref, core_ref, near_ref = refs[:3]
-    outs, combine_ref = refs[3 : n_ep - 1], refs[n_ep - 1]
-    routes_ref, logits_ref, hidden_ref, gain_ref, pick_ref, head_ref, sems = refs[n_ep:]
+    outs = refs[: n_ep - 4]
+    pick_ref, combine_ref, hidden_ref, gain_ref, routes_ref, logits_ref, sems = refs[n_ep - 4 :]
     me = lax.axis_index("ep")
     part = lax.axis_index("tp")
     tokens, width = hidden_ref.shape
@@ -72,9 +71,8 @@
         rows = slice(d * CAP, (d + 1) * CAP)
         pick_ref[rows, :] = jnp.where(match, 1.0, 0.0).astype(BF16)
         combine_ref[rows, :] = jnp.where(match, gain_of[d : d + 1, :], 0.0).astype(BF16)
-    pick = pick_ref[...]
-    head = 4 * CAP
-    square = jnp.zeros((n_ep * CAP, 1), F32)
+    pick = pick_ref[4 * CAP :, :]
+    square = jnp.zeros((pick.shape[0], 1), F32)
     middle = len(large) // 2
     for i, c in enumerate(starts):
         if i == 0 or i == middle:
@@ -82,16 +80,19 @@
                 copy.wait()
         got = jnp.dot(pick, hidden_ref[:, c : c + step], preferred_element_type=F32)
         square = square + jnp.sum(got * got, axis=1, keepdims=True)
-        head_ref[:, c : c + step] = got[:head]
     small[2].wait()
     scale = lax.rsqrt(square / width + EPS)
-    got = jnp.dot(pick[head:], columns_of(hidden_ref, part, n_tp, share), preferred_element_type=F32)
-    rest = (got * scale[head:] * columns_of(gain_ref, part, n_tp, share)).astype(BF16)
-    at = 0
-    for out in outs:
-        out[...] = rest[at : at + out.shape[0]]
-        at += out.shape[0]
-    whole = (head_ref[...] * scale[:head] * gain_ref[...]).astype(BF16)
+    got = jnp.dot(pick, columns_of(hidden_ref, part, n_tp, share), preferred_element_type=F32)
+    rows = (got * scale * columns_of(gain_ref, part, n_tp, share)).astype(BF16)
+    for i, out in enumerate(outs):
+        out[...] = rows[i * CAP : (i + 1) * CAP]
+
+
+def near_kernel(n_tp, pick_ref, hidden_ref, gain_ref, own_ref, core_ref, near_ref):
+    share = hidden_ref.shape[1] // n_tp
+    got = jnp.dot(pick_ref[: 4 * CAP, :], hidden_ref[...], preferred_element_type=F32)
+    scale = lax.rsqrt(jnp.mean(got * got, axis=1, keepdims=True) + EPS)
+    whole = (got * scale * gain_ref[...]).astype(BF16)
     own_ref[...] = whole[:CAP]
     for q in range(n_tp):
         columns = slice(q * share, (q + 1) * share)
@@ -179,19 +180,13 @@
     owners_ref,
     positions_ref,
     combine_ref,
-    hidden_hbm,
+    hidden_ref,
     rows_ref,
     mix_ref,
     at_ref,
-    hidden_ref,
-    sem,
 ):
     part = lax.axis_index("tp")
-    tokens, share = hidden_ref.shape
-    if hidden_hbm.shape[1] != share:
-        hidden_hbm = hidden_hbm.at[:, pl.ds(pl.multiple_of(part * share, 128), share)]
-    copy = pltpu.make_async_copy(hidden_hbm, hidden_ref, sem)
-    copy.start()
+    tokens, width = hidden_ref.shape
     source_rows = tokens // n_tp
     owners = owners_ref[...] ^ part
     owner = lax.broadcasted_iota(jnp.int32, (n_tp, tokens), 0)
@@ -211,8 +206,8 @@
     ).astype(BF16)
     place = jnp.where(held[:seats], positions_ref[...].astype(F32), 0.0)
     at_ref[...] = jnp.sum(place, axis=1, keepdims=True)
-    copy.wait()
-    rows_ref[...] = jnp.dot(pick, hidden_ref[...], preferred_element_type=F32).astype(BF16)
+    hidden = columns_of(hidden_ref, part, n_tp, width // n_tp)
+    rows_ref[...] = jnp.dot(pick, hidden, preferred_element_type=F32).astype(BF16)
 
 
 def cache_kernel(n_z, n_tp, cache_width, *refs):
@@ -224,7 +219,8 @@
     for d in range(n_z - 2):
         at = (2 * d + 4) * CAP
         back_ref[at : at + CAP, :] = far[d][:CAP, :]
-        back_ref[at + CAP : at + 2 * CAP, :] = core_ref[d * CAP : (d + 1) * CAP, :]
+        last = (n_z - 3 - d) * CAP
+        back_ref[at + CAP : at + 2 * CAP, :] = core_ref[last : last + CAP, :]
     mixed = jnp.dot(mix_ref[...], back_ref[...], preferred_element_type=F32)
     state = rows_ref[...].astype(F32) + mixed
     square = jnp.sum(state * state, axis=1, keepdims=True)
@@ -327,24 +323,26 @@
     struct = jax.ShapeDtypeStruct
     chunks = width // 512 if width % 512 == 0 else 1
 
-    own, to_core, to_near, *outgoing, combine = call(
+    *outgoing, pick, combine, hidden, gain = call(
         functools.partial(dispatch_kernel, n_ep, n_tp),
-        [struct((CAP, width), BF16), struct((n_tp * CAP, share), BF16)]
-        + [struct((2 * n_tp * CAP, share), BF16)]
-        + [struct((CAP, share), BF16)] * (n_ep - 4)
-        + [struct((slots, tokens), BF16)],
+        [struct((CAP, share), BF16)] * (n_ep - 4)
+        + [struct((slots, tokens), BF16)] * 2
+        + [struct(hidden.shape, BF16), struct((1, width), F32)],
         (routes.T, route_logits.T, hidden, moe_gain),
         [
             pltpu.VMEM(routes.T.shape, jnp.int32),
             pltpu.VMEM(routes.T.shape, F32),
-            pltpu.VMEM(hidden.shape, BF16),
-            pltpu.VMEM((1, width), F32),
-            pltpu.VMEM((slots, tokens), BF16),
-            pltpu.VMEM((4 * CAP, width), F32),
             pltpu.SemaphoreType.DMA((3 + chunks,)),
         ],
-        flops=4 * slots * tokens * width,
+        flops=2 * slots * tokens * width,
         hbm=(0, 1, 2, 3),
+    )
+    own, to_core, to_near = call(
+        functools.partial(near_kernel, n_tp),
+        [struct((CAP, width), BF16), struct((n_tp * CAP, share), BF16)]
+        + [struct((2 * n_tp * CAP, share), BF16)],
+        (pick, hidden, gain),
+        flops=8 * CAP * tokens * width,
     )
     order = [*range(4, n_ep, 2), *range(5, n_ep, 2)]
     arrived = [swap(outgoing[d - 4], "ep", d) for d in order]
@@ -378,9 +376,6 @@
     )
     terms = list(terms)
     combine, terms[0] = lax.optimization_barrier((combine, terms[0]))
-    share_of = hidden
-    if share % 128:
-        share_of = lax.dynamic_slice_in_dim(hidden, lax.axis_index("tp") * share, share, 1)
     rows, mix, at = call(
         functools.partial(seats_kernel, n_tp, seat_cap),
         [
@@ -388,10 +383,8 @@
             struct((n_tp * seats, slots), BF16),
             struct((seats, 1), F32),
         ],
-        (owners[None, :], positions[None, :], combine, share_of),
-        [pltpu.VMEM((tokens, share), BF16), pltpu.SemaphoreType.DMA(())],
+        (owners[None, :], positions[None, :], combine, hidden),
         flops=2 * n_tp * seats * tokens * (share + slots),
-        hbm=(3,),
     )
     near_pieces, rows, mix = lax.optimization_barrier((near_pieces, rows, mix))
     freqs = ROPE_BASE ** (-jnp.arange(half, dtype=F32) / half)
@@ -410,7 +403,7 @@
         functools.partial(sum_kernel, n_tp), [struct((CAP, share), BF16)] * 4, near_terms
     )
     near_back = [near_done[0]] + [swap(near_done[d], "ep", d) for d in (1, 2, 3)]
-    crossed = swap(jnp.concatenate([piece[CAP:] for piece in far_back], axis=0), "ep", 1)
+    crossed = swap(jnp.concatenate([piece[CAP:] for piece in far_back[::-1]], axis=0), "ep", 1)
     partial = call(
         functools.partial(cache_kernel, n_z, n_tp, cache_width),
         [struct((seats, wide), BF16)] * n_tp,

time: 52.7 us -> 51.8 us (0.983)
  waiting for transfers between devices: 14.7 us -> 11.2 us
  starting transfers between devices: 26.2 us -> 29.3 us
    ppermute x25, waiting for transfers between devices: 14.7 us -> 11.2 us  [swap(): lax.ppermute(value, axis, [(i, i ^ d) for i in range(lax.axis_size(axis))])]
    ppermute x25, starting transfers between devices: 26.2 us -> 29.3 us  [swap(): lax.ppermute(value, axis, [(i, i ^ d) for i in range(lax.axis_size(axis))])]
    pallas_call x9 -> x10, Pallas kernels: 10.3 us -> 9.88 us  [call(): pl.pallas_call(kernel, out_shape=out_shape, in_specs=[pl.BlockSpec(memory...]
  transfers between devices with their start and end apart: 25 -> 25, of which waited for: 15 -> 14; matrix products, arithmetic and copies ran while one was open for 1% -> 1% of each run, Pallas kernels for 10% -> 10%
where the time goes in v3:
time: 51.8 us; the launch traced here: 51.6 us
  starting transfers between devices  29.3 us (57%)
  waiting for transfers between devices  11.2 us (22%)
  Pallas kernels  9.88 us (19%)
  between operations  0.84 us (2%)
    ppermute x25, starting transfers between devices, swap(): lax.ppermute(value, axis, [(i, i ^ d) for i in range(lax.axis_size(axis))])  29.3 us
    ppermute x25, waiting for transfers between devices, swap(): lax.ppermute(value, axis, [(i, i ^ d) for i in range(lax.axis_size(axis))])  11.2 us
    pallas_call x10, Pallas kernels, call(): pl.pallas_call(kernel, out_shape=out_shape, in_specs=[pl.BlockSpec(memory...  9.88 us
  transfers between devices with their start and end apart: 25, of which 14 were waited for; matrix products, arithmetic and copies ran while one was open for 1% of the time, Pallas kernels for 10%

profile of v3, /device:TPU:0, one launch (start us, length us, event | category | flops | bytes accessed | tf_op | source)
XLA Modules:
  0.0 51.6 jit_solution(9165643353901712433)
XLA Ops:
  0.6 2.2 %shard_map.131 = (bf16[16,896]{1,0:T(8,128)(2,1)S(1)}, bf16[16,896]{1,0:T(8,128)(2,1)S(1)}, bf16[16,896]{1,0:T(8,128)(2,1)S(1)}, bf16[16,896]{1,0:T(8,128)(2,1)S...) custom-call(s32[8,256]{1,0:T(8,128)} %bitcast.16, ...), custom_call_target="tpu_custom_call" | custom-call | flops 234881024 | bytes 1865728 | tf_op jit(solution)/shard_map/pallas_call | solution.py:271
  2.8 4.1 %collective-permute-start = (bf16[16,896]{1,0:T(8,128)(2,1)S(1)}, bf16[16,896]{1,0:T(8,128)(2,1)S(1)}, u32[]{:S(2)}, u32[]{:S(2)}) collective-permute-start(bf16[16,896]{1,0:T(8,128)(2,1)S(1)} %get-tuple-element.57), channel_id=1, source_target_pairs={{0,16},{4,20},{8,24},{12,28},{16,0},{20,4},{24,8},{28,12},{1,17},{... | collective-permute-start | bytes 86024 | tf_op jit(solution)/shard_map/ppermute | solution.py:285
  6.9 1.3 %collective-permute-start.1 = (bf16[16,896]{1,0:T(8,128)(2,1)S(1)}, bf16[16,896]{1,0:T(8,128)(2,1)S(1)}, u32[]{:S(2)}, u32[]{:S(2)}) collective-permute-start(bf16[16,896]{1,0:T(8,128)(2,1)S(1)} %get-tuple-element.58), channel_id=1, source_target_pairs={{0,24},{4,28},{8,16},{12,20},{16,8},{20,12},{24,0},{28,4},{1,25},{... | collective-permute-start | bytes 86024 | tf_op jit(solution)/shard_map/ppermute | solution.py:285
  8.3 0.6 %collective-permute-start.2 = (bf16[16,896]{1,0:T(8,128)(2,1)S(1)}, bf16[16,896]{1,0:T(8,128)(2,1)S(1)}, u32[]{:S(2)}, u32[]{:S(2)}) collective-permute-start(bf16[16,896]{1,0:T(8,128)(2,1)S(1)} %get-tuple-element.59), channel_id=1, source_target_pairs={{0,20},{4,16},{8,28},{12,24},{16,4},{20,0},{24,12},{28,8},{1,21},{... | collective-permute-start | bytes 86024 | tf_op jit(solution)/shard_map/ppermute | solution.py:285
  8.9 1.7 %collective-permute-start.3 = (bf16[16,896]{1,0:T(8,128)(2,1)S(1)}, bf16[16,896]{1,0:T(8,128)(2,1)S(1)}, u32[]{:S(2)}, u32[]{:S(2)}) collective-permute-start(bf16[16,896]{1,0:T(8,128)(2,1)S(1)} %get-tuple-element.60), channel_id=1, source_target_pairs={{0,28},{4,24},{8,20},{12,16},{16,12},{20,8},{24,4},{28,0},{1,29},{... | collective-permute-start | bytes 86024 | tf_op jit(solution)/shard_map/ppermute | solution.py:285
  10.6 0.6 %shard_map.132 = (bf16[16,3584]{1,0:T(8,128)(2,1)S(1)}, bf16[64,896]{1,0:T(8,128)(2,1)S(1)}, bf16[128,896]{1,0:T(8,128)(2,1)S(1)}) custom-call(bf16[128,256]{1,0:T(8,128)(2,1)S(1)} %get-tuple-element.53.pick_ref, bf16[256,3584]{1,0:T(8,128)(2,1)S(1)} %get-tuple-element.54.hidden_ref, f32[1,3584]{1,0:T(1,128)S(1)} %get-tuple-element.55.gain_ref), custom_call_target="tpu_custom_call" | custom-call | flops 117440512 | bytes 1914880 | tf_op jit(solution)/shard_map/pallas_call | solution.py:271
  11.6 0.7 %collective-permute-start.5 = (bf16[64,896]{1,0:T(8,128)(2,1)S(1)}, bf16[64,896]{1,0:T(8,128)(2,1)S(1)}, u32[]{:S(2)}, u32[]{:S(2)}) collective-permute-start(bf16[64,896]{1,0:T(8,128)(2,1)S(1)} %get-tuple-element.105), channel_id=1, source_target_pairs={{0,8},{4,12},{8,0},{12,4},{16,24},{20,28},{24,16},{28,20},{1,9},{5... | collective-permute-start | bytes 344072 | tf_op jit(solution)/shard_map/ppermute | solution.py:285
  12.6 0.6 %collective-permute-start.6 = (bf16[64,896]{1,0:T(8,128)(2,1)S(1)}, bf16[64,896]{1,0:T(8,128)(2,1)S(1)}, u32[]{:S(2)}, u32[]{:S(2)}) collective-permute-start(bf16[64,896]{1,0:T(8,128)(2,1)S(1)} %get-tuple-element.104), channel_id=1, source_target_pairs={{0,12},{4,8},{8,4},{12,0},{16,28},{20,24},{24,20},{28,16},{1,13},{... | collective-permute-start | bytes 344072 | tf_op jit(solution)/shard_map/ppermute | solution.py:285
  13.4 0.6 %collective-permute-done.3 = bf16[16,896]{1,0:T(8,128)(2,1)S(1)} collective-permute-done((bf16[16,896]{1,0:T(8,128)(2,1)S(1)}, bf16[16,896]{1,0:T(8,128)(2,1)S(1)}, u32[]{:S(2)}, u32[]{:S(2)}) %collective-permute-start.3) | collective-permute-done | bytes 28704 | tf_op jit(solution)/shard_map/ppermute | solution.py:285
  14.0 2.5 %collective-permute-start.7 = (bf16[64,896]{1,0:T(8,128)(2,1)S(1)}, bf16[64,896]{1,0:T(8,128)(2,1)S(1)}, u32[]{:S(2)}, u32[]{:S(2)}) collective-permute-start(bf16[64,896]{1,0:T(8,128)(2,1)S(1)} %constant_dynamic-update-slice_fusion.mine_ref), channel_id=1, source_target_pairs={{0,3},{1,2},{2,1},{3,0},{4,7},{5,6},{6,5},{7,4},{8,11},{9,10},{10,... | collective-permute-start | bytes 344072 | tf_op jit(solution)/shard_map/ppermute | solution.py:285
  17.6 2.6 %shard_map.133 = (bf16[3584,256]{1,0:T(8,128)(2,1)S(1)}, bf16[3584,256]{1,0:T(8,128)(2,1)S(1)}, bf16[256,3584]{1,0:T(8,128)(2,1)S(1)}, f32[8,128]{1,0:T(8,128)S(1)}) custom-call(bf16[128,256]{1,0:T(8,128)(2,1)S(1)} %get-tuple-element.80.after_ref.combine_ref, bf16[3584,256]{1,0:T(8,128)(2,1)} %bitcast.13, bf16[3584,256]{1,0:T(8,128)(2,1)} %bitcast.14, ...), custom_call_target="tpu_custom_call" | custom-call | bytes 5570560 | tf_op jit(solution)/shard_map/pallas_call | solution.py:271
  20.2 1.2 %shard_map.134 = (bf16[64,896]{1,0:T(8,128)(2,1)S(1)}, bf16[64,896]{1,0:T(8,128)(2,1)S(1)}, bf16[64,896]{1,0:T(8,128)(2,1)S(1)}, bf16[64,896]{1,0:T(8,128)(2,1)S...) custom-call(bf16[16,3584]{1,0:T(8,128)(2,1)S(1)} %get-tuple-element.56.own_ref, ...), custom_call_target="tpu_custom_call" | custom-call | flops 234881024 | bytes 6082560 | tf_op jit(solution)/shard_map/pallas_call | solution.py:271
  21.4 2.0 %collective-permute-done.8.refs_1_ = bf16[64,896]{1,0:T(8,128)(2,1)S(1)} collective-permute-done((bf16[64,896]{1,0:T(8,128)(2,1)S(1)}, bf16[64,896]{1,0:T(8,128)(2,1)S(1)}, u32[]{:S(2)}, u32[]{:S(2)}) %collective-permute-start.8) | collective-permute-done | bytes 114720 | tf_op jit(solution)/shard_map/ppermute | solution.py:285
  23.5 1.0 %shard_map.135 = (bf16[64,896]{1,0:T(8,128)(2,1)S(1)}, bf16[64,896]{1,0:T(8,128)(2,1)S(1)}, bf16[64,896]{1,0:T(8,128)(2,1)S(1)}, bf16[64,896]{1,0:T(8,128)(2,1)S(1)}) custom-call(bf16[64,896]{1,0:T(8,128)(2,1)S(1)} %collective-permute-done.7.refs_0_, bf16[64,896]{1,0:T(8,128)(2,1)S(1)} %collective-permute-done.8.refs_1_, ...), custom_call_target="tpu_custom_call" | custom-call | flops 704643072 | bytes 5980160 | tf_op jit(solution)/shard_map/pallas_call | solution.py:271
  24.5 2.0 %collective-permute-start.16 = (bf16[64,896]{1,0:T(8,128)(2,1)S(1)}, bf16[64,896]{1,0:T(8,128)(2,1)S(1)}, u32[]{:S(2)}, u32[]{:S(2)}) collective-permute-start(bf16[64,896]{1,0:T(8,128)(2,1)S(1)} %get-tuple-element.91), channel_id=1, source_target_pairs={{0,3},{1,2},{2,1},{3,0},{4,7},{5,6},{6,5},{7,4},{8,11},{9,10},{10,... | collective-permute-start | bytes 344072 | tf_op jit(solution)/shard_map/ppermute | solution.py:285
  26.5 1.0 %collective-permute-start.17 = (bf16[64,896]{1,0:T(8,128)(2,1)S(1)}, bf16[64,896]{1,0:T(8,128)(2,1)S(1)}, u32[]{:S(2)}, u32[]{:S(2)}) collective-permute-start(bf16[64,896]{1,0:T(8,128)(2,1)S(1)} %get-tuple-element.92), channel_id=1, source_target_pairs={{0,2},{1,3},{2,0},{3,1},{4,6},{5,7},{6,4},{7,5},{8,10},{9,11},{10,... | collective-permute-start | bytes 344072 | tf_op jit(solution)/shard_map/ppermute | solution.py:285
  28.5 2.0 %collective-permute-start.10 = (bf16[64,896]{1,0:T(8,128)(2,1)S(1)}, bf16[64,896]{1,0:T(8,128)(2,1)S(1)}, u32[]{:S(2)}, u32[]{:S(2)}) collective-permute-start(bf16[64,896]{1,0:T(8,128)(2,1)S(1)} %get-tuple-element.83), channel_id=1, source_target_pairs={{0,3},{1,2},{2,1},{3,0},{4,7},{5,6},{6,5},{7,4},{8,11},{9,10},{10,... | collective-permute-start | bytes 344072 | tf_op jit(solution)/shard_map/ppermute | solution.py:285
  30.6 1.0 %collective-permute-start.11 = (bf16[64,896]{1,0:T(8,128)(2,1)S(1)}, bf16[64,896]{1,0:T(8,128)(2,1)S(1)}, u32[]{:S(2)}, u32[]{:S(2)}) collective-permute-start(bf16[64,896]{1,0:T(8,128)(2,1)S(1)} %get-tuple-element.84), channel_id=1, source_target_pairs={{0,2},{1,3},{2,0},{3,1},{4,6},{5,7},{6,4},{7,5},{8,10},{9,11},{10,... | collective-permute-start | bytes 344072 | tf_op jit(solution)/shard_map/ppermute | solution.py:285
  31.5 1.4 %collective-permute-start.12 = (bf16[64,896]{1,0:T(8,128)(2,1)S(1)}, bf16[64,896]{1,0:T(8,128)(2,1)S(1)}, u32[]{:S(2)}, u32[]{:S(2)}) collective-permute-start(bf16[64,896]{1,0:T(8,128)(2,1)S(1)} %get-tuple-element.85), channel_id=1, source_target_pairs={{0,1},{1,0},{2,3},{3,2},{4,5},{5,4},{6,7},{7,6},{8,9},{9,8},{10,11... | collective-permute-start | bytes 344072 | tf_op jit(solution)/shard_map/ppermute | solution.py:285
  32.9 1.2 %collective-permute-done.17.refs_1_ = bf16[64,896]{1,0:T(8,128)(2,1)S(1)} collective-permute-done((bf16[64,896]{1,0:T(8,128)(2,1)S(1)}, bf16[64,896]{1,0:T(8,128)(2,1)S(1)}, u32[]{:S(2)}, u32[]{:S(2)}) %collective-permute-start.17) | collective-permute-done | bytes 114720 | tf_op jit(solution)/shard_map/ppermute | solution.py:285
  34.2 1.5 %collective-permute-start.19 = (bf16[32,896]{1,0:T(8,128)(2,1)S(1)}, bf16[32,896]{1,0:T(8,128)(2,1)S(1)}, u32[]{:S(2)}, u32[]{:S(2)}) collective-permute-start(bf16[32,896]{1,0:T(8,128)(2,1)S(1)} %get-tuple-element.95), channel_id=1, source_target_pairs={{0,16},{4,20},{8,24},{12,28},{16,0},{20,4},{24,8},{28,12},{1,17},{... | collective-permute-start | bytes 172040 | tf_op jit(solution)/shard_map/ppermute | solution.py:285
  35.7 1.4 %collective-permute-start.20 = (bf16[32,896]{1,0:T(8,128)(2,1)S(1)}, bf16[32,896]{1,0:T(8,128)(2,1)S(1)}, u32[]{:S(2)}, u32[]{:S(2)}) collective-permute-start(bf16[32,896]{1,0:T(8,128)(2,1)S(1)} %get-tuple-element.96), channel_id=1, source_target_pairs={{0,24},{4,28},{8,16},{12,20},{16,8},{20,12},{24,0},{28,4},{1,25},{... | collective-permute-start | bytes 172040 | tf_op jit(solution)/shard_map/ppermute | solution.py:285
  37.1 0.9 %collective-permute-done.11.refs_1_ = bf16[64,896]{1,0:T(8,128)(2,1)S(1)} collective-permute-done((bf16[64,896]{1,0:T(8,128)(2,1)S(1)}, bf16[64,896]{1,0:T(8,128)(2,1)S(1)}, u32[]{:S(2)}, u32[]{:S(2)}) %collective-permute-start.11) | collective-permute-done | bytes 114720 | tf_op jit(solution)/shard_map/ppermute | solution.py:285
  38.2 1.8 %collective-permute-start.15 = (bf16[16,896]{1,0:T(8,128)(2,1)S(1)}, bf16[16,896]{1,0:T(8,128)(2,1)S(1)}, u32[]{:S(2)}, u32[]{:S(2)}) collective-permute-start(bf16[16,896]{1,0:T(8,128)(2,1)S(1)} %get-tuple-element.90), channel_id=1, source_target_pairs={{0,12},{4,8},{8,4},{12,0},{16,28},{20,24},{24,20},{28,16},{1,13},{... | collective-permute-start | bytes 86024 | tf_op jit(solution)/shard_map/ppermute | solution.py:285
  40.0 0.6 %collective-permute-done.19.refs_4_ = bf16[32,896]{1,0:T(8,128)(2,1)S(1)} collective-permute-done((bf16[32,896]{1,0:T(8,128)(2,1)S(1)}, bf16[32,896]{1,0:T(8,128)(2,1)S(1)}, u32[]{:S(2)}, u32[]{:S(2)}) %collective-permute-start.19) | collective-permute-done | bytes 57376 | tf_op jit(solution)/shard_map/ppermute | solution.py:285
  40.6 1.3 %collective-permute-done.20.refs_5_ = bf16[32,896]{1,0:T(8,128)(2,1)S(1)} collective-permute-done((bf16[32,896]{1,0:T(8,128)(2,1)S(1)}, bf16[32,896]{1,0:T(8,128)(2,1)S(1)}, u32[]{:S(2)}, u32[]{:S(2)}) %collective-permute-start.20) | collective-permute-done | bytes 57376 | tf_op jit(solution)/shard_map/ppermute | solution.py:285
  43.3 0.8 %shard_map.139 = (bf16[64,640]{1,0:T(8,128)(2,1)S(1)}, bf16[64,640]{1,0:T(8,128)(2,1)S(1)}, bf16[64,640]{1,0:T(8,128)(2,1)S(1)}, bf16[64,640]{1,0:T(8,128)(2,1)S(1)}) custom-call(bf16[16,896]{1,0:T(8,128)(2,1)S(1)} %get-tuple-element.87.refs_0_, bf16[16,896]{1,0:T(8,128)(2,1)S(1)} %collective-permute-done.13.refs_1_, ...), custom_call_target="tpu_custom_call" | custom-call | flops 322961408 | bytes 1846784 | tf_op jit(solution)/shard_map/pallas_call | solution.py:271
  44.1 0.7 %collective-permute-start.22 = (bf16[64,640]{1,0:T(8,128)(2,1)S(1)}, bf16[64,640]{1,0:T(8,128)(2,1)S(1)}, u32[]{:S(2)}, u32[]{:S(2)}) collective-permute-start(bf16[64,640]{1,0:T(8,128)(2,1)S(1)} %get-tuple-element.99), channel_id=1, source_target_pairs={{0,3},{1,2},{2,1},{3,0},{4,7},{5,6},{6,5},{7,4},{8,11},{9,10},{10,... | collective-permute-start | bytes 245768 | tf_op jit(solution)/shard_map/ppermute | solution.py:285
  44.7 1.5 %collective-permute-start.23 = (bf16[64,640]{1,0:T(8,128)(2,1)S(1)}, bf16[64,640]{1,0:T(8,128)(2,1)S(1)}, u32[]{:S(2)}, u32[]{:S(2)}) collective-permute-start(bf16[64,640]{1,0:T(8,128)(2,1)S(1)} %get-tuple-element.100), channel_id=1, source_target_pairs={{0,2},{1,3},{2,0},{3,1},{4,6},{5,7},{6,4},{7,5},{8,10},{9,11},{10,... | collective-permute-start | bytes 245768 | tf_op jit(solution)/shard_map/ppermute | solution.py:285
  46.2 1.4 %collective-permute-start.24 = (bf16[64,640]{1,0:T(8,128)(2,1)S(1)}, bf16[64,640]{1,0:T(8,128)(2,1)S(1)}, u32[]{:S(2)}, u32[]{:S(2)}) collective-permute-start(bf16[64,640]{1,0:T(8,128)(2,1)S(1)} %get-tuple-element.101), channel_id=1, source_target_pairs={{0,1},{1,0},{2,3},{3,2},{4,5},{5,4},{6,7},{7,6},{8,9},{9,8},{10,11... | collective-permute-start | bytes 245768 | tf_op jit(solution)/shard_map/ppermute | solution.py:285
  47.8 2.5 %collective-permute-done.22.refs_0_ = bf16[64,640]{1,0:T(8,128)(2,1)S(1)} collective-permute-done((bf16[64,640]{1,0:T(8,128)(2,1)S(1)}, bf16[64,640]{1,0:T(8,128)(2,1)S(1)}, u32[]{:S(2)}, u32[]{:S(2)}) %collective-permute-start.22) | collective-permute-done | bytes 81952 | tf_op jit(solution)/shard_map/ppermute | solution.py:285
  50.7 0.9 %shard_map.140 = (bf16[64,512]{1,0:T(8,128)(2,1)}, bf16[64,64]{1,0:T(8,128)(2,1)}) custom-call(bf16[64,640]{1,0:T(8,128)(2,1)S(1)} %collective-permute-done.22.refs_0_, bf16[64,640]{1,0:T(8,128)(2,1)S(1)} %collective-permute-done.23.refs_1_, bf16[64,640]{1,0:T(8,128)(2,1)S(1)} %collective-permute-done.24.refs_2_, ...), custom_call_target="tpu_custom_call" | custom-call | bytes 346112 | tf_op jit(solution)/shard_map/pallas_call | solution.py:271
  (50 shorter events, 5.1 us)
Async XLA Ops:
  2.8 8.7 %collective-permute-start = (bf16[16,896]{1,0:T(8,128)(2,1)S(1)}, bf16[16,896]{1,0:T(8,128)(2,1)S(1)}, u32[]{:S(2)}, u32[]{:S(2)}) collective-permute-start(bf16[16,896]{1,0:T(8,128)(2,1)S(1)} %get-tuple-element.57), channel_id=1, source_target_pairs={{0,16},{4,20},{8,24},{12,28},{16,0},{20,4},{24,8},{28,12},{1,17},{... | collective-permute-start | bytes 86024 | tf_op jit(solution)/shard_map/ppermute | solution.py:285
  6.9 5.7 %collective-permute-start.1 = (bf16[16,896]{1,0:T(8,128)(2,1)S(1)}, bf16[16,896]{1,0:T(8,128)(2,1)S(1)}, u32[]{:S(2)}, u32[]{:S(2)}) collective-permute-start(bf16[16,896]{1,0:T(8,128)(2,1)S(1)} %get-tuple-element.58), channel_id=1, source_target_pairs={{0,24},{4,28},{8,16},{12,20},{16,8},{20,12},{24,0},{28,4},{1,25},{... | collective-permute-start | bytes 86024 | tf_op jit(solution)/shard_map/ppermute | solution.py:285
  8.3 5.1 %collective-permute-start.2 = (bf16[16,896]{1,0:T(8,128)(2,1)S(1)}, bf16[16,896]{1,0:T(8,128)(2,1)S(1)}, u32[]{:S(2)}, u32[]{:S(2)}) collective-permute-start(bf16[16,896]{1,0:T(8,128)(2,1)S(1)} %get-tuple-element.59), channel_id=1, source_target_pairs={{0,20},{4,16},{8,28},{12,24},{16,4},{20,0},{24,12},{28,8},{1,21},{... | collective-permute-start | bytes 86024 | tf_op jit(solution)/shard_map/ppermute | solution.py:285
  8.9 5.1 %collective-permute-start.3 = (bf16[16,896]{1,0:T(8,128)(2,1)S(1)}, bf16[16,896]{1,0:T(8,128)(2,1)S(1)}, u32[]{:S(2)}, u32[]{:S(2)}) collective-permute-start(bf16[16,896]{1,0:T(8,128)(2,1)S(1)} %get-tuple-element.60), channel_id=1, source_target_pairs={{0,28},{4,24},{8,20},{12,16},{16,12},{20,8},{24,4},{28,0},{1,29},{... | collective-permute-start | bytes 86024 | tf_op jit(solution)/shard_map/ppermute | solution.py:285
  11.2 2.8 %collective-permute-start.4 = (bf16[64,896]{1,0:T(8,128)(2,1)S(1)}, bf16[64,896]{1,0:T(8,128)(2,1)S(1)}, u32[]{:S(2)}, u32[]{:S(2)}) collective-permute-start(bf16[64,896]{1,0:T(8,128)(2,1)S(1)} %get-tuple-element.61), channel_id=1, source_target_pairs={{0,4},{4,0},{8,12},{12,8},{16,20},{20,16},{24,28},{28,24},{1,5},{5... | collective-permute-start | bytes 344072 | tf_op jit(solution)/shard_map/ppermute | solution.py:285
  11.6 8.6 %collective-permute-start.5 = (bf16[64,896]{1,0:T(8,128)(2,1)S(1)}, bf16[64,896]{1,0:T(8,128)(2,1)S(1)}, u32[]{:S(2)}, u32[]{:S(2)}) collective-permute-start(bf16[64,896]{1,0:T(8,128)(2,1)S(1)} %get-tuple-element.105), channel_id=1, source_target_pairs={{0,8},{4,12},{8,0},{12,4},{16,24},{20,28},{24,16},{28,20},{1,9},{5... | collective-permute-start | bytes 344072 | tf_op jit(solution)/shard_map/ppermute | solution.py:285
  12.6 7.6 %collective-permute-start.6 = (bf16[64,896]{1,0:T(8,128)(2,1)S(1)}, bf16[64,896]{1,0:T(8,128)(2,1)S(1)}, u32[]{:S(2)}, u32[]{:S(2)}) collective-permute-start(bf16[64,896]{1,0:T(8,128)(2,1)S(1)} %get-tuple-element.104), channel_id=1, source_target_pairs={{0,12},{4,8},{8,4},{12,0},{16,28},{20,24},{24,20},{28,16},{1,13},{... | collective-permute-start | bytes 344072 | tf_op jit(solution)/shard_map/ppermute | solution.py:285
  14.0 7.4 %collective-permute-start.7 = (bf16[64,896]{1,0:T(8,128)(2,1)S(1)}, bf16[64,896]{1,0:T(8,128)(2,1)S(1)}, u32[]{:S(2)}, u32[]{:S(2)}) collective-permute-start(bf16[64,896]{1,0:T(8,128)(2,1)S(1)} %constant_dynamic-update-slice_fusion.mine_ref), channel_id=1, source_target_pairs={{0,3},{1,2},{2,1},{3,0},{4,7},{5,6},{6,5},{7,4},{8,11},{9,10},{10,... | collective-permute-start | bytes 344072 | tf_op jit(solution)/shard_map/ppermute | solution.py:285
  16.5 6.9 %collective-permute-start.8 = (bf16[64,896]{1,0:T(8,128)(2,1)S(1)}, bf16[64,896]{1,0:T(8,128)(2,1)S(1)}, u32[]{:S(2)}, u32[]{:S(2)}) collective-permute-start(bf16[64,896]{1,0:T(8,128)(2,1)S(1)} %constant_dynamic-update-slice_fusion.mine_ref), channel_id=1, source_target_pairs={{0,2},{1,3},{2,0},{3,1},{4,6},{5,7},{6,4},{7,5},{8,10},{9,11},{10,... | collective-permute-start | bytes 344072 | tf_op jit(solution)/shard_map/ppermute | solution.py:285
  17.0 6.4 %collective-permute-start.9 = (bf16[64,896]{1,0:T(8,128)(2,1)S(1)}, bf16[64,896]{1,0:T(8,128)(2,1)S(1)}, u32[]{:S(2)}, u32[]{:S(2)}) collective-permute-start(bf16[64,896]{1,0:T(8,128)(2,1)S(1)} %constant_dynamic-update-slice_fusion.mine_ref), channel_id=1, source_target_pairs={{0,1},{1,0},{2,3},{3,2},{4,5},{5,4},{6,7},{7,6},{8,9},{9,8},{10,11... | collective-permute-start | bytes 344072 | tf_op jit(solution)/shard_map/ppermute | solution.py:285
  23.5 4.6 %copy-start.2 = (s32[256]{0:T(256)S(1)}, s32[256]{0:T(256)}, u32[]{:S(2)}) copy-start(s32[256]{0:T(256)} %param.23) | copy-start | bytes 3076
  23.5 4.6 %copy-start.3 = (s32[256]{0:T(256)S(1)}, s32[256]{0:T(256)}, u32[]{:S(2)}) copy-start(s32[256]{0:T(256)} %param.22) | copy-start | bytes 3076
  24.4 17.7 %copy-start.4 = (f32[896]{0:T(1024)S(1)}, f32[896]{0:T(1024)}, u32[]{:S(2)}) copy-start(f32[896]{0:T(1024)} %param.19) | copy-start | bytes 10756
  24.5 18.9 %copy-start = (bf16[896,576]{0,1:T(8,128)(2,1)S(1)}, bf16[896,576]{0,1:T(8,128)(2,1)}, u32[]{:S(2)}) copy-start(bf16[896,576]{0,1:T(8,128)(2,1)} %param.20) | copy-start | bytes 3096580
  24.5 7.1 %collective-permute-start.16 = (bf16[64,896]{1,0:T(8,128)(2,1)S(1)}, bf16[64,896]{1,0:T(8,128)(2,1)S(1)}, u32[]{:S(2)}, u32[]{:S(2)}) collective-permute-start(bf16[64,896]{1,0:T(8,128)(2,1)S(1)} %get-tuple-element.91), channel_id=1, source_target_pairs={{0,3},{1,2},{2,1},{3,0},{4,7},{5,6},{6,5},{7,4},{8,11},{9,10},{10,... | collective-permute-start | bytes 344072 | tf_op jit(solution)/shard_map/ppermute | solution.py:285
  26.5 7.6 %collective-permute-start.17 = (bf16[64,896]{1,0:T(8,128)(2,1)S(1)}, bf16[64,896]{1,0:T(8,128)(2,1)S(1)}, u32[]{:S(2)}, u32[]{:S(2)}) collective-permute-start(bf16[64,896]{1,0:T(8,128)(2,1)S(1)} %get-tuple-element.92), channel_id=1, source_target_pairs={{0,2},{1,3},{2,0},{3,1},{4,6},{5,7},{6,4},{7,5},{8,10},{9,11},{10,... | collective-permute-start | bytes 344072 | tf_op jit(solution)/shard_map/ppermute | solution.py:285
  27.5 6.7 %collective-permute-start.18 = (bf16[64,896]{1,0:T(8,128)(2,1)S(1)}, bf16[64,896]{1,0:T(8,128)(2,1)S(1)}, u32[]{:S(2)}, u32[]{:S(2)}) collective-permute-start(bf16[64,896]{1,0:T(8,128)(2,1)S(1)} %get-tuple-element.93), channel_id=1, source_target_pairs={{0,1},{1,0},{2,3},{3,2},{4,5},{5,4},{6,7},{7,6},{8,9},{9,8},{10,11... | collective-permute-start | bytes 344072 | tf_op jit(solution)/shard_map/ppermute | solution.py:285
  28.5 22.2 %copy-start.1 = (f32[512]{0:T(512)S(1)}, f32[512]{0:T(512)}, u32[]{:S(2)}) copy-start(f32[512]{0:T(512)} %param.21) | copy-start | bytes 6148
  28.5 8.6 %collective-permute-start.10 = (bf16[64,896]{1,0:T(8,128)(2,1)S(1)}, bf16[64,896]{1,0:T(8,128)(2,1)S(1)}, u32[]{:S(2)}, u32[]{:S(2)}) collective-permute-start(bf16[64,896]{1,0:T(8,128)(2,1)S(1)} %get-tuple-element.83), channel_id=1, source_target_pairs={{0,3},{1,2},{2,1},{3,0},{4,7},{5,6},{6,5},{7,4},{8,11},{9,10},{10,... | collective-permute-start | bytes 344072 | tf_op jit(solution)/shard_map/ppermute | solution.py:285
  30.6 7.4 %collective-permute-start.11 = (bf16[64,896]{1,0:T(8,128)(2,1)S(1)}, bf16[64,896]{1,0:T(8,128)(2,1)S(1)}, u32[]{:S(2)}, u32[]{:S(2)}) collective-permute-start(bf16[64,896]{1,0:T(8,128)(2,1)S(1)} %get-tuple-element.84), channel_id=1, source_target_pairs={{0,2},{1,3},{2,0},{3,1},{4,6},{5,7},{6,4},{7,5},{8,10},{9,11},{10,... | collective-permute-start | bytes 344072 | tf_op jit(solution)/shard_map/ppermute | solution.py:285
  31.5 6.5 %collective-permute-start.12 = (bf16[64,896]{1,0:T(8,128)(2,1)S(1)}, bf16[64,896]{1,0:T(8,128)(2,1)S(1)}, u32[]{:S(2)}, u32[]{:S(2)}) collective-permute-start(bf16[64,896]{1,0:T(8,128)(2,1)S(1)} %get-tuple-element.85), channel_id=1, source_target_pairs={{0,1},{1,0},{2,3},{3,2},{4,5},{5,4},{6,7},{7,6},{8,9},{9,8},{10,11... | collective-permute-start | bytes 344072 | tf_op jit(solution)/shard_map/ppermute | solution.py:285
  34.2 6.4 %collective-permute-start.19 = (bf16[32,896]{1,0:T(8,128)(2,1)S(1)}, bf16[32,896]{1,0:T(8,128)(2,1)S(1)}, u32[]{:S(2)}, u32[]{:S(2)}) collective-permute-start(bf16[32,896]{1,0:T(8,128)(2,1)S(1)} %get-tuple-element.95), channel_id=1, source_target_pairs={{0,16},{4,20},{8,24},{12,28},{16,0},{20,4},{24,8},{28,12},{1,17},{... | collective-permute-start | bytes 172040 | tf_op jit(solution)/shard_map/ppermute | solution.py:285
  35.7 6.3 %collective-permute-start.20 = (bf16[32,896]{1,0:T(8,128)(2,1)S(1)}, bf16[32,896]{1,0:T(8,128)(2,1)S(1)}, u32[]{:S(2)}, u32[]{:S(2)}) collective-permute-start(bf16[32,896]{1,0:T(8,128)(2,1)S(1)} %get-tuple-element.96), channel_id=1, source_target_pairs={{0,24},{4,28},{8,16},{12,20},{16,8},{20,12},{24,0},{28,4},{1,25},{... | collective-permute-start | bytes 172040 | tf_op jit(solution)/shard_map/ppermute | solution.py:285
  38.1 4.1 %collective-permute-start.13 = (bf16[16,896]{1,0:T(8,128)(2,1)S(1)}, bf16[16,896]{1,0:T(8,128)(2,1)S(1)}, u32[]{:S(2)}, u32[]{:S(2)}) collective-permute-start(bf16[16,896]{1,0:T(8,128)(2,1)S(1)} %get-tuple-element.88), channel_id=1, source_target_pairs={{0,4},{4,0},{8,12},{12,8},{16,20},{20,16},{24,28},{28,24},{1,5},{5... | collective-permute-start | bytes 86024 | tf_op jit(solution)/shard_map/ppermute | solution.py:285
  38.2 4.3 %collective-permute-start.14 = (bf16[16,896]{1,0:T(8,128)(2,1)S(1)}, bf16[16,896]{1,0:T(8,128)(2,1)S(1)}, u32[]{:S(2)}, u32[]{:S(2)}) collective-permute-start(bf16[16,896]{1,0:T(8,128)(2,1)S(1)} %get-tuple-element.89), channel_id=1, source_target_pairs={{0,8},{4,12},{8,0},{12,4},{16,24},{20,28},{24,16},{28,20},{1,9},{5... | collective-permute-start | bytes 86024 | tf_op jit(solution)/shard_map/ppermute | solution.py:285
  38.2 4.6 %collective-permute-start.15 = (bf16[16,896]{1,0:T(8,128)(2,1)S(1)}, bf16[16,896]{1,0:T(8,128)(2,1)S(1)}, u32[]{:S(2)}, u32[]{:S(2)}) collective-permute-start(bf16[16,896]{1,0:T(8,128)(2,1)S(1)} %get-tuple-element.90), channel_id=1, source_target_pairs={{0,12},{4,8},{8,4},{12,0},{16,28},{20,24},{24,20},{28,16},{1,13},{... | collective-permute-start | bytes 86024 | tf_op jit(solution)/shard_map/ppermute | solution.py:285
  42.0 1.3 %collective-permute-start.21 = (bf16[32,896]{1,0:T(8,128)(2,1)S(1)}, bf16[32,896]{1,0:T(8,128)(2,1)S(1)}, u32[]{:S(2)}, u32[]{:S(2)}) collective-permute-start(bf16[32,896]{1,0:T(8,128)(2,1)S(1)} %pad_maximum_fusion), channel_id=1, source_target_pairs={{0,4},{4,0},{8,12},{12,8},{16,20},{20,16},{24,28},{28,24},{1,5},{5... | collective-permute-start | bytes 172040 | tf_op jit(solution)/shard_map/ppermute | solution.py:285
  44.1 6.3 %collective-permute-start.22 = (bf16[64,640]{1,0:T(8,128)(2,1)S(1)}, bf16[64,640]{1,0:T(8,128)(2,1)S(1)}, u32[]{:S(2)}, u32[]{:S(2)}) collective-permute-start(bf16[64,640]{1,0:T(8,128)(2,1)S(1)} %get-tuple-element.99), channel_id=1, source_target_pairs={{0,3},{1,2},{2,1},{3,0},{4,7},{5,6},{6,5},{7,4},{8,11},{9,10},{10,... | collective-permute-start | bytes 245768 | tf_op jit(solution)/shard_map/ppermute | solution.py:285
  44.7 6.0 %collective-permute-start.23 = (bf16[64,640]{1,0:T(8,128)(2,1)S(1)}, bf16[64,640]{1,0:T(8,128)(2,1)S(1)}, u32[]{:S(2)}, u32[]{:S(2)}) collective-permute-start(bf16[64,640]{1,0:T(8,128)(2,1)S(1)} %get-tuple-element.100), channel_id=1, source_target_pairs={{0,2},{1,3},{2,0},{3,1},{4,6},{5,7},{6,4},{7,5},{8,10},{9,11},{10,... | collective-permute-start | bytes 245768 | tf_op jit(solution)/shard_map/ppermute | solution.py:285
  46.2 4.5 %collective-permute-start.24 = (bf16[64,640]{1,0:T(8,128)(2,1)S(1)}, bf16[64,640]{1,0:T(8,128)(2,1)S(1)}, u32[]{:S(2)}, u32[]{:S(2)}) collective-permute-start(bf16[64,640]{1,0:T(8,128)(2,1)S(1)} %get-tuple-element.101), channel_id=1, source_target_pairs={{0,1},{1,0},{2,3},{3,2},{4,5},{5,4},{6,7},{7,6},{8,9},{9,8},{10,11... | collective-permute-start | bytes 245768 | tf_op jit(solution)/shard_map/ppermute | solution.py:285

commit v4 on v3

--- a/solution.py
+++ b/solution.py
@@ -25,9 +25,10 @@
     return out
 
 
-def dispatch_kernel(n_ep, n_tp, routes_hbm, logits_hbm, hidden_hbm, gain_hbm, *refs):
-    outs = refs[: n_ep - 4]
-    pick_ref, combine_ref, hidden_ref, gain_ref, routes_ref, logits_ref, sems = refs[n_ep - 4 :]
+def dispatch_kernel(n_ep, n_tp, order, routes_hbm, logits_hbm, hidden_hbm, gain_hbm, *refs):
+    outs = refs[: len(order)]
+    pick_ref, combine_ref, hidden_ref, gain_ref = refs[len(order) : len(order) + 4]
+    whole, (routes_ref, logits_ref, sems) = refs[len(order) + 4 : -3], refs[-3:]
     me = lax.axis_index("ep")
     part = lax.axis_index("tp")
     tokens, width = hidden_ref.shape
@@ -84,21 +85,22 @@
     scale = lax.rsqrt(square / width + EPS)
     got = jnp.dot(pick, columns_of(hidden_ref, part, n_tp, share), preferred_element_type=F32)
     rows = (got * scale * columns_of(gain_ref, part, n_tp, share)).astype(BF16)
-    for i, out in enumerate(outs):
-        out[...] = rows[i * CAP : (i + 1) * CAP]
-
-
-def near_kernel(n_tp, pick_ref, hidden_ref, gain_ref, own_ref, core_ref, near_ref):
+    for d, out in zip(order, outs):
+        out[...] = rows[(d - 4) * CAP : (d - 3) * CAP]
+    whole_rows(n_tp, pick_ref, hidden_ref, gain_ref, *whole)
+
+
+def whole_rows(n_tp, pick_ref, hidden_ref, gain_ref, own_ref, core_ref, *outs):
     share = hidden_ref.shape[1] // n_tp
-    got = jnp.dot(pick_ref[: 4 * CAP, :], hidden_ref[...], preferred_element_type=F32)
+    pick = jnp.concatenate([pick_ref[: 4 * CAP, :], pick_ref[5 * CAP : 6 * CAP, :]], axis=0)
+    got = jnp.dot(pick, hidden_ref[...], preferred_element_type=F32)
     scale = lax.rsqrt(jnp.mean(got * got, axis=1, keepdims=True) + EPS)
     whole = (got * scale * gain_ref[...]).astype(BF16)
     own_ref[...] = whole[:CAP]
-    for q in range(n_tp):
-        columns = slice(q * share, (q + 1) * share)
-        core_ref[q * CAP : (q + 1) * CAP, :] = whole[CAP : 2 * CAP, columns]
-        near_ref[q * CAP : (q + 1) * CAP, :] = whole[2 * CAP : 3 * CAP, columns]
-        near_ref[(n_tp + q) * CAP : (n_tp + q + 1) * CAP, :] = whole[3 * CAP :, columns]
+    for i, out in enumerate((core_ref, *outs)):
+        for q in range(n_tp):
+            columns = slice(q * share, (q + 1) * share)
+            out[q * CAP : (q + 1) * CAP, :] = whole[(i + 1) * CAP : (i + 2) * CAP, columns]
 
 
 def load_kernel(after_ref, *refs):
@@ -114,13 +116,13 @@
         copy.wait()
 
 
-def first_kernel(n_tp, own_ref, core_ref, near_ref, cross_ref, mine_ref, *refs):
+def first_kernel(n_tp, own_ref, core_ref, near_ref, wide_ref, cross_ref, mine_ref, *refs):
     gate_ref, up_ref, down_ref, _ = refs[:4]
-    outs, (gate_sum_ref, up_sum_ref, head_ref) = refs[4 : n_tp + 4], refs[n_tp + 4 :]
+    outs, (wide_inner_ref, gate_sum_ref, up_sum_ref, head_ref) = refs[4 : n_tp + 4], refs[n_tp + 4 :]
     part = lax.axis_index("tp")
     share = mine_ref.shape[1]
     head_ref[:CAP, :] = own_ref[...]
-    for i, ref in enumerate((core_ref, near_ref, cross_ref)):
+    for i, ref in enumerate((core_ref, near_ref, cross_ref, wide_ref)):
         for q in range(n_tp):
             rows = slice((i + 1) * CAP, (i + 2) * CAP)
             head_ref[rows, q * share : (q + 1) * share] = ref[q * CAP : (q + 1) * CAP, :]
@@ -131,15 +133,17 @@
     for weight_ref, sum_ref in zip((gate_ref, up_ref), (gate_sum_ref, up_sum_ref)):
         sum_ref[...] = jnp.dot(mine_ref[...], weight_ref[depth, :], preferred_element_type=F32)
     inner = (gate / (1.0 + jnp.exp(-gate)) * upper).astype(BF16)
+    wide_inner_ref[...] = inner[4 * CAP :]
+    inner = inner[: 4 * CAP]
     for d in range(n_tp):
         down = columns_of(down_ref, part ^ d, n_tp, share)
         outs[d][...] = jnp.dot(inner, down, preferred_element_type=F32).astype(BF16)
 
 
-def expert_kernel(n_tp, *refs):
+def expert_kernel(n_tp, order, *refs):
     rows = refs[: n_tp - 1]
-    gate_ref, up_ref, down_ref, gate_sum_ref, up_sum_ref = refs[n_tp - 1 : n_tp + 4]
-    outs = refs[n_tp + 4 :]
+    gate_ref, up_ref, down_ref, wide_ref, gate_sum_ref, up_sum_ref = refs[n_tp - 1 : n_tp + 5]
+    outs = refs[n_tp + 5 :]
     part = lax.axis_index("tp")
     share = rows[0].shape[1]
     gate = gate_sum_ref[...]
@@ -150,13 +154,9 @@
         gate = gate + jnp.dot(value, gate_ref[depth, :], preferred_element_type=F32)
         upper = upper + jnp.dot(value, up_ref[depth, :], preferred_element_type=F32)
     far = (gate / (1.0 + jnp.exp(-gate)) * upper).astype(BF16)
-    count = far.shape[0]
-    groups = [
-        far[start : start + CAP]
-        for at in range(0, count // 2, CAP)
-        for start in (at, count // 2 + at)
-    ]
-    inner = jnp.concatenate(groups, axis=0)
+    groups = {d: far[i * CAP : (i + 1) * CAP] for i, d in enumerate(order)}
+    groups[5] = wide_ref[...]
+    inner = jnp.concatenate([groups[d] for d in sorted(groups)], axis=0)
     for d in range(n_tp):
         down = columns_of(down_ref, part ^ d, n_tp, share)
         outs[d][...] = jnp.dot(inner, down, preferred_element_type=F32).astype(BF16)
@@ -323,31 +323,26 @@
     struct = jax.ShapeDtypeStruct
     chunks = width // 512 if width % 512 == 0 else 1
 
-    *outgoing, pick, combine, hidden, gain = call(
-        functools.partial(dispatch_kernel, n_ep, n_tp),
-        [struct((CAP, share), BF16)] * (n_ep - 4)
+    order = [*range(4, n_ep, 2), *range(7, n_ep, 2)]
+    *outgoing, _, combine, hidden, _, own, to_core, to_near, to_cross, to_wide = call(
+        functools.partial(dispatch_kernel, n_ep, n_tp, order),
+        [struct((CAP, share), BF16)] * len(order)
         + [struct((slots, tokens), BF16)] * 2
-        + [struct(hidden.shape, BF16), struct((1, width), F32)],
+        + [struct(hidden.shape, BF16), struct((1, width), F32), struct((CAP, width), BF16)]
+        + [struct((n_tp * CAP, share), BF16)] * 4,
         (routes.T, route_logits.T, hidden, moe_gain),
         [
             pltpu.VMEM(routes.T.shape, jnp.int32),
             pltpu.VMEM(routes.T.shape, F32),
             pltpu.SemaphoreType.DMA((3 + chunks,)),
         ],
-        flops=2 * slots * tokens * width,
+        flops=4 * slots * tokens * width,
         hbm=(0, 1, 2, 3),
     )
-    own, to_core, to_near = call(
-        functools.partial(near_kernel, n_tp),
-        [struct((CAP, width), BF16), struct((n_tp * CAP, share), BF16)]
-        + [struct((2 * n_tp * CAP, share), BF16)],
-        (pick, hidden, gain),
-        flops=8 * CAP * tokens * width,
-    )
-    order = [*range(4, n_ep, 2), *range(5, n_ep, 2)]
-    arrived = [swap(outgoing[d - 4], "ep", d) for d in order]
-    near = swap(to_near[: n_tp * CAP], "ep", 2)
-    near_crossed = swap(to_near[n_tp * CAP :], "ep", 3)
+    arrived = [swap(piece, "ep", d) for d, piece in zip(order, outgoing)]
+    wide_rows = swap(to_wide, "ep", 5)
+    near = swap(to_near, "ep", 2)
+    near_crossed = swap(to_cross, "ep", 3)
     from_core = swap(to_core, "ep", 1)
     gate_w, up_w, down_w = gate_weight[0], up_weight[0], down_weight[0]
     *loaded, mark = call(
@@ -361,17 +356,19 @@
     mine = jnp.concatenate(arrived, axis=0)
     shares = spread(mine, n_tp)
     near_rows, far_rows = 4 * CAP, slots - 4 * CAP
-    *near_pieces, gate_sum, up_sum = call(
+    *near_pieces, wide_inner, gate_sum, up_sum = call(
         functools.partial(first_kernel, n_tp),
-        [struct((near_rows, share), BF16)] * n_tp + [struct((far_rows, ff), F32)] * 2,
-        (own, from_core, near, near_crossed, mine, *loaded, mark),
-        [pltpu.VMEM((4 * CAP, width), BF16)],
+        [struct((near_rows, share), BF16)] * n_tp
+        + [struct((CAP, ff), BF16)]
+        + [struct((len(order) * CAP, ff), F32)] * 2,
+        (own, from_core, near, wide_rows, near_crossed, mine, *loaded, mark),
+        [pltpu.VMEM((5 * CAP, width), BF16)],
         flops=2 * slots * width * ff,
     )
     terms = call(
-        functools.partial(expert_kernel, n_tp),
+        functools.partial(expert_kernel, n_tp, order),
         [struct((far_rows, share), BF16)] * n_tp,
-        (*shares, *loaded, gate_sum, up_sum),
+        (*shares, *loaded, wide_inner, gate_sum, up_sum),
         flops=2 * slots * width * ff * 3,
     )
     terms = list(terms)

time: 51.8 us -> 52.3 us (level)
  waiting for transfers between devices: 11.2 us -> 12.7 us
  starting transfers between devices: 29.3 us -> 28.4 us
    ppermute x25, waiting for transfers between devices: 11.2 us -> 12.7 us  [swap(): lax.ppermute(value, axis, [(i, i ^ d) for i in range(lax.axis_size(axis))])]
    ppermute x25, starting transfers between devices: 29.3 us -> 28.4 us  [swap(): lax.ppermute(value, axis, [(i, i ^ d) for i in range(lax.axis_size(axis))])]
    pallas_call x10 -> x9, Pallas kernels: 9.88 us -> 9.73 us  [call(): pl.pallas_call(kernel, out_shape=out_shape, in_specs=[pl.BlockSpec(memory...]
  transfers between devices with their start and end apart: 25 -> 25, of which waited for: 14 -> 13; matrix products, arithmetic and copies ran while one was open for 1% -> 1% of each run, Pallas kernels for 10% -> 8%
where the time goes in v4:
time: 52.3 us; the launch traced here: 52.1 us
  starting transfers between devices  28.4 us (54%)
  waiting for transfers between devices  12.7 us (24%)
  Pallas kernels  9.73 us (19%)
  between operations  0.85 us (2%)
    ppermute x25, starting transfers between devices, swap(): lax.ppermute(value, axis, [(i, i ^ d) for i in range(lax.axis_size(axis))])  28.4 us
    ppermute x25, waiting for transfers between devices, swap(): lax.ppermute(value, axis, [(i, i ^ d) for i in range(lax.axis_size(axis))])  12.7 us
    pallas_call x9, Pallas kernels, call(): pl.pallas_call(kernel, out_shape=out_shape, in_specs=[pl.BlockSpec(memory...  9.73 us
  transfers between devices with their start and end apart: 25, of which 13 were waited for; matrix products, arithmetic and copies ran while one was open for 1% of the time, Pallas kernels for 8%

profile of v4, /device:TPU:0, one launch (start us, length us, event | category | flops | bytes accessed | tf_op | source)
XLA Modules:
  0.0 52.1 jit_solution(13859133642963532494)
XLA Ops:
  0.6 2.6 %shard_map.131 = (bf16[16,896]{1,0:T(8,128)(2,1)S(1)}, bf16[16,896]{1,0:T(8,128)(2,1)S(1)}, bf16[16,896]{1,0:T(8,128)(2,1)S(1)}, bf16[128,256]{1,0:T(8,128)(2,1)...) custom-call(s32[8,256]{1,0:T(8,128)} %bitcast.16, ...), custom_call_target="tpu_custom_call" | custom-call | flops 469762048 | bytes 1865728 | tf_op jit(solution)/shard_map/pallas_call | solution.py:271
  3.3 0.5 collective-permute-start.3
  3.8 3.7 %collective-permute-start = (bf16[16,896]{1,0:T(8,128)(2,1)S(1)}, bf16[16,896]{1,0:T(8,128)(2,1)S(1)}, u32[]{:S(2)}, u32[]{:S(2)}) collective-permute-start(bf16[16,896]{1,0:T(8,128)(2,1)S(1)} %get-tuple-element.53), channel_id=1, source_target_pairs={{0,16},{4,20},{8,24},{12,28},{16,0},{20,4},{24,8},{28,12},{1,17},{... | collective-permute-start | bytes 86024 | tf_op jit(solution)/shard_map/ppermute | solution.py:285
  7.5 1.3 %collective-permute-start.1 = (bf16[16,896]{1,0:T(8,128)(2,1)S(1)}, bf16[16,896]{1,0:T(8,128)(2,1)S(1)}, u32[]{:S(2)}, u32[]{:S(2)}) collective-permute-start(bf16[16,896]{1,0:T(8,128)(2,1)S(1)} %get-tuple-element.54), channel_id=1, source_target_pairs={{0,24},{4,28},{8,16},{12,20},{16,8},{20,12},{24,0},{28,4},{1,25},{... | collective-permute-start | bytes 86024 | tf_op jit(solution)/shard_map/ppermute | solution.py:285
  8.8 2.0 %collective-permute-start.2 = (bf16[16,896]{1,0:T(8,128)(2,1)S(1)}, bf16[16,896]{1,0:T(8,128)(2,1)S(1)}, u32[]{:S(2)}, u32[]{:S(2)}) collective-permute-start(bf16[16,896]{1,0:T(8,128)(2,1)S(1)} %get-tuple-element.55), channel_id=1, source_target_pairs={{0,28},{4,24},{8,20},{12,16},{16,12},{20,8},{24,4},{28,0},{1,29},{... | collective-permute-start | bytes 86024 | tf_op jit(solution)/shard_map/ppermute | solution.py:285
  10.8 1.9 %collective-permute-start.5 = (bf16[64,896]{1,0:T(8,128)(2,1)S(1)}, bf16[64,896]{1,0:T(8,128)(2,1)S(1)}, u32[]{:S(2)}, u32[]{:S(2)}) collective-permute-start(bf16[64,896]{1,0:T(8,128)(2,1)S(1)} %get-tuple-element.59), channel_id=1, source_target_pairs={{0,20},{4,16},{8,28},{12,24},{16,4},{20,0},{24,12},{28,8},{1,21},{... | collective-permute-start | bytes 344072 | tf_op jit(solution)/shard_map/ppermute | solution.py:285
  12.6 0.6 %collective-permute-done.1 = bf16[16,896]{1,0:T(8,128)(2,1)S(1)} collective-permute-done((bf16[16,896]{1,0:T(8,128)(2,1)S(1)}, bf16[16,896]{1,0:T(8,128)(2,1)S(1)}, u32[]{:S(2)}, u32[]{:S(2)}) %collective-permute-start.1) | collective-permute-done | bytes 28704 | tf_op jit(solution)/shard_map/ppermute | solution.py:285
  13.2 1.1 %collective-permute-start.6 = (bf16[64,896]{1,0:T(8,128)(2,1)S(1)}, bf16[64,896]{1,0:T(8,128)(2,1)S(1)}, u32[]{:S(2)}, u32[]{:S(2)}) collective-permute-start(bf16[64,896]{1,0:T(8,128)(2,1)S(1)} %get-tuple-element.60), channel_id=1, source_target_pairs={{0,12},{4,8},{8,4},{12,0},{16,28},{20,24},{24,20},{28,16},{1,13},{... | collective-permute-start | bytes 344072 | tf_op jit(solution)/shard_map/ppermute | solution.py:285
  14.4 2.5 %collective-permute-start.7 = (bf16[48,896]{1,0:T(8,128)(2,1)S(1)}, bf16[48,896]{1,0:T(8,128)(2,1)S(1)}, u32[]{:S(2)}, u32[]{:S(2)}) collective-permute-start(bf16[48,896]{1,0:T(8,128)(2,1)S(1)} %constant_dynamic-update-slice_fusion.mine_ref), channel_id=1, source_target_pairs={{0,3},{1,2},{2,1},{3,0},{4,7},{5,6},{6,5},{7,4},{8,11},{9,10},{10,... | collective-permute-start | bytes 258056 | tf_op jit(solution)/shard_map/ppermute | solution.py:285
  17.4 1.5 %collective-permute-done.4.near_ref = bf16[64,896]{1,0:T(8,128)(2,1)S(1)} collective-permute-done((bf16[64,896]{1,0:T(8,128)(2,1)S(1)}, bf16[64,896]{1,0:T(8,128)(2,1)S(1)}, u32[]{:S(2)}, u32[]{:S(2)}) %collective-permute-start.4) | collective-permute-done | bytes 114720 | tf_op jit(solution)/shard_map/ppermute | solution.py:285
  18.9 1.5 %collective-permute-start.9 = (bf16[48,896]{1,0:T(8,128)(2,1)S(1)}, bf16[48,896]{1,0:T(8,128)(2,1)S(1)}, u32[]{:S(2)}, u32[]{:S(2)}) collective-permute-start(bf16[48,896]{1,0:T(8,128)(2,1)S(1)} %constant_dynamic-update-slice_fusion.mine_ref), channel_id=1, source_target_pairs={{0,1},{1,0},{2,3},{3,2},{4,5},{5,4},{6,7},{7,6},{8,9},{9,8},{10,11... | collective-permute-start | bytes 258056 | tf_op jit(solution)/shard_map/ppermute | solution.py:285
  20.4 2.6 %shard_map.132 = (bf16[3584,256]{1,0:T(8,128)(2,1)S(1)}, bf16[3584,256]{1,0:T(8,128)(2,1)S(1)}, bf16[256,3584]{1,0:T(8,128)(2,1)S(1)}, f32[8,128]{1,0:T(8,128)S(1)}) custom-call(bf16[128,256]{1,0:T(8,128)(2,1)S(1)} %get-tuple-element.77.after_ref.combine_ref, bf16[3584,256]{1,0:T(8,128)(2,1)} %bitcast.13, bf16[3584,256]{1,0:T(8,128)(2,1)} %bitcast.14, ...), custom_call_target="tpu_custom_call" | custom-call | bytes 5570560 | tf_op jit(solution)/shard_map/pallas_call | solution.py:271
  23.0 1.2 %shard_map.133 = (bf16[64,896]{1,0:T(8,128)(2,1)S(1)}, bf16[64,896]{1,0:T(8,128)(2,1)S(1)}, bf16[64,896]{1,0:T(8,128)(2,1)S(1)}, bf16[64,896]{1,0:T(8,128)(2,1)S...) custom-call(bf16[16,3584]{1,0:T(8,128)(2,1)S(1)} %get-tuple-element.52.own_ref, ...), custom_call_target="tpu_custom_call" | custom-call | flops 234881024 | bytes 6168576 | tf_op jit(solution)/shard_map/pallas_call | solution.py:271
  24.3 1.0 %shard_map.134 = (bf16[64,896]{1,0:T(8,128)(2,1)S(1)}, bf16[64,896]{1,0:T(8,128)(2,1)S(1)}, bf16[64,896]{1,0:T(8,128)(2,1)S(1)}, bf16[64,896]{1,0:T(8,128)(2,1)S(1)}) custom-call(bf16[48,896]{1,0:T(8,128)(2,1)S(1)} %collective-permute-done.7.refs_0_, bf16[48,896]{1,0:T(8,128)(2,1)S(1)} %collective-permute-done.8.refs_1_, ...), custom_call_target="tpu_custom_call" | custom-call | flops 704643072 | bytes 5869568 | tf_op jit(solution)/shard_map/pallas_call | solution.py:271
  25.3 1.6 %collective-permute-start.16 = (bf16[64,896]{1,0:T(8,128)(2,1)S(1)}, bf16[64,896]{1,0:T(8,128)(2,1)S(1)}, u32[]{:S(2)}, u32[]{:S(2)}) collective-permute-start(bf16[64,896]{1,0:T(8,128)(2,1)S(1)} %get-tuple-element.89), channel_id=1, source_target_pairs={{0,3},{1,2},{2,1},{3,0},{4,7},{5,6},{6,5},{7,4},{8,11},{9,10},{10,... | collective-permute-start | bytes 344072 | tf_op jit(solution)/shard_map/ppermute | solution.py:285
  27.4 1.5 %collective-permute-start.18 = (bf16[64,896]{1,0:T(8,128)(2,1)S(1)}, bf16[64,896]{1,0:T(8,128)(2,1)S(1)}, u32[]{:S(2)}, u32[]{:S(2)}) collective-permute-start(bf16[64,896]{1,0:T(8,128)(2,1)S(1)} %get-tuple-element.91), channel_id=1, source_target_pairs={{0,1},{1,0},{2,3},{3,2},{4,5},{5,4},{6,7},{7,6},{8,9},{9,8},{10,11... | collective-permute-start | bytes 344072 | tf_op jit(solution)/shard_map/ppermute | solution.py:285
  29.4 1.6 %collective-permute-start.10 = (bf16[64,896]{1,0:T(8,128)(2,1)S(1)}, bf16[64,896]{1,0:T(8,128)(2,1)S(1)}, u32[]{:S(2)}, u32[]{:S(2)}) collective-permute-start(bf16[64,896]{1,0:T(8,128)(2,1)S(1)} %get-tuple-element.81), channel_id=1, source_target_pairs={{0,3},{1,2},{2,1},{3,0},{4,7},{5,6},{6,5},{7,4},{8,11},{9,10},{10,... | collective-permute-start | bytes 344072 | tf_op jit(solution)/shard_map/ppermute | solution.py:285
  31.0 0.5 collective-permute-start.11
  31.5 0.7 %collective-permute-done.16.refs_0_ = bf16[64,896]{1,0:T(8,128)(2,1)S(1)} collective-permute-done((bf16[64,896]{1,0:T(8,128)(2,1)S(1)}, bf16[64,896]{1,0:T(8,128)(2,1)S(1)}, u32[]{:S(2)}, u32[]{:S(2)}) %collective-permute-start.16) | collective-permute-done | bytes 114720 | tf_op jit(solution)/shard_map/ppermute | solution.py:285
  32.2 0.8 %collective-permute-start.12 = (bf16[64,896]{1,0:T(8,128)(2,1)S(1)}, bf16[64,896]{1,0:T(8,128)(2,1)S(1)}, u32[]{:S(2)}, u32[]{:S(2)}) collective-permute-start(bf16[64,896]{1,0:T(8,128)(2,1)S(1)} %get-tuple-element.83), channel_id=1, source_target_pairs={{0,1},{1,0},{2,3},{3,2},{4,5},{5,4},{6,7},{7,6},{8,9},{9,8},{10,11... | collective-permute-start | bytes 344072 | tf_op jit(solution)/shard_map/ppermute | solution.py:285
  32.9 2.6 %collective-permute-done.17.refs_1_ = bf16[64,896]{1,0:T(8,128)(2,1)S(1)} collective-permute-done((bf16[64,896]{1,0:T(8,128)(2,1)S(1)}, bf16[64,896]{1,0:T(8,128)(2,1)S(1)}, u32[]{:S(2)}, u32[]{:S(2)}) %collective-permute-start.17) | collective-permute-done | bytes 114720 | tf_op jit(solution)/shard_map/ppermute | solution.py:285
  35.6 1.4 %collective-permute-start.20 = (bf16[32,896]{1,0:T(8,128)(2,1)S(1)}, bf16[32,896]{1,0:T(8,128)(2,1)S(1)}, u32[]{:S(2)}, u32[]{:S(2)}) collective-permute-start(bf16[32,896]{1,0:T(8,128)(2,1)S(1)} %get-tuple-element.94), channel_id=1, source_target_pairs={{0,24},{4,28},{8,16},{12,20},{16,8},{20,12},{24,0},{28,4},{1,25},{... | collective-permute-start | bytes 172040 | tf_op jit(solution)/shard_map/ppermute | solution.py:285
  37.1 1.2 %collective-permute-done.11.refs_1_ = bf16[64,896]{1,0:T(8,128)(2,1)S(1)} collective-permute-done((bf16[64,896]{1,0:T(8,128)(2,1)S(1)}, bf16[64,896]{1,0:T(8,128)(2,1)S(1)}, u32[]{:S(2)}, u32[]{:S(2)}) %collective-permute-start.11) | collective-permute-done | bytes 114720 | tf_op jit(solution)/shard_map/ppermute | solution.py:285
  38.5 0.8 %collective-permute-start.14 = (bf16[16,896]{1,0:T(8,128)(2,1)S(1)}, bf16[16,896]{1,0:T(8,128)(2,1)S(1)}, u32[]{:S(2)}, u32[]{:S(2)}) collective-permute-start(bf16[16,896]{1,0:T(8,128)(2,1)S(1)} %get-tuple-element.87), channel_id=1, source_target_pairs={{0,8},{4,12},{8,0},{12,4},{16,24},{20,28},{24,16},{28,20},{1,9},{5... | collective-permute-start | bytes 86024 | tf_op jit(solution)/shard_map/ppermute | solution.py:285
  39.4 1.0 %collective-permute-start.15 = (bf16[16,896]{1,0:T(8,128)(2,1)S(1)}, bf16[16,896]{1,0:T(8,128)(2,1)S(1)}, u32[]{:S(2)}, u32[]{:S(2)}) collective-permute-start(bf16[16,896]{1,0:T(8,128)(2,1)S(1)} %get-tuple-element.88), channel_id=1, source_target_pairs={{0,12},{4,8},{8,4},{12,0},{16,28},{20,24},{24,20},{28,16},{1,13},{... | collective-permute-start | bytes 86024 | tf_op jit(solution)/shard_map/ppermute | solution.py:285
  40.7 1.1 %collective-permute-done.20.refs_5_ = bf16[32,896]{1,0:T(8,128)(2,1)S(1)} collective-permute-done((bf16[32,896]{1,0:T(8,128)(2,1)S(1)}, bf16[32,896]{1,0:T(8,128)(2,1)S(1)}, u32[]{:S(2)}, u32[]{:S(2)}) %collective-permute-start.20) | collective-permute-done | bytes 57376 | tf_op jit(solution)/shard_map/ppermute | solution.py:285
  43.1 0.8 %shard_map.138 = (bf16[64,640]{1,0:T(8,128)(2,1)S(1)}, bf16[64,640]{1,0:T(8,128)(2,1)S(1)}, bf16[64,640]{1,0:T(8,128)(2,1)S(1)}, bf16[64,640]{1,0:T(8,128)(2,1)S(1)}) custom-call(bf16[16,896]{1,0:T(8,128)(2,1)S(1)} %get-tuple-element.85.refs_0_, bf16[16,896]{1,0:T(8,128)(2,1)S(1)} %collective-permute-done.13.refs_1_, ...), custom_call_target="tpu_custom_call" | custom-call | flops 322961408 | bytes 1846784 | tf_op jit(solution)/shard_map/pallas_call | solution.py:271
  43.9 2.1 %collective-permute-start.22 = (bf16[64,640]{1,0:T(8,128)(2,1)S(1)}, bf16[64,640]{1,0:T(8,128)(2,1)S(1)}, u32[]{:S(2)}, u32[]{:S(2)}) collective-permute-start(bf16[64,640]{1,0:T(8,128)(2,1)S(1)} %get-tuple-element.97), channel_id=1, source_target_pairs={{0,3},{1,2},{2,1},{3,0},{4,7},{5,6},{6,5},{7,4},{8,11},{9,10},{10,... | collective-permute-start | bytes 245768 | tf_op jit(solution)/shard_map/ppermute | solution.py:285
  46.1 1.3 %collective-permute-start.24 = (bf16[64,640]{1,0:T(8,128)(2,1)S(1)}, bf16[64,640]{1,0:T(8,128)(2,1)S(1)}, u32[]{:S(2)}, u32[]{:S(2)}) collective-permute-start(bf16[64,640]{1,0:T(8,128)(2,1)S(1)} %get-tuple-element.99), channel_id=1, source_target_pairs={{0,1},{1,0},{2,3},{3,2},{4,5},{5,4},{6,7},{7,6},{8,9},{9,8},{10,11... | collective-permute-start | bytes 245768 | tf_op jit(solution)/shard_map/ppermute | solution.py:285
  47.6 1.8 %collective-permute-done.22.refs_0_ = bf16[64,640]{1,0:T(8,128)(2,1)S(1)} collective-permute-done((bf16[64,640]{1,0:T(8,128)(2,1)S(1)}, bf16[64,640]{1,0:T(8,128)(2,1)S(1)}, u32[]{:S(2)}, u32[]{:S(2)}) %collective-permute-start.22) | collective-permute-done | bytes 81952 | tf_op jit(solution)/shard_map/ppermute | solution.py:285
  49.5 1.7 %collective-permute-done.23.refs_1_ = bf16[64,640]{1,0:T(8,128)(2,1)S(1)} collective-permute-done((bf16[64,640]{1,0:T(8,128)(2,1)S(1)}, bf16[64,640]{1,0:T(8,128)(2,1)S(1)}, u32[]{:S(2)}, u32[]{:S(2)}) %collective-permute-start.23) | collective-permute-done | bytes 81952 | tf_op jit(solution)/shard_map/ppermute | solution.py:285
  51.1 0.9 %shard_map.139 = (bf16[64,512]{1,0:T(8,128)(2,1)}, bf16[64,64]{1,0:T(8,128)(2,1)}) custom-call(bf16[64,640]{1,0:T(8,128)(2,1)S(1)} %collective-permute-done.22.refs_0_, bf16[64,640]{1,0:T(8,128)(2,1)S(1)} %collective-permute-done.23.refs_1_, bf16[64,640]{1,0:T(8,128)(2,1)S(1)} %collective-permute-done.24.refs_2_, ...), custom_call_target="tpu_custom_call" | custom-call | bytes 346112 | tf_op jit(solution)/shard_map/pallas_call | solution.py:271
  (47 shorter events, 3.9 us)
Async XLA Ops:
  3.3 11.1 %collective-permute-start.3 = (bf16[64,896]{1,0:T(8,128)(2,1)S(1)}, bf16[64,896]{1,0:T(8,128)(2,1)S(1)}, u32[]{:S(2)}, u32[]{:S(2)}) collective-permute-start(bf16[64,896]{1,0:T(8,128)(2,1)S(1)} %get-tuple-element.56), channel_id=1, source_target_pairs={{0,4},{4,0},{8,12},{12,8},{16,20},{20,16},{24,28},{28,24},{1,5},{5... | collective-permute-start | bytes 344072 | tf_op jit(solution)/shard_map/ppermute | solution.py:285
  3.8 7.0 %collective-permute-start = (bf16[16,896]{1,0:T(8,128)(2,1)S(1)}, bf16[16,896]{1,0:T(8,128)(2,1)S(1)}, u32[]{:S(2)}, u32[]{:S(2)}) collective-permute-start(bf16[16,896]{1,0:T(8,128)(2,1)S(1)} %get-tuple-element.53), channel_id=1, source_target_pairs={{0,16},{4,20},{8,24},{12,28},{16,0},{20,4},{24,8},{28,12},{1,17},{... | collective-permute-start | bytes 86024 | tf_op jit(solution)/shard_map/ppermute | solution.py:285
  7.5 5.8 %collective-permute-start.1 = (bf16[16,896]{1,0:T(8,128)(2,1)S(1)}, bf16[16,896]{1,0:T(8,128)(2,1)S(1)}, u32[]{:S(2)}, u32[]{:S(2)}) collective-permute-start(bf16[16,896]{1,0:T(8,128)(2,1)S(1)} %get-tuple-element.54), channel_id=1, source_target_pairs={{0,24},{4,28},{8,16},{12,20},{16,8},{20,12},{24,0},{28,4},{1,25},{... | collective-permute-start | bytes 86024 | tf_op jit(solution)/shard_map/ppermute | solution.py:285
  8.8 5.5 %collective-permute-start.2 = (bf16[16,896]{1,0:T(8,128)(2,1)S(1)}, bf16[16,896]{1,0:T(8,128)(2,1)S(1)}, u32[]{:S(2)}, u32[]{:S(2)}) collective-permute-start(bf16[16,896]{1,0:T(8,128)(2,1)S(1)} %get-tuple-element.55), channel_id=1, source_target_pairs={{0,28},{4,24},{8,20},{12,16},{16,12},{20,8},{24,4},{28,0},{1,29},{... | collective-permute-start | bytes 86024 | tf_op jit(solution)/shard_map/ppermute | solution.py:285
  10.8 8.1 %collective-permute-start.4 = (bf16[64,896]{1,0:T(8,128)(2,1)S(1)}, bf16[64,896]{1,0:T(8,128)(2,1)S(1)}, u32[]{:S(2)}, u32[]{:S(2)}) collective-permute-start(bf16[64,896]{1,0:T(8,128)(2,1)S(1)} %get-tuple-element.58), channel_id=1, source_target_pairs={{0,8},{4,12},{8,0},{12,4},{16,24},{20,28},{24,16},{28,20},{1,9},{5... | collective-permute-start | bytes 344072 | tf_op jit(solution)/shard_map/ppermute | solution.py:285
  10.8 12.2 %collective-permute-start.5 = (bf16[64,896]{1,0:T(8,128)(2,1)S(1)}, bf16[64,896]{1,0:T(8,128)(2,1)S(1)}, u32[]{:S(2)}, u32[]{:S(2)}) collective-permute-start(bf16[64,896]{1,0:T(8,128)(2,1)S(1)} %get-tuple-element.59), channel_id=1, source_target_pairs={{0,20},{4,16},{8,28},{12,24},{16,4},{20,0},{24,12},{28,8},{1,21},{... | collective-permute-start | bytes 344072 | tf_op jit(solution)/shard_map/ppermute | solution.py:285
  13.2 9.8 %collective-permute-start.6 = (bf16[64,896]{1,0:T(8,128)(2,1)S(1)}, bf16[64,896]{1,0:T(8,128)(2,1)S(1)}, u32[]{:S(2)}, u32[]{:S(2)}) collective-permute-start(bf16[64,896]{1,0:T(8,128)(2,1)S(1)} %get-tuple-element.60), channel_id=1, source_target_pairs={{0,12},{4,8},{8,4},{12,0},{16,28},{20,24},{24,20},{28,16},{1,13},{... | collective-permute-start | bytes 344072 | tf_op jit(solution)/shard_map/ppermute | solution.py:285
  14.4 9.9 %collective-permute-start.7 = (bf16[48,896]{1,0:T(8,128)(2,1)S(1)}, bf16[48,896]{1,0:T(8,128)(2,1)S(1)}, u32[]{:S(2)}, u32[]{:S(2)}) collective-permute-start(bf16[48,896]{1,0:T(8,128)(2,1)S(1)} %constant_dynamic-update-slice_fusion.mine_ref), channel_id=1, source_target_pairs={{0,3},{1,2},{2,1},{3,0},{4,7},{5,6},{6,5},{7,4},{8,11},{9,10},{10,... | collective-permute-start | bytes 258056 | tf_op jit(solution)/shard_map/ppermute | solution.py:285
  16.9 7.4 %collective-permute-start.8 = (bf16[48,896]{1,0:T(8,128)(2,1)S(1)}, bf16[48,896]{1,0:T(8,128)(2,1)S(1)}, u32[]{:S(2)}, u32[]{:S(2)}) collective-permute-start(bf16[48,896]{1,0:T(8,128)(2,1)S(1)} %constant_dynamic-update-slice_fusion.mine_ref), channel_id=1, source_target_pairs={{0,2},{1,3},{2,0},{3,1},{4,6},{5,7},{6,4},{7,5},{8,10},{9,11},{10,... | collective-permute-start | bytes 258056 | tf_op jit(solution)/shard_map/ppermute | solution.py:285
  18.9 5.4 %collective-permute-start.9 = (bf16[48,896]{1,0:T(8,128)(2,1)S(1)}, bf16[48,896]{1,0:T(8,128)(2,1)S(1)}, u32[]{:S(2)}, u32[]{:S(2)}) collective-permute-start(bf16[48,896]{1,0:T(8,128)(2,1)S(1)} %constant_dynamic-update-slice_fusion.mine_ref), channel_id=1, source_target_pairs={{0,1},{1,0},{2,3},{3,2},{4,5},{5,4},{6,7},{7,6},{8,9},{9,8},{10,11... | collective-permute-start | bytes 258056 | tf_op jit(solution)/shard_map/ppermute | solution.py:285
  24.3 4.6 %copy-start.2 = (s32[256]{0:T(256)S(1)}, s32[256]{0:T(256)}, u32[]{:S(2)}) copy-start(s32[256]{0:T(256)} %param.23) | copy-start | bytes 3076
  24.3 4.6 %copy-start.3 = (s32[256]{0:T(256)S(1)}, s32[256]{0:T(256)}, u32[]{:S(2)}) copy-start(s32[256]{0:T(256)} %param.22) | copy-start | bytes 3076
  25.3 16.6 %copy-start.4 = (f32[896]{0:T(1024)S(1)}, f32[896]{0:T(1024)}, u32[]{:S(2)}) copy-start(f32[896]{0:T(1024)} %param.19) | copy-start | bytes 10756
  25.3 17.8 %copy-start = (bf16[896,576]{0,1:T(8,128)(2,1)S(1)}, bf16[896,576]{0,1:T(8,128)(2,1)}, u32[]{:S(2)}) copy-start(bf16[896,576]{0,1:T(8,128)(2,1)} %param.20) | copy-start | bytes 3096580
  25.3 6.9 %collective-permute-start.16 = (bf16[64,896]{1,0:T(8,128)(2,1)S(1)}, bf16[64,896]{1,0:T(8,128)(2,1)S(1)}, u32[]{:S(2)}, u32[]{:S(2)}) collective-permute-start(bf16[64,896]{1,0:T(8,128)(2,1)S(1)} %get-tuple-element.89), channel_id=1, source_target_pairs={{0,3},{1,2},{2,1},{3,0},{4,7},{5,6},{6,5},{7,4},{8,11},{9,10},{10,... | collective-permute-start | bytes 344072 | tf_op jit(solution)/shard_map/ppermute | solution.py:285
  26.9 8.6 %collective-permute-start.17 = (bf16[64,896]{1,0:T(8,128)(2,1)S(1)}, bf16[64,896]{1,0:T(8,128)(2,1)S(1)}, u32[]{:S(2)}, u32[]{:S(2)}) collective-permute-start(bf16[64,896]{1,0:T(8,128)(2,1)S(1)} %get-tuple-element.90), channel_id=1, source_target_pairs={{0,2},{1,3},{2,0},{3,1},{4,6},{5,7},{6,4},{7,5},{8,10},{9,11},{10,... | collective-permute-start | bytes 344072 | tf_op jit(solution)/shard_map/ppermute | solution.py:285
  27.4 8.1 %collective-permute-start.18 = (bf16[64,896]{1,0:T(8,128)(2,1)S(1)}, bf16[64,896]{1,0:T(8,128)(2,1)S(1)}, u32[]{:S(2)}, u32[]{:S(2)}) collective-permute-start(bf16[64,896]{1,0:T(8,128)(2,1)S(1)} %get-tuple-element.91), channel_id=1, source_target_pairs={{0,1},{1,0},{2,3},{3,2},{4,5},{5,4},{6,7},{7,6},{8,9},{9,8},{10,11... | collective-permute-start | bytes 344072 | tf_op jit(solution)/shard_map/ppermute | solution.py:285
  29.4 21.8 %copy-start.1 = (f32[512]{0:T(512)S(1)}, f32[512]{0:T(512)}, u32[]{:S(2)}) copy-start(f32[512]{0:T(512)} %param.21) | copy-start | bytes 6148
  29.4 7.7 %collective-permute-start.10 = (bf16[64,896]{1,0:T(8,128)(2,1)S(1)}, bf16[64,896]{1,0:T(8,128)(2,1)S(1)}, u32[]{:S(2)}, u32[]{:S(2)}) collective-permute-start(bf16[64,896]{1,0:T(8,128)(2,1)S(1)} %get-tuple-element.81), channel_id=1, source_target_pairs={{0,3},{1,2},{2,1},{3,0},{4,7},{5,6},{6,5},{7,4},{8,11},{9,10},{10,... | collective-permute-start | bytes 344072 | tf_op jit(solution)/shard_map/ppermute | solution.py:285
  31.0 7.3 %collective-permute-start.11 = (bf16[64,896]{1,0:T(8,128)(2,1)S(1)}, bf16[64,896]{1,0:T(8,128)(2,1)S(1)}, u32[]{:S(2)}, u32[]{:S(2)}) collective-permute-start(bf16[64,896]{1,0:T(8,128)(2,1)S(1)} %get-tuple-element.82), channel_id=1, source_target_pairs={{0,2},{1,3},{2,0},{3,1},{4,6},{5,7},{6,4},{7,5},{8,10},{9,11},{10,... | collective-permute-start | bytes 344072 | tf_op jit(solution)/shard_map/ppermute | solution.py:285
  32.2 6.2 %collective-permute-start.12 = (bf16[64,896]{1,0:T(8,128)(2,1)S(1)}, bf16[64,896]{1,0:T(8,128)(2,1)S(1)}, u32[]{:S(2)}, u32[]{:S(2)}) collective-permute-start(bf16[64,896]{1,0:T(8,128)(2,1)S(1)} %get-tuple-element.83), channel_id=1, source_target_pairs={{0,1},{1,0},{2,3},{3,2},{4,5},{5,4},{6,7},{7,6},{8,9},{9,8},{10,11... | collective-permute-start | bytes 344072 | tf_op jit(solution)/shard_map/ppermute | solution.py:285
  35.6 5.2 %collective-permute-start.19 = (bf16[32,896]{1,0:T(8,128)(2,1)S(1)}, bf16[32,896]{1,0:T(8,128)(2,1)S(1)}, u32[]{:S(2)}, u32[]{:S(2)}) collective-permute-start(bf16[32,896]{1,0:T(8,128)(2,1)S(1)} %get-tuple-element.93), channel_id=1, source_target_pairs={{0,16},{4,20},{8,24},{12,28},{16,0},{20,4},{24,8},{28,12},{1,17},{... | collective-permute-start | bytes 172040 | tf_op jit(solution)/shard_map/ppermute | solution.py:285
  35.6 6.2 %collective-permute-start.20 = (bf16[32,896]{1,0:T(8,128)(2,1)S(1)}, bf16[32,896]{1,0:T(8,128)(2,1)S(1)}, u32[]{:S(2)}, u32[]{:S(2)}) collective-permute-start(bf16[32,896]{1,0:T(8,128)(2,1)S(1)} %get-tuple-element.94), channel_id=1, source_target_pairs={{0,24},{4,28},{8,16},{12,20},{16,8},{20,12},{24,0},{28,4},{1,25},{... | collective-permute-start | bytes 172040 | tf_op jit(solution)/shard_map/ppermute | solution.py:285
  38.4 3.6 %collective-permute-start.13 = (bf16[16,896]{1,0:T(8,128)(2,1)S(1)}, bf16[16,896]{1,0:T(8,128)(2,1)S(1)}, u32[]{:S(2)}, u32[]{:S(2)}) collective-permute-start(bf16[16,896]{1,0:T(8,128)(2,1)S(1)} %get-tuple-element.86), channel_id=1, source_target_pairs={{0,4},{4,0},{8,12},{12,8},{16,20},{20,16},{24,28},{28,24},{1,5},{5... | collective-permute-start | bytes 86024 | tf_op jit(solution)/shard_map/ppermute | solution.py:285
  38.5 4.0 %collective-permute-start.14 = (bf16[16,896]{1,0:T(8,128)(2,1)S(1)}, bf16[16,896]{1,0:T(8,128)(2,1)S(1)}, u32[]{:S(2)}, u32[]{:S(2)}) collective-permute-start(bf16[16,896]{1,0:T(8,128)(2,1)S(1)} %get-tuple-element.87), channel_id=1, source_target_pairs={{0,8},{4,12},{8,0},{12,4},{16,24},{20,28},{24,16},{28,20},{1,9},{5... | collective-permute-start | bytes 86024 | tf_op jit(solution)/shard_map/ppermute | solution.py:285
  39.4 3.5 %collective-permute-start.15 = (bf16[16,896]{1,0:T(8,128)(2,1)S(1)}, bf16[16,896]{1,0:T(8,128)(2,1)S(1)}, u32[]{:S(2)}, u32[]{:S(2)}) collective-permute-start(bf16[16,896]{1,0:T(8,128)(2,1)S(1)} %get-tuple-element.88), channel_id=1, source_target_pairs={{0,12},{4,8},{8,4},{12,0},{16,28},{20,24},{24,20},{28,16},{1,13},{... | collective-permute-start | bytes 86024 | tf_op jit(solution)/shard_map/ppermute | solution.py:285
  41.8 1.3 %collective-permute-start.21 = (bf16[32,896]{1,0:T(8,128)(2,1)S(1)}, bf16[32,896]{1,0:T(8,128)(2,1)S(1)}, u32[]{:S(2)}, u32[]{:S(2)}) collective-permute-start(bf16[32,896]{1,0:T(8,128)(2,1)S(1)} %pad_maximum_fusion), channel_id=1, source_target_pairs={{0,4},{4,0},{8,12},{12,8},{16,20},{20,16},{24,28},{28,24},{1,5},{5... | collective-permute-start | bytes 172040 | tf_op jit(solution)/shard_map/ppermute | solution.py:285
  43.9 5.6 %collective-permute-start.22 = (bf16[64,640]{1,0:T(8,128)(2,1)S(1)}, bf16[64,640]{1,0:T(8,128)(2,1)S(1)}, u32[]{:S(2)}, u32[]{:S(2)}) collective-permute-start(bf16[64,640]{1,0:T(8,128)(2,1)S(1)} %get-tuple-element.97), channel_id=1, source_target_pairs={{0,3},{1,2},{2,1},{3,0},{4,7},{5,6},{6,5},{7,4},{8,11},{9,10},{10,... | collective-permute-start | bytes 245768 | tf_op jit(solution)/shard_map/ppermute | solution.py:285
  46.0 5.1 %collective-permute-start.23 = (bf16[64,640]{1,0:T(8,128)(2,1)S(1)}, bf16[64,640]{1,0:T(8,128)(2,1)S(1)}, u32[]{:S(2)}, u32[]{:S(2)}) collective-permute-start(bf16[64,640]{1,0:T(8,128)(2,1)S(1)} %get-tuple-element.98), channel_id=1, source_target_pairs={{0,2},{1,3},{2,0},{3,1},{4,6},{5,7},{6,4},{7,5},{8,10},{9,11},{10,... | collective-permute-start | bytes 245768 | tf_op jit(solution)/shard_map/ppermute | solution.py:285
  46.1 5.0 %collective-permute-start.24 = (bf16[64,640]{1,0:T(8,128)(2,1)S(1)}, bf16[64,640]{1,0:T(8,128)(2,1)S(1)}, u32[]{:S(2)}, u32[]{:S(2)}) collective-permute-start(bf16[64,640]{1,0:T(8,128)(2,1)S(1)} %get-tuple-element.99), channel_id=1, source_target_pairs={{0,1},{1,0},{2,3},{3,2},{4,5},{5,4},{6,7},{7,6},{8,9},{9,8},{10,11... | collective-permute-start | bytes 245768 | tf_op jit(solution)/shard_map/ppermute | solution.py:285
